TPU v7x, 32 devices: a whole 2x2x4 slice. The times are simulated.
32 devices in a mesh: groups: 2 (over y), tiles: 4 (over z), sub: 2 (over x), modes: 2 (over core).
Axes of the slice: x: 2, y: 2, z: 4, core: 2. Of those that a mesh axis runs over, the one named last changes fastest.
Arguments:
- object_field: float32 [2, 2048, 1024], P(None, ('groups', 'tiles')), parts along dimension 1, may hold values from -5 to 5
- probe: bfloat16 [4, 256, 512], P('groups'), parts along dimension 0, may hold values from -6 to 6
- intensity: bfloat16 [8, 32, 256, 256], P(('groups', 'tiles'), ('sub', 'modes')), parts along dimension 0, may hold values from 0.099609375 to 10
- centres: int32 [8, 32, 2], P(('groups', 'tiles')), parts along dimension 0, may hold values from 128 to 896, as said below
- counts: int32 [8], P(('groups', 'tiles')), parts along dimension 0, may hold values from 1 to 32, 64 in all
Outputs:
- object_grad: float32 [2, 2048, 1024], P(None, ('groups', 'tiles'), ('sub', 'modes')), parts along dimension 1
- probe_grad: float32 [4, 256, 512], P('groups'), parts along dimension 0
There are 2 independent parts, one for each index of `groups`. A program takes and returns all parts, laid end to end along the dimension named above; each array names one. Nothing has to cross between parts.
Inputs may be any that keep to these rules, and one draw needn't show every extreme that they name: centres[t, j, 0] is a row in [t * 256, (t + 1) * 256) and in [128, 896]; centres[t, j, 1] is a column in [128, 896]. Slots j >= counts[t] of strip t are not scan points and contribute nothing.
All inputs are finite; a program needn't handle non-finite values. No bound on the sum of `counts` on one device may be relied on, other than what follows from the above.
Results may differ from a plain program's by a relative error of at most 0.0041.
Values sent between devices are 32-bit elements; how exact they have to be, the bound alone decides.
No kernel may reach another device: no remote copies, remote signals or barrier semaphores. Data moves between devices by JAX's collectives and lax.ppermute only.
A program may use at most 64 MiB of HBM per device.

v0:
```python
import math

import jax
import jax.numpy as jnp
from jax import lax
from jax.sharding import PartitionSpec as P


def padded(cells, sides, width):
    for axis, dim in sides:
        count = lax.axis_size(axis)
        ends = count - 1
        head = lax.slice_in_dim(cells, 0, width, axis=dim)
        tail = lax.slice_in_dim(cells, cells.shape[dim] - width, cells.shape[dim], axis=dim)
        cells = jnp.concatenate(
            [
                lax.ppermute(tail, axis, [(i, (i + 1) % count) for i in range(ends)]),
                cells,
                lax.ppermute(head, axis, [((i + 1) % count, i) for i in range(ends)]),
            ],
            axis=dim,
        )
    return cells


def dft_tables(size):
    index = jnp.arange(size, dtype=jnp.int32)
    wrapped = index[:, None] * index[None, :] % size
    angle = wrapped.astype(jnp.float32) * (2.0 * math.pi / size)
    scale = 1.0 / math.sqrt(size)
    return (
        (jnp.cos(angle) * scale).astype(jnp.bfloat16),
        (-jnp.sin(angle) * scale).astype(jnp.bfloat16),
    )


def transform(field, cos_part, sin_part):
    size = cos_part.shape[0]
    left = jnp.concatenate([cos_part, sin_part], axis=0)
    right = jnp.concatenate(
        [
            jnp.concatenate([cos_part, sin_part], axis=1),
            jnp.concatenate([-sin_part, cos_part], axis=1),
        ],
        axis=0,
    )
    stacked = jnp.einsum("ak,smkc->smac", left, field, preferred_element_type=jnp.float32)
    real = stacked[..., :size, :size] - stacked[..., size:, size:]
    imag = stacked[..., :size, size:] + stacked[..., size:, :size]
    middle = jnp.concatenate([real, imag], axis=-1).astype(jnp.bfloat16)
    return jnp.einsum("smac,cd->smad", middle, right, preferred_element_type=jnp.float32)


def point_terms(patches, probe, inten, cos_part, sin_part):
    size = probe.shape[1]
    probe_re = probe[None, :, :, :size].astype(jnp.float32)
    probe_im = probe[None, :, :, size:].astype(jnp.float32)
    obj_re = patches[:, None, :, :size]
    obj_im = patches[:, None, :, size:]
    wave = jnp.concatenate(
        [probe_re * obj_re - probe_im * obj_im, probe_re * obj_im + probe_im * obj_re], axis=-1
    ).astype(jnp.bfloat16)
    far = transform(wave, cos_part, sin_part)
    power = jnp.sum(far[..., :size] ** 2 + far[..., size:] ** 2, axis=1)
    model = jnp.sqrt(power + 1.0)
    measured = jnp.sqrt(inten.astype(jnp.float32) + 1.0)
    ratio = 1.0 - measured / model
    chi = (far * jnp.concatenate([ratio, ratio], axis=-1)[:, None]).astype(jnp.bfloat16)
    back = transform(chi, cos_part, -sin_part)
    back_re = back[..., :size]
    back_im = back[..., size:]
    obj_terms = jnp.concatenate(
        [
            jnp.sum(probe_re * back_re + probe_im * back_im, axis=1),
            jnp.sum(probe_re * back_im - probe_im * back_re, axis=1),
        ],
        axis=-1,
    )
    probe_terms = jnp.concatenate(
        [obj_re * back_re + obj_im * back_im, obj_re * back_im - obj_im * back_re], axis=-1
    )
    return (obj_terms, probe_terms)


def fold_rims(grad, extended, half, strip_rows, patch_side):
    core = grad[:, half : half + strip_rows]
    core = core.at[:, :half].add(extended[:, :half])
    core = core.at[:, strip_rows - half :].add(extended[:, patch_side + half :])
    return core


def on_device(object_field, probe, intensity, centres, counts):
    patch_side = probe.shape[1]
    half = patch_side // 2
    strip_rows = object_field.shape[1]
    slot_count = intensity.shape[1]
    member = lax.axis_index("sub") * lax.axis_size("modes") + lax.axis_index("modes")
    strip_index = lax.axis_index("tiles")
    cos_part, sin_part = dft_tables(patch_side)
    margined = padded(object_field, (("tiles", 1),), half)
    spots = lax.dynamic_slice_in_dim(centres[0], member * slot_count, slot_count, 0)
    slots = member * slot_count + jnp.arange(slot_count, dtype=jnp.int32)
    valid = (slots < counts[0]).astype(jnp.float32)
    row_start = spots[:, 0] - strip_index * strip_rows
    col_start = spots[:, 1] - half

    def cut(row, col):
        piece = lax.dynamic_slice(margined, (jnp.int32(0), row, col), (2, patch_side, patch_side))
        return jnp.concatenate([piece[0], piece[1]], axis=-1)

    patches = jax.vmap(cut)(row_start, col_start)
    obj_terms, probe_terms = point_terms(patches, probe, intensity[0], cos_part, sin_part)
    probe_local = jnp.sum(probe_terms * valid[:, None, None, None], axis=0)
    grad = jnp.zeros(margined.shape, jnp.float32)
    for slot in range(slot_count):
        update = obj_terms[slot] * valid[slot]
        update = jnp.stack([update[:, :patch_side], update[:, patch_side:]])
        start = (jnp.int32(0), row_start[slot], col_start[slot])
        grad = lax.dynamic_update_slice(
            grad, lax.dynamic_slice(grad, start, (2, patch_side, patch_side)) + update, start
        )
    rims = jnp.concatenate([grad[:, :half], grad[:, strip_rows + half :]], axis=1)
    extended = padded(rims, (("tiles", 1),), half)
    core = fold_rims(grad, extended, half, strip_rows, patch_side)
    object_grad = lax.psum_scatter(core, ("sub", "modes"), scatter_dimension=2, tiled=True)
    probe_grad = lax.psum(probe_local, ("tiles", "sub", "modes"))
    return (object_grad, probe_grad)


def solution(mesh):
    return jax.shard_map(
        on_device,
        mesh=mesh,
        in_specs=(
            P(None, ("groups", "tiles"), None),
            P("groups", None, None),
            P(("groups", "tiles"), ("sub", "modes"), None, None),
            P(("groups", "tiles"), None, None),
            P(("groups", "tiles")),
        ),
        out_specs=(P(None, ("groups", "tiles"), ("sub", "modes")), P("groups", None, None)),
        check_vma=False,
    )
```

profile of v0, /device:TPU:0, one launch (start us, length us, event | category | flops | bytes accessed | tf_op | source)
XLA Modules:
  0.0 331.2 jit_solution(7781244550890634584)
XLA Ops:
  11.4 5.9 %collective-permute-start = (f32[2,128,1024]{2,1,0:T(8,128)}, f32[2,128,1024]{2,1,0:T(8,128)}, u32[]{:S(2)}, u32[]{:S(2)}) collective-permute-start(f32[2,128,1024]{2,1,0:T(8,128)} %get-tuple-element.72), channel_id=1, source_target_pairs={{0,4},{4,8},{8,12},{1,5},{5,9},{9,13},{2,6},{6,10},{10,14},{3,7},{... | collective-permute-start | bytes 3145736 | tf_op jit(solution)/shard_map/ppermute | solution.py:17
  56.5 4.4 %pad_maximum_fusion = f32[2,512,1024]{2,1,0:T(8,128)} fusion(f32[2,128,1024]{2,1,0:T(8,128)} %collective-permute-done.1, f32[2,256,1024]{2,1,0:T(8,128)S(1)} %copy-done.9, f32[2,128,1024]{2,1,0:T(8,128)} %collective-permute-done), kind=kLoop, calls=%fused_computation.33 | loop fusion | flops 2097152 | bytes 8388608 | tf_op jit(solution)/shard_map/concatenate | solution.py:15
  60.9 32.5 %while.3 = (s32[]{:T(128)}, f32[2,512,1024]{2,1,0:T(8,128)}, s32[8,3]{0,1:T(4,128)S(1)}, f32[8,2,256,256]{3,2,1,0:T(8,128)}, s32[]{:T(128)}) while((s32[]{:T(128)}, f32[2,512,1024]{2,1,0:T(8,128)}, s32[8,3]{0,1:T(4,128)S(1)}, f32[8,2,256,256]{3,2,1,0:T(8,128)}, s32[]{:T(128)}) %tuple.91), condition=%wide.while_cond.2, body=%wide.while_body.2.sunk | while | flops 2 | bytes 1050217 | solution.py:108
  65.6 3.5 %bitcast_dynamic-update-slice_fusion.2 = f32[8,2,256,256]{3,2,1,0:T(8,128)} fusion(f32[8,2,256,256]{3,2,1,0:T(8,128)} %get-tuple-element.167, s32[]{:T(128)} %get-tuple-element.164, f32[2,512,1024]{2,1,0:T(8,128)} %get-tuple-element.170, s32[]{:T(128)} %bitcast.115, s32[]{:T(128)} %bitcast.116), kind=kLoop, calls=%fused_computation.clone.1 | loop fusion | bytes 1050112 | tf_op jit(solution)/shard_map/vmap()/gather
  77.8 3.5 %bitcast_dynamic-update-slice_fusion.2 = f32[8,2,256,256]{3,2,1,0:T(8,128)} fusion(f32[8,2,256,256]{3,2,1,0:T(8,128)} %get-tuple-element.167, s32[]{:T(128)} %get-tuple-element.164, f32[2,512,1024]{2,1,0:T(8,128)} %get-tuple-element.170, s32[]{:T(128)} %bitcast.115, s32[]{:T(128)} %bitcast.116), kind=kLoop, calls=%fused_computation.clone.1 | loop fusion | bytes 1050112 | tf_op jit(solution)/shard_map/vmap()/gather
  89.9 3.5 %bitcast_dynamic-update-slice_fusion.2 = f32[8,2,256,256]{3,2,1,0:T(8,128)} fusion(f32[8,2,256,256]{3,2,1,0:T(8,128)} %get-tuple-element.167, s32[]{:T(128)} %get-tuple-element.164, f32[2,512,1024]{2,1,0:T(8,128)} %get-tuple-element.170, s32[]{:T(128)} %bitcast.115, s32[]{:T(128)} %bitcast.116), kind=kLoop, calls=%fused_computation.clone.1 | loop fusion | bytes 1050112 | tf_op jit(solution)/shard_map/vmap()/gather
  93.4 4.7 %slice_bitcast_fusion.1 = (f32[8,256,256]{2,1,0:T(8,128)}, f32[8,256,256]{2,1,0:T(8,128)}) fusion(f32[8,2,256,256]{3,2,1,0:T(8,128)} %get-tuple-element.33), kind=kLoop, calls=%fused_computation.56 | loop fusion | bytes 8388608 | tf_op jit(solution)/shard_map/mul | solution.py:61
  100.0 3.6 %copy.19 = f32[8,256,256]{1,2,0:T(8,128)} copy(f32[8,256,256]{2,1,0:T(8,128)} %get-tuple-element.71) | data formatting | bytes 4194304 | tf_op jit(solution)/shard_map/mul | solution.py:61
  119.9 7.1 %convolution_bitcast_fusion = f32[8,2,512,512]{2,3,1,0:T(8,128)S(1)} fusion(f32[8,2,256,512]{3,2,1,0:T(8,128)} %copy-done.2, f32[8,256,512]{2,1,0:T(8,128)} %pad_maximum_fusion.1, bf16[256,256]{1,0:T(8,128)(2,1)} %copy-done.10, bf16[256,256]{1,0:T(8,128)(2,1)} %copy-done.14), kind=kOutput, calls=%fused_computation.16 | convolution fusion | flops 2152202240 | bytes 29622272 | tf_op jit(solution)/shard_map/ak,smkc->smac/dot_general | solution.py:47
  131.4 4.8 %multiply_add_fusion = (f32[8,2,256,256]{2,3,1,0:T(8,128)}, f32[8,2,256,256]{2,3,1,0:T(8,128)}, f32[8,256,256]{1,2,0:T(8,128)S(1)}, f32[8,256,256]{1,2,0:T(8,128)S(1)}) fusion(f32[8,2,256,512]{2,3,1,0:T(8,128)S(1)} %fusion.14, f32[8,256,256]{1,2,0:T(8,128)S(1)} %copy-done.6, f32[8,256,256]{1,2,0:T(8,128)S(1)} %copy-done.5, f32[2,256,256]{1,2,0:T(8,128)S(1)} %copy.18, ...), kind=kLoop, calls=%fused_computation.47 | loop fusion | flops 13631488 | bytes 26214400 | tf_op jit(solution)/shard_map/add | solution.py:80
  138.2 4.1 %fusion.50 = (f32[256,512]{0,1:T(8,128)S(1)}, f32[256,512]{0,1:T(8,128)S(1)}, f32[256,512]{0,1:T(8,128)S(1)}, f32[256,512]{0,1:T(8,128)S(1)}, f32[256,512]{0,1:T(8,128)S(1)}, /*index=5*/f32[256,512]{0,1:T(8,128)S(1)}) fusion(f32[8,256,256]{1,2,0:T(8,128)S(1)} %get-tuple-element.57, f32[8,256,256]{1,2,0:T(8,128)S(1)} %get-tuple-element.56, f32[]{:T(128)} %bitcast.59, ...), kind=kLoop, calls=%fused_computation.92 | loop fusion | flops 1572864 | bytes 7340056 | tf_op jit(solution)/shard_map/mul | solution.py:116
  145.8 6.5 %dynamic_update_slice.24 = f32[2,512,1024]{1,2,0:T(8,128)} dynamic-update-slice(f32[2,512,1024]{1,2,0:T(8,128)} %broadcast_in_dim.2, f32[2,256,256]{1,2,0:T(8,128)S(1)} %pad_maximum_fusion.9, s32[]{:T(128)} %constant.93.clone.1, s32[]{:T(128)S(6)} %select_n.106, s32[]{:T(128)S(6)} %select_n.107) | dynamic-update-slice | bytes 1048580 | tf_op jit(solution)/shard_map/dynamic_update_slice | solution.py:119
  153.8 6.5 %dynamic_update_slice.25 = f32[2,512,1024]{1,2,0:T(8,128)} dynamic-update-slice(f32[2,512,1024]{1,2,0:T(8,128)} %dynamic_update_slice.24, f32[2,256,256]{1,2,0:T(8,128)S(1)} %maximum_add_fusion, s32[]{:T(128)} %constant.93.clone.1, s32[]{:T(128)S(6)} %select_n.108, s32[]{:T(128)S(6)} %select_n.109) | dynamic-update-slice | bytes 1048580 | tf_op jit(solution)/shard_map/dynamic_update_slice | solution.py:119
  161.7 6.6 %dynamic_update_slice.26 = f32[2,512,1024]{1,2,0:T(8,128)} dynamic-update-slice(f32[2,512,1024]{1,2,0:T(8,128)} %dynamic_update_slice.25, f32[2,256,256]{1,2,0:T(8,128)S(1)} %maximum_add_fusion.1, s32[]{:T(128)} %constant.93.clone.1, s32[]{:T(128)S(6)} %select_n.110, s32[]{:T(128)S(6)} %select_n.111) | dynamic-update-slice | bytes 1048580 | tf_op jit(solution)/shard_map/dynamic_update_slice | solution.py:119
  169.7 6.5 %dynamic_update_slice.27 = f32[2,512,1024]{1,2,0:T(8,128)} dynamic-update-slice(f32[2,512,1024]{1,2,0:T(8,128)} %dynamic_update_slice.26, f32[2,256,256]{1,2,0:T(8,128)S(1)} %maximum_add_fusion.2, s32[]{:T(128)} %constant.93.clone.1, s32[]{:T(128)S(6)} %select_n.112, s32[]{:T(128)S(6)} %select_n.113) | dynamic-update-slice | bytes 1048580 | tf_op jit(solution)/shard_map/dynamic_update_slice | solution.py:119
  177.7 5.8 %dynamic_update_slice.28 = f32[2,512,1024]{1,2,0:T(8,128)} dynamic-update-slice(f32[2,512,1024]{1,2,0:T(8,128)} %dynamic_update_slice.27, f32[2,256,256]{1,2,0:T(8,128)S(1)} %maximum_add_fusion.3, s32[]{:T(128)} %constant.93.clone.1, s32[]{:T(128)S(6)} %select_n.114, s32[]{:T(128)S(6)} %select_n.115) | dynamic-update-slice | bytes 1048580 | tf_op jit(solution)/shard_map/dynamic_update_slice | solution.py:119
  184.9 5.8 %dynamic_update_slice.29 = f32[2,512,1024]{1,2,0:T(8,128)} dynamic-update-slice(f32[2,512,1024]{1,2,0:T(8,128)} %dynamic_update_slice.28, f32[2,256,256]{1,2,0:T(8,128)S(1)} %maximum_add_fusion.4, s32[]{:T(128)} %constant.93.clone.1, s32[]{:T(128)S(6)} %select_n.116, s32[]{:T(128)S(6)} %select_n.117) | dynamic-update-slice | bytes 1048580 | tf_op jit(solution)/shard_map/dynamic_update_slice | solution.py:119
  192.1 5.8 %dynamic_update_slice.30 = f32[2,512,1024]{1,2,0:T(8,128)} dynamic-update-slice(f32[2,512,1024]{1,2,0:T(8,128)} %dynamic_update_slice.29, f32[2,256,256]{1,2,0:T(8,128)S(1)} %maximum_add_fusion.5, s32[]{:T(128)} %constant.93.clone.1, s32[]{:T(128)S(6)} %select_n.118, s32[]{:T(128)S(6)} %select_n.119) | dynamic-update-slice | bytes 1048580 | tf_op jit(solution)/shard_map/dynamic_update_slice | solution.py:119
  199.2 6.5 %dynamic_update_slice.31 = f32[2,512,1024]{1,2,0:T(8,128)} dynamic-update-slice(f32[2,512,1024]{1,2,0:T(8,128)} %dynamic_update_slice.30, f32[2,256,256]{1,2,0:T(8,128)S(1)} %maximum_add_fusion.6, s32[]{:T(128)} %constant.93.clone.1, s32[]{:T(128)S(6)} %select_n.120, s32[]{:T(128)S(6)} %select_n.121) | dynamic-update-slice | bytes 1048580 | tf_op jit(solution)/shard_map/dynamic_update_slice | solution.py:119
  208.9 8.9 %collective-permute-start.2 = (f32[2,128,1024]{1,2,0:T(8,128)}, f32[2,128,1024]{1,2,0:T(8,128)}, u32[]{:S(2)}, u32[]{:S(2)}) collective-permute-start(f32[2,128,1024]{1,2,0:T(8,128)} %get-tuple-element.61), channel_id=1, source_target_pairs={{0,4},{4,8},{8,12},{1,5},{5,9},{9,13},{2,6},{6,10},{10,14},{3,7},{... | collective-permute-start | bytes 3145736 | tf_op jit(solution)/shard_map/ppermute | solution.py:17
  219.4 3.8 %fusion = f32[2,256,512]{1,2,0:T(8,128)} fusion(f32[8,2,256,256]{2,3,1,0:T(8,128)} %get-tuple-element.55, f32[8,2,256,256]{2,3,1,0:T(8,128)S(1)} %copy-done.7, f32[8]{0:T(128)S(1)} %compare_convert_fusion), kind=kLoop, calls=%fused_computation.19 | loop fusion | flops 6029312 | bytes 9437216 | tf_op jit(solution)/shard_map/reduce_sum | solution.py:113
  223.3 19.8 %collective-permute-done.2 = f32[2,128,1024]{1,2,0:T(8,128)} collective-permute-done((f32[2,128,1024]{1,2,0:T(8,128)}, f32[2,128,1024]{1,2,0:T(8,128)}, u32[]{:S(2)}, u32[]{:S(2)}) %collective-permute-start.2) | collective-permute-done | bytes 1048608 | tf_op jit(solution)/shard_map/ppermute | solution.py:17
  244.8 5.4 %collective-permute-done.3 = f32[2,128,1024]{1,2,0:T(8,128)S(1)} collective-permute-done((f32[2,128,1024]{1,2,0:T(8,128)}, f32[2,128,1024]{1,2,0:T(8,128)S(1)}, u32[]{:S(2)}, u32[]{:S(2)}) %collective-permute-start.3) | collective-permute-done | bytes 1048608 | tf_op jit(solution)/shard_map/ppermute | solution.py:19
  251.7 67.4 %all-reduce.2.cloned.1.call-done = f32[2,256,512]{1,2,0:T(8,128)} async-done(((f32[2,256,512]{1,2,0:T(8,128)}), f32[2,256,512]{1,2,0:T(8,128)}) %all-reduce.2.cloned.1.call-update) | async-done | bytes 1048592 | tf_op jit(solution)/shard_map/psum | solution.py:126
  (116 shorter events, 84.4 us)
Async XLA Ops:
  8.0 10.7 %copy-start = (s32[1,32,2]{1,2,0:T(2,128)S(1)}, s32[1,32,2]{1,2,0:T(2,128)}, u32[]{:S(2)}) copy-start(s32[1,32,2]{1,2,0:T(2,128)} %param.12) | copy-start | bytes 772
  8.0 48.5 %copy-start.9 = (f32[2,256,1024]{2,1,0:T(8,128)S(1)}, f32[2,256,1024]{2,1,0:T(8,128)}, u32[]{:S(2)}) copy-start(f32[2,256,1024]{2,1,0:T(8,128)} %param.9) | copy-start | bytes 6291460
  8.0 32.0 %copy-start.16 = (bf16[2,256,512]{2,1,0:T(8,128)(2,1)S(1)}, bf16[2,256,512]{2,1,0:T(8,128)(2,1)}, u32[]{:S(2)}) copy-start(bf16[2,256,512]{2,1,0:T(8,128)(2,1)} %param.10) | copy-start | bytes 1572868
  8.0 311.1 %all-reduce.2.cloned.1.call-start = ((), (), s32[]{:S(2)}) async-start(), calls=%async_computation.2 | async-start | bytes 2097152 | tf_op jit(solution)/shard_map/psum | solution.py:126
  11.4 45.1 %collective-permute-start = (f32[2,128,1024]{2,1,0:T(8,128)}, f32[2,128,1024]{2,1,0:T(8,128)}, u32[]{:S(2)}, u32[]{:S(2)}) collective-permute-start(f32[2,128,1024]{2,1,0:T(8,128)} %get-tuple-element.72), channel_id=1, source_target_pairs={{0,4},{4,8},{8,12},{1,5},{5,9},{9,13},{2,6},{6,10},{10,14},{3,7},{... | collective-permute-start | bytes 3145736 | tf_op jit(solution)/shard_map/ppermute | solution.py:17
  17.4 39.2 %collective-permute-start.1 = (f32[2,128,1024]{2,1,0:T(8,128)}, f32[2,128,1024]{2,1,0:T(8,128)}, u32[]{:S(2)}, u32[]{:S(2)}) collective-permute-start(f32[2,128,1024]{2,1,0:T(8,128)} %get-tuple-element.73), channel_id=1, source_target_pairs={{4,0},{8,4},{12,8},{5,1},{9,5},{13,9},{6,2},{10,6},{14,10},{7,3},{... | collective-permute-start | bytes 3145736 | tf_op jit(solution)/shard_map/ppermute | solution.py:19
  55.4 55.4 %copy-start.14 = (bf16[256,256]{1,0:T(8,128)(2,1)}, bf16[256,256]{1,0:T(8,128)(2,1)S(1)}, u32[]{:S(2)}) copy-start(bf16[256,256]{1,0:T(8,128)(2,1)S(1)} %fusion.67) | copy-start | bytes 393220
  56.5 54.3 %copy-start.10 = (bf16[256,256]{1,0:T(8,128)(2,1)}, bf16[256,256]{1,0:T(8,128)(2,1)S(1)}, u32[]{:S(2)}) copy-start(bf16[256,256]{1,0:T(8,128)(2,1)S(1)} %get-tuple-element.129) | copy-start | bytes 393220
  56.5 54.3 %copy-start.17 = (bf16[256,256]{1,0:T(8,128)(2,1)}, bf16[256,256]{1,0:T(8,128)(2,1)S(1)}, u32[]{:S(2)}) copy-start(bf16[256,256]{1,0:T(8,128)(2,1)S(1)} %get-tuple-element.128) | copy-start | bytes 393220
  100.0 6.5 %copy-start.4 = (f32[8,256,256]{1,2,0:T(8,128)}, f32[8,256,256]{1,2,0:T(8,128)S(1)}, u32[]{:S(2)}) copy-start(f32[8,256,256]{1,2,0:T(8,128)S(1)} %copy.17) | copy-start | bytes 6291460
  113.2 3.3 copy-start.2
  113.2 3.3 copy-start.12
  127.0 1.8 copy-start.11
  127.0 1.8 copy-start.15
  127.0 1.8 copy-start.18
  128.8 2.6 copy-start.5
  128.8 2.6 copy-start.6
  161.7 21.8 %copy-start.13 = (f32[1,256,256]{1,2,0:T(8,128)S(1)}, f32[1,256,256]{1,2,0:T(8,128)}, u32[]{:S(2)}) copy-start(f32[1,256,256]{1,2,0:T(8,128)} %get-tuple-element.79) | copy-start | bytes 786436
  205.8 13.4 %copy-start.3 = (f32[2,512,1024]{1,2,0:T(8,128)S(1)}, f32[2,512,1024]{1,2,0:T(8,128)}, u32[]{:S(2)}) copy-start(f32[2,512,1024]{1,2,0:T(8,128)} %dynamic_update_slice.31) | copy-start | bytes 12582916
  205.8 13.7 %copy-start.7 = (f32[8,2,256,256]{2,3,1,0:T(8,128)S(1)}, f32[8,2,256,256]{2,3,1,0:T(8,128)}, u32[]{:S(2)}) copy-start(f32[8,2,256,256]{2,3,1,0:T(8,128)} %get-tuple-element.54) | copy-start | bytes 12582916
  208.9 34.2 %collective-permute-start.2 = (f32[2,128,1024]{1,2,0:T(8,128)}, f32[2,128,1024]{1,2,0:T(8,128)}, u32[]{:S(2)}, u32[]{:S(2)}) collective-permute-start(f32[2,128,1024]{1,2,0:T(8,128)} %get-tuple-element.61), channel_id=1, source_target_pairs={{0,4},{4,8},{8,12},{1,5},{5,9},{9,13},{2,6},{6,10},{10,14},{3,7},{... | collective-permute-start | bytes 3145736 | tf_op jit(solution)/shard_map/ppermute | solution.py:17
  217.9 32.3 %collective-permute-start.3 = (f32[2,128,1024]{1,2,0:T(8,128)}, f32[2,128,1024]{1,2,0:T(8,128)S(1)}, u32[]{:S(2)}, u32[]{:S(2)}) collective-permute-start(f32[2,128,1024]{1,2,0:T(8,128)} %get-tuple-element.60), channel_id=1, source_target_pairs={{4,0},{8,4},{12,8},{5,1},{9,5},{13,9},{6,2},{10,6},{14,10},{7,3},{... | collective-permute-start | bytes 3145736 | tf_op jit(solution)/shard_map/ppermute | solution.py:19
  223.2 98.5 %reduce-scatter.2.cloned.1.call-start = ((), (), s32[]{:S(2)}) async-start(), calls=%async_computation.1 | async-start | bytes 2621440 | tf_op jit(solution)/shard_map/reduce_scatter | solution.py:125
  243.1 80.6 %copy-start.1 = (s32[1,32,2]{1,2,0:T(2,128)S(1)}, s32[1,32,2]{1,2,0:T(2,128)}, u32[]{:S(2)}) copy-start(s32[1,32,2]{1,2,0:T(2,128)} %param.12) | copy-start | bytes 772
  (1 other events, 1.3 us)
Sparse Core Ops, SparseCore 0:
  223.4 95.7 all-reduce.1
Sparse Core Ops, SparseCore 1:
  251.8 29.9 reduce-scatter.1
where the time goes:
time: 334 us; the launch traced here: 331 us
  local copies, waits for them, and re-layouts  115 us (34%)
  waiting for transfers between devices  92.7 us (28%)
  between operations  46.6 us (14%)
  other arithmetic  44.9 us (13%)
  starting transfers between devices  17.5 us (5%)
  matrix products  14.4 us (4%)
    psum x1, waiting for transfers between devices, on_device(): probe_grad = lax.psum(probe_local, ('tiles', 'sub', 'modes'))  67.4 us
    dynamic_update_slice x8, local copies, waits for them, and re-layouts, on_device(): lax.dynamic_update_slice(grad, lax.dynamic_slice(grad, start, (2, patch_s...  50 us
    gather x24, local copies, waits for them, and re-layouts  32.4 us
    ppermute x2, waiting for transfers between devices, padded(): lax.ppermute(tail, axis, [(i, (i + 1) % count) for i in range(ends)])  19.8 us
    ppermute x2, starting transfers between devices, padded(): lax.ppermute(tail, axis, [(i, (i + 1) % count) for i in range(ends)])  14.9 us
    add x7, other arithmetic, on_device(): lax.dynamic_slice(grad, start, (2, patch_side, patch_side)) + update  9.76 us
    dot_general x2, matrix products, transform(): jnp.einsum('ak,smkc->smac', left, field, preferred_element_type=jnp.float32)  9.45 us
    unnamed x40, local copies, waits for them, and re-layouts  8.48 us
  transfers between devices with their start and end apart: 6, of which 3 were waited for; matrix products, arithmetic and copies ran while one was open for 5% of the time, Pallas kernels for 0%

commit v1 on v0

v1 whole, which is shorter than its diff:
```python
import functools
import math

import jax
import jax.numpy as jnp
import ml_dtypes
import numpy as np
from jax import lax
from jax.experimental import pallas as pl
from jax.experimental.pallas import tpu as pltpu
from jax.sharding import PartitionSpec as P

LANES = 128
CHUNK = 64


def dft_tables(size):
    index = np.arange(size)
    angle = (index[:, None] * index[None, :] % size) * (2.0 * math.pi / size)
    scale = 1.0 / math.sqrt(size)
    cos_part = (np.cos(angle) * scale).astype(np.float32).astype(ml_dtypes.bfloat16)
    sin_part = (-np.sin(angle) * scale).astype(np.float32).astype(ml_dtypes.bfloat16)
    plain = np.block([[cos_part, -sin_part], [sin_part, cos_part]])
    turned = np.block([[cos_part, sin_part], [-sin_part, cos_part]])
    return plain, turned


def point_kernel(
    place,
    counts,
    spots,
    own,
    up_a,
    dn_a,
    up_b,
    dn_b,
    probe,
    inten,
    plain,
    turned,
    *rest,
    owners,
):
    outs = rest[:owners]
    probe_grad = rest[owners]
    field, grad, probe_f32, patch, wave, half_buf, far, sems, out_sems = rest[owners + 1 :]
    strip, sub, mode = place[0], place[1], place[2]
    member = sub * 2 + mode
    side = probe.shape[1]
    rim = side // 2
    strip_rows = own.shape[1]
    blocks = own.shape[2] // LANES
    slots = inten.shape[0]
    total = jnp.clip(counts[0] - member * slots, 0, slots)

    copies = []

    def fetch(src, dst):
        copies.append(pltpu.make_async_copy(src, dst, sems.at[len(copies)]))

    for block in range(blocks):
        cols = pl.ds(block * LANES, LANES)
        for plane in range(2):
            fetch(own.at[plane, :, cols], field.at[plane, block, pl.ds(rim, strip_rows)])
        for up, dn, plane in ((up_a, dn_a, mode), (up_b, dn_b, 1 - mode)):
            fetch(up.at[:, cols], field.at[plane, block, pl.ds(0, rim)])
            fetch(dn.at[:, cols], field.at[plane, block, pl.ds(rim + strip_rows, rim)])
    for copy in copies:
        copy.start()

    probe_grad[...] = jnp.zeros_like(probe_grad)
    for m in range(2):
        probe_f32[m] = probe[m].astype(jnp.float32)

    @pl.loop(0, grad.shape[0])
    def clear(block):
        grad[block] = jnp.zeros(grad.shape[1:], jnp.float32)

    for copy in copies:
        copy.wait()

    lane = lax.broadcasted_iota(jnp.int32, (CHUNK, LANES), 1)

    @pl.loop(0, total)
    def point(slot):
        base = 2 * (member * slots + slot)
        row = spots[base] - strip * strip_rows
        col = spots[base + 1] - rim
        block = col // LANES
        off = col % LANES
        back_shift = (LANES - off) % LANES
        for plane in range(2):
            for chunk in range(0, side, CHUNK):
                rows = pl.ds(row + chunk, CHUNK)
                rolled = [
                    pltpu.roll(field[plane, block + j, rows, :], back_shift, 1) for j in range(3)
                ]
                for j in range(2):
                    patch[plane, chunk : chunk + CHUNK, j * LANES : (j + 1) * LANES] = jnp.where(
                        lane < LANES - off, rolled[j], rolled[j + 1]
                    )
        for chunk in range(0, side, CHUNK):
            rows = slice(chunk, chunk + CHUNK)
            obj_re, obj_im = patch[0, rows], patch[1, rows]
            for m in range(2):
                probe_re = probe_f32[m, rows, :side]
                probe_im = probe_f32[m, rows, side:]
                cols = slice(m * side, (m + 1) * side)
                wave[rows, cols] = (probe_re * obj_re - probe_im * obj_im).astype(jnp.bfloat16)
                wave[side + chunk : side + chunk + CHUNK, cols] = (
                    probe_re * obj_im + probe_im * obj_re
                ).astype(jnp.bfloat16)
        for m in range(2):
            cols = slice(m * side, (m + 1) * side)
            stacked = jnp.dot(plain[...], wave[:, cols], preferred_element_type=jnp.float32)
            half_buf[cols, :side] = stacked[:side].astype(jnp.bfloat16)
            half_buf[cols, side:] = stacked[side:].astype(jnp.bfloat16)
        for m in range(2):
            rows = slice(m * side, (m + 1) * side)
            far[rows] = jnp.dot(half_buf[rows], turned[...], preferred_element_type=jnp.float32)
        for chunk in range(0, side, CHUNK):
            parts = []
            power = 1.0
            for m in range(2):
                rows = slice(m * side + chunk, m * side + chunk + CHUNK)
                far_re, far_im = far[rows, :side], far[rows, side:]
                power = power + (far_re * far_re + far_im * far_im)
                parts.append((far_re, far_im))
            level = inten[slot, chunk : chunk + CHUNK].astype(jnp.float32) + 1.0
            ratio = 1.0 - level * lax.rsqrt(level * power)
            for m in range(2):
                cols = slice(m * side, (m + 1) * side)
                wave[chunk : chunk + CHUNK, cols] = (parts[m][0] * ratio).astype(jnp.bfloat16)
                wave[side + chunk : side + chunk + CHUNK, cols] = (parts[m][1] * ratio).astype(
                    jnp.bfloat16
                )
        for m in range(2):
            cols = slice(m * side, (m + 1) * side)
            stacked = jnp.dot(turned[...], wave[:, cols], preferred_element_type=jnp.float32)
            half_buf[cols, :side] = stacked[:side].astype(jnp.bfloat16)
            half_buf[cols, side:] = stacked[side:].astype(jnp.bfloat16)
        for m in range(2):
            rows = slice(m * side, (m + 1) * side)
            far[rows] = jnp.dot(half_buf[rows], plain[...], preferred_element_type=jnp.float32)
        for chunk in range(0, side, CHUNK):
            rows = slice(chunk, chunk + CHUNK)
            obj_re, obj_im = patch[0, rows], patch[1, rows]
            terms = [0.0, 0.0]
            for m in range(2):
                probe_re = probe_f32[m, rows, :side]
                probe_im = probe_f32[m, rows, side:]
                far_rows = slice(m * side + chunk, m * side + chunk + CHUNK)
                back_re, back_im = far[far_rows, :side], far[far_rows, side:]
                terms[0] = terms[0] + (probe_re * back_re + probe_im * back_im)
                terms[1] = terms[1] + (probe_re * back_im - probe_im * back_re)
                probe_grad[m, rows, :side] += obj_re * back_re + obj_im * back_im
                probe_grad[m, rows, side:] += obj_re * back_im - obj_im * back_re
            target = pl.ds(row + chunk, CHUNK)
            for plane in range(2):
                left = pltpu.roll(terms[plane][:, :LANES], off, 1)
                right = pltpu.roll(terms[plane][:, LANES:], off, 1)
                grad[block, plane, target, :] += jnp.where(lane < off, 0.0, left)
                grad[block + 1, plane, target, :] += jnp.where(lane < off, left, right)
                grad[block + 2, plane, target, :] += jnp.where(lane < off, right, 0.0)

    width = blocks // owners
    sends = []
    for step in range(owners // 2):
        for swap in range(2):
            owner = 2 * lax.rem(sub + step, owners // 2) + (mode + swap) % 2
            index = 2 * step + swap
            sends.append(
                pltpu.make_async_copy(
                    grad.at[pl.ds(owner * width, width)], outs[index], out_sems.at[index]
                )
            )
    for copy in sends:
        copy.start()
    for copy in sends:
        copy.wait()


def point_sums(place, counts, spots, own, halos, probe, inten, owners):
    plain, turned = dft_tables(probe.shape[1])
    side = probe.shape[1]
    blocks = own.shape[2] // LANES
    rows = own.shape[1] + side
    piece = jax.ShapeDtypeStruct((blocks // owners, 2, rows, LANES), jnp.float32)
    smem = pl.BlockSpec(memory_space=pltpu.SMEM)
    vmem = pl.BlockSpec(memory_space=pltpu.VMEM)
    anywhere = pl.BlockSpec(memory_space=pl.ANY)
    slots = inten.shape[0]
    return pl.pallas_call(
        functools.partial(point_kernel, owners=owners),
        out_shape=[piece] * owners
        + [jax.ShapeDtypeStruct((2, side, 2 * side), jnp.float32)],
        in_specs=[smem] * 3 + [anywhere] * 5 + [vmem] * 4,
        out_specs=[anywhere] * owners + [vmem],
        scratch_shapes=[
            pltpu.VMEM((2, blocks + 1, rows, LANES), jnp.float32),
            pltpu.VMEM((blocks + 1, 2, rows, LANES), jnp.float32),
            pltpu.VMEM((2, side, 2 * side), jnp.float32),
            pltpu.VMEM((2, side, side), jnp.float32),
            pltpu.VMEM((2 * side, 2 * side), jnp.bfloat16),
            pltpu.VMEM((2 * side, 2 * side), jnp.bfloat16),
            pltpu.VMEM((2 * side, 2 * side), jnp.float32),
            pltpu.SemaphoreType.DMA((6 * blocks,)),
            pltpu.SemaphoreType.DMA((owners,)),
        ],
        compiler_params=pltpu.CompilerParams(vmem_limit_bytes=60 * 1024 * 1024),
        cost_estimate=pl.CostEstimate(
            flops=slots * 32 * 2 * side**3, bytes_accessed=16 * 1024 * 1024, transcendentals=0
        ),
        name="point_sums",
    )(place, counts, spots, own, *halos, probe, inten, jnp.asarray(plain), jnp.asarray(turned))


def shift_up(cells, axis):
    count = lax.axis_size(axis)
    return lax.ppermute(cells, axis, [(i, i + 1) for i in range(count - 1)])


def shift_down(cells, axis):
    count = lax.axis_size(axis)
    return lax.ppermute(cells, axis, [(i + 1, i) for i in range(count - 1)])


def rotated(cells, axis, step):
    count = lax.axis_size(axis)
    return lax.ppermute(cells, axis, [(i, (i + step) % count) for i in range(count)])


def scatter_sum(cells, axis):
    count = lax.axis_size(axis)
    share = cells.shape[0] // count
    index = lax.axis_index(axis)
    turned = lax.dynamic_slice_in_dim(
        jnp.concatenate([cells, cells]), index * share, cells.shape[0], 0
    )
    total = turned[:share]
    for step in range(1, count):
        total = total + rotated(turned[step * share : (step + 1) * share], axis, step)
    return total


def gather_parts(part, axis):
    count = lax.axis_size(axis)
    index = lax.axis_index(axis)
    parts = [part] + [rotated(part, axis, step) for step in range(1, count)]
    parts = jnp.concatenate(parts[:1] + parts[:0:-1])
    share = part.shape[0]
    start = (count - index) % count * share
    return lax.dynamic_slice_in_dim(jnp.concatenate([parts, parts]), start, count * share, 0)


def sum_over_strips(cells):
    if lax.axis_size("tiles") > 4:
        return lax.psum(cells, ("tiles", "sub"))
    middle = cells.shape[0] // 2
    first = scatter_sum(cells[:middle], "tiles")
    second = scatter_sum(cells[middle:], "sub")
    for step in range(1, lax.axis_size("sub")):
        first = first + rotated(first, "sub", step)
    second = scatter_sum(second, "tiles")
    second = gather_parts(second, "tiles")
    first = gather_parts(first, "tiles")
    second = gather_parts(second, "sub")
    return jnp.concatenate([first, second])


def swap(cells):
    return lax.ppermute(cells, "modes", [(0, 1), (1, 0)])


def on_device(object_field, probe, intensity, centres, counts):
    side = probe.shape[1]
    rim = side // 2
    strip_rows = object_field.shape[1]
    strip = lax.axis_index("tiles")
    sub = lax.axis_index("sub")
    mode = lax.axis_index("modes")
    subs = lax.axis_size("sub")
    owners = subs * lax.axis_size("modes")
    place = jnp.stack([strip, sub, mode]).astype(jnp.int32)

    own_plane = lax.dynamic_index_in_dim(object_field, mode, 0, keepdims=False)
    up_a = shift_up(own_plane[strip_rows - rim :], "tiles")
    dn_a = shift_down(own_plane[:rim], "tiles")
    halos = (up_a, dn_a, swap(up_a), swap(dn_a))

    sums = point_sums(
        place, counts, centres.reshape(-1), object_field, halos, probe, intensity[0], owners
    )
    probe_grad = sums[owners]

    mine = []
    for step in range(subs):
        mine.append(sums[2 * step] + swap(sums[2 * step + 1]))
    total = mine[0]
    for step in range(1, subs):
        total = total + lax.ppermute(
            mine[step], "sub", [(i, (i + step) % subs) for i in range(subs)]
        )
    total = total.transpose(1, 2, 0, 3).reshape(2, strip_rows + side, -1)
    core = total[:, rim : rim + strip_rows]
    core = core.at[:, :rim].add(shift_up(total[:, rim + strip_rows :], "tiles"))
    core = core.at[:, strip_rows - rim :].add(shift_down(total[:, :rim], "tiles"))

    kept = lax.dynamic_index_in_dim(probe_grad, mode, 0, keepdims=False)
    given = lax.dynamic_index_in_dim(probe_grad, 1 - mode, 0, keepdims=False)
    kept = sum_over_strips(kept + swap(given))
    other = swap(kept)
    probe_out = jnp.where(mode == 0, jnp.stack([kept, other]), jnp.stack([other, kept]))
    return (core, probe_out)


def solution(mesh):
    return jax.shard_map(
        on_device,
        mesh=mesh,
        in_specs=(
            P(None, ("groups", "tiles"), None),
            P("groups", None, None),
            P(("groups", "tiles"), ("sub", "modes"), None, None),
            P(("groups", "tiles"), None, None),
            P(("groups", "tiles")),
        ),
        out_specs=(P(None, ("groups", "tiles"), ("sub", "modes")), P("groups", None, None)),
        check_vma=False,
    )
```

time: 334 us -> 121 us (0.36)
  local copies, waits for them, and re-layouts: 115 us -> 6.46 us
  between operations: 46.6 us -> 1.73 us
  waiting for transfers between devices: 92.7 us -> 51.7 us
  other arithmetic: 44.9 us -> 4.9 us
  Pallas kernels: 0 us -> 23 us
  starting transfers between devices: 17.5 us -> 32.6 us
  matrix products: 14.4 us -> 0 us
    psum x1 -> x0, waiting for transfers between devices: 67.4 us -> none  [on_device(): probe_grad = lax.psum(probe_local, ('tiles', 'sub', 'modes'))]
    dynamic_update_slice x8 -> x0, local copies, waits for them, and re-layouts: 50 us -> none  [on_device(): lax.dynamic_update_slice(grad, lax.dynamic_slice(grad, start, (2, patch_s...]
    gather x24 -> x0, local copies, waits for them, and re-layouts: 32.4 us -> none
    ppermute x4 -> x26, waiting for transfers between devices: 25.2 us -> 51.7 us  [the longest x15 17.7 us: rotated(): lax.ppermute(cells, axis, [(i, (i + step) % count) for i in range(count)])]
    pallas_call x0 -> x1, Pallas kernels: none -> 23 us  [point_sums(): pl.pallas_call(functools.partial(point_kernel, owners=owners), out_shape=...]
    ppermute x4 -> x26, starting transfers between devices: 17.4 us -> 32.6 us  [the longest x15 20.3 us: rotated(): lax.ppermute(cells, axis, [(i, (i + step) % count) for i in range(count)])]
    dot_general x4 -> x0, matrix products: 14.4 us -> none  [the longest x2 9.45 us: transform(): jnp.einsum('ak,smkc->smac', left, field, preferred_element_type=jnp.float32)]
    add x8 -> x4, other arithmetic: 14.5 us -> 1.26 us  [the longest x1 1.12 us: on_device(): kept = sum_over_strips(kept + swap(given))]
  transfers between devices with their start and end apart: 6 -> 26, of which waited for: 3 -> 13; matrix products, arithmetic and copies ran while one was open for 5% -> 6% of each run, Pallas kernels for 0% -> 0%
where the time goes in v1:
time: 121 us; the launch traced here: 120 us
  waiting for transfers between devices  51.7 us (43%)
  starting transfers between devices  32.6 us (27%)
  Pallas kernels  23 us (19%)
  local copies, waits for them, and re-layouts  6.46 us (5%)
  other arithmetic  4.9 us (4%)
  between operations  1.73 us (1%)
    pallas_call x1, Pallas kernels, point_sums(): pl.pallas_call(functools.partial(point_kernel, owners=owners), out_shape=...  23 us
    ppermute x15, starting transfers between devices, rotated(): lax.ppermute(cells, axis, [(i, (i + step) % count) for i in range(count)])  20.3 us
    ppermute x15, waiting for transfers between devices, rotated(): lax.ppermute(cells, axis, [(i, (i + step) % count) for i in range(count)])  17.7 us
    ppermute x1, waiting for transfers between devices, on_device(): lax.ppermute(mine[step], 'sub', [(i, (i + step) % subs) for i in range(su...  14.2 us
    ppermute x2, waiting for transfers between devices, shift_up(): return lax.ppermute(cells, axis, [(i, i + 1) for i in range(count - 1)])  10.3 us
    ppermute x2, waiting for transfers between devices, shift_down(): return lax.ppermute(cells, axis, [(i + 1, i) for i in range(count - 1)])  8.19 us
    ppermute x2, starting transfers between devices, shift_up(): return lax.ppermute(cells, axis, [(i, i + 1) for i in range(count - 1)])  7.4 us
    ppermute x2, starting transfers between devices, shift_down(): return lax.ppermute(cells, axis, [(i + 1, i) for i in range(count - 1)])  2.58 us
  transfers between devices with their start and end apart: 26, of which 13 were waited for; matrix products, arithmetic and copies ran while one was open for 6% of the time, Pallas kernels for 0%

profile of v1, /device:TPU:0, one launch (start us, length us, event | category | flops | bytes accessed | tf_op | source)
XLA Modules:
  0.0 120.3 jit_solution(2176808072145124915)
XLA Ops:
  0.6 1.3 %dynamic-slice_bitcast_fusion = (f32[128,1024]{1,0:T(8,128)S(1)}, f32[128,1024]{1,0:T(8,128)S(1)}) fusion(f32[2,256,1024]{2,1,0:T(8,128)} %own.1, s32[]{:T(128)S(6)} %select_n.48, s32[]{:T(128)S(6)} %add.112), kind=kLoop, calls=%fused_computation.2 | loop fusion | bytes 2097160 | tf_op jit(solution)/shard_map/slice | solution.py:288
  2.0 5.0 %collective-permute-start = (f32[128,1024]{1,0:T(8,128)S(1)}, f32[128,1024]{1,0:T(8,128)S(1)}, u32[]{:S(2)}, u32[]{:S(2)}) collective-permute-start(f32[128,1024]{1,0:T(8,128)S(1)} %get-tuple-element.43), channel_id=1, source_target_pairs={{0,4},{4,8},{8,12},{1,5},{5,9},{9,13},{2,6},{6,10},{10,14},{3,7},{... | collective-permute-start | bytes 1572872 | tf_op jit(solution)/shard_map/ppermute | solution.py:220
  6.9 1.3 %collective-permute-start.1 = (f32[128,1024]{1,0:T(8,128)S(1)}, f32[128,1024]{1,0:T(8,128)S(1)}, u32[]{:S(2)}, u32[]{:S(2)}) collective-permute-start(f32[128,1024]{1,0:T(8,128)S(1)} %get-tuple-element.42), channel_id=1, source_target_pairs={{4,0},{8,4},{12,8},{5,1},{9,5},{13,9},{6,2},{10,6},{14,10},{7,3},{... | collective-permute-start | bytes 1572872 | tf_op jit(solution)/shard_map/ppermute | solution.py:225
  8.2 9.8 %collective-permute-done.up_a = f32[128,1024]{1,0:T(8,128)S(1)} collective-permute-done((f32[128,1024]{1,0:T(8,128)S(1)}, f32[128,1024]{1,0:T(8,128)S(1)}, u32[]{:S(2)}, u32[]{:S(2)}) %collective-permute-start) | collective-permute-done | bytes 524320 | tf_op jit(solution)/shard_map/ppermute | solution.py:220
  18.1 4.1 %collective-permute-done.1.dn_a = f32[128,1024]{1,0:T(8,128)S(1)} collective-permute-done((f32[128,1024]{1,0:T(8,128)S(1)}, f32[128,1024]{1,0:T(8,128)S(1)}, u32[]{:S(2)}, u32[]{:S(2)}) %collective-permute-start.1) | collective-permute-done | bytes 524320 | tf_op jit(solution)/shard_map/ppermute | solution.py:225
  25.3 23.0 %point_sums.1 = (f32[2,2,512,128]{3,2,1,0:T(8,128)}, f32[2,2,512,128]{3,2,1,0:T(8,128)}, f32[2,2,512,128]{3,2,1,0:T(8,128)}, f32[2,2,512,128]{3,2,1,0:T(8,128)}, f32[2,256,512]{2,1,0:T(8,128)}) custom-call(s32[3]{0:T(128)} %pad_add_fusion.place, s32[1]{0:T(128)S(6)} %copy.29.counts, s32[64]{0:T(128)} %reshape.72.spots, f32[2,256,1024]{2,1,0:T(8,128)} %own.1, ...), custom_call_target="tpu_custom_call" | custom-call | flops 8589934592 | bytes 16777216 | tf_op jit(solution)/shard_map/point_sums/pallas_call | solution.py:193
  50.1 1.3 %collective-permute-done.9 = f32[256,512]{1,0:T(8,128)S(1)} collective-permute-done((f32[256,512]{1,0:T(8,128)S(1)}, f32[256,512]{1,0:T(8,128)S(1)}, u32[]{:S(2)}, u32[]{:S(2)}) %collective-permute-start.9) | collective-permute-done | bytes 524320 | tf_op jit(solution)/shard_map/ppermute | solution.py:272
  52.9 4.3 %collective-permute-start.11 = (f32[32,512]{1,0:T(8,128)S(1)}, f32[32,512]{1,0:T(8,128)S(1)}, u32[]{:S(2)}, u32[]{:S(2)}) collective-permute-start(f32[32,512]{1,0:T(8,128)S(1)} %get-tuple-element.51), channel_id=1, source_target_pairs={{0,8},{4,12},{8,0},{12,4},{1,9},{5,13},{9,1},{13,5},{2,10},{6,14},... | collective-permute-start | bytes 196616 | tf_op jit(solution)/shard_map/ppermute | solution.py:230
  58.3 1.8 %collective-permute-start.12 = (f32[32,512]{1,0:T(8,128)S(1)}, f32[32,512]{1,0:T(8,128)S(1)}, u32[]{:S(2)}, u32[]{:S(2)}) collective-permute-start(f32[32,512]{1,0:T(8,128)S(1)} %get-tuple-element.52), channel_id=1, source_target_pairs={{0,12},{4,0},{8,4},{12,8},{1,13},{5,1},{9,5},{13,9},{2,14},{6,2},{... | collective-permute-start | bytes 196616 | tf_op jit(solution)/shard_map/ppermute | solution.py:230
  60.2 1.3 %collective-permute-start.18 = (f32[16,512]{1,0:T(8,128)S(1)}, f32[16,512]{1,0:T(8,128)S(1)}, u32[]{:S(2)}, u32[]{:S(2)}) collective-permute-start(f32[16,512]{1,0:T(8,128)S(1)} %get-tuple-element.53), channel_id=1, source_target_pairs={{0,4},{4,8},{8,12},{12,0},{1,5},{5,9},{9,13},{13,1},{2,6},{6,10},{... | collective-permute-start | bytes 98312 | tf_op jit(solution)/shard_map/ppermute | solution.py:230
  61.5 2.7 %collective-permute-start.19 = (f32[16,512]{1,0:T(8,128)S(1)}, f32[16,512]{1,0:T(8,128)S(1)}, u32[]{:S(2)}, u32[]{:S(2)}) collective-permute-start(f32[16,512]{1,0:T(8,128)S(1)} %get-tuple-element.54), channel_id=1, source_target_pairs={{0,8},{4,12},{8,0},{12,4},{1,9},{5,13},{9,1},{13,5},{2,10},{6,14},... | collective-permute-start | bytes 98312 | tf_op jit(solution)/shard_map/ppermute | solution.py:230
  64.1 2.9 %collective-permute-start.20 = (f32[16,512]{1,0:T(8,128)S(1)}, f32[16,512]{1,0:T(8,128)S(1)}, u32[]{:S(2)}, u32[]{:S(2)}) collective-permute-start(f32[16,512]{1,0:T(8,128)S(1)} %get-tuple-element.55), channel_id=1, source_target_pairs={{0,12},{4,0},{8,4},{12,8},{1,13},{5,1},{9,5},{13,9},{2,14},{6,2},{... | collective-permute-start | bytes 98312 | tf_op jit(solution)/shard_map/ppermute | solution.py:230
  67.6 1.5 %collective-permute-done.20 = f32[16,512]{1,0:T(8,128)S(1)} collective-permute-done((f32[16,512]{1,0:T(8,128)S(1)}, f32[16,512]{1,0:T(8,128)S(1)}, u32[]{:S(2)}, u32[]{:S(2)}) %collective-permute-start.20) | collective-permute-done | bytes 32800 | tf_op jit(solution)/shard_map/ppermute | solution.py:230
  69.2 3.7 %collective-permute-start.21 = (f32[16,512]{1,0:T(8,128)S(1)}, f32[16,512]{1,0:T(8,128)S(1)}, u32[]{:S(2)}, u32[]{:S(2)}) collective-permute-start(f32[16,512]{1,0:T(8,128)S(1)} %get-tuple-element.41), channel_id=1, source_target_pairs={{0,12},{4,0},{8,4},{12,8},{1,13},{5,1},{9,5},{13,9},{2,14},{6,2},{... | collective-permute-start | bytes 98312 | tf_op jit(solution)/shard_map/ppermute | solution.py:230
  74.4 1.5 %collective-permute-start.22 = (f32[16,512]{1,0:T(8,128)S(1)}, f32[16,512]{1,0:T(8,128)S(1)}, u32[]{:S(2)}, u32[]{:S(2)}) collective-permute-start(f32[16,512]{1,0:T(8,128)S(1)} %get-tuple-element.41), channel_id=1, source_target_pairs={{0,8},{4,12},{8,0},{12,4},{1,9},{5,13},{9,1},{13,5},{2,10},{6,14},... | collective-permute-start | bytes 98312 | tf_op jit(solution)/shard_map/ppermute | solution.py:230
  75.9 4.6 %collective-permute-done.22 = f32[16,512]{1,0:T(8,128)S(1)} collective-permute-done((f32[16,512]{1,0:T(8,128)S(1)}, f32[16,512]{1,0:T(8,128)S(1)}, u32[]{:S(2)}, u32[]{:S(2)}) %collective-permute-start.22) | collective-permute-done | bytes 32800 | tf_op jit(solution)/shard_map/ppermute | solution.py:230
  81.0 5.2 %collective-permute-done.23 = f32[16,512]{1,0:T(8,128)S(1)} collective-permute-done((f32[16,512]{1,0:T(8,128)S(1)}, f32[16,512]{1,0:T(8,128)S(1)}, u32[]{:S(2)}, u32[]{:S(2)}) %collective-permute-start.23) | collective-permute-done | bytes 32800 | tf_op jit(solution)/shard_map/ppermute | solution.py:230
  87.1 1.5 %collective-permute-start.6 = (f32[2,2,512,128]{3,2,1,0:T(8,128)S(1)}, f32[2,2,512,128]{3,2,1,0:T(8,128)S(1)}, u32[]{:S(2)}, u32[]{:S(2)}) collective-permute-start(f32[2,2,512,128]{3,2,1,0:T(8,128)S(1)} %add.88), channel_id=1, source_target_pairs={{0,2},{2,0},{1,3},{3,1},{4,6},{6,4},{5,7},{7,5},{8,10},{10,8},{9,1... | collective-permute-start | bytes 3145736 | tf_op jit(solution)/shard_map/ppermute | solution.py:301
  88.6 3.7 %collective-permute-done.16 = f32[32,512]{1,0:T(8,128)S(1)} collective-permute-done((f32[32,512]{1,0:T(8,128)S(1)}, f32[32,512]{1,0:T(8,128)S(1)}, u32[]{:S(2)}, u32[]{:S(2)}) %collective-permute-start.16) | collective-permute-done | bytes 65568 | tf_op jit(solution)/shard_map/ppermute | solution.py:230
  93.1 14.2 %collective-permute-done.6 = f32[2,2,512,128]{3,2,1,0:T(8,128)S(1)} collective-permute-done((f32[2,2,512,128]{3,2,1,0:T(8,128)S(1)}, f32[2,2,512,128]{3,2,1,0:T(8,128)S(1)}, u32[]{:S(2)}, u32[]{:S(2)}) %collective-permute-start.6) | collective-permute-done | bytes 1048608 | tf_op jit(solution)/shard_map/ppermute | solution.py:301
  108.6 2.4 %collective-permute-start.7 = (f32[2,128,256]{1,2,0:T(8,128)}, f32[2,128,256]{1,2,0:T(8,128)S(1)}, u32[]{:S(2)}, u32[]{:S(2)}) collective-permute-start(f32[2,128,256]{1,2,0:T(8,128)} %get-tuple-element.45), channel_id=1, source_target_pairs={{0,4},{4,8},{8,12},{1,5},{5,9},{9,13},{2,6},{6,10},{10,14},{3,7},{... | collective-permute-start | bytes 786440 | tf_op jit(solution)/shard_map/ppermute | solution.py:220
  111.0 1.3 %collective-permute-start.8 = (f32[2,128,256]{1,2,0:T(8,128)S(1)}, f32[2,128,256]{1,2,0:T(8,128)S(1)}, u32[]{:S(2)}, u32[]{:S(2)}) collective-permute-start(f32[2,128,256]{1,2,0:T(8,128)S(1)} %get-tuple-element.44), channel_id=1, source_target_pairs={{4,0},{8,4},{12,8},{5,1},{9,5},{13,9},{6,2},{10,6},{14,10},{7,3},{... | collective-permute-start | bytes 786440 | tf_op jit(solution)/shard_map/ppermute | solution.py:225
  112.3 2.3 %maximum_select_fusion = f32[2,256,512]{2,1,0:T(8,128)} fusion(f32[1,256,512]{2,1,0:T(8,128)} %bitcast.11, f32[1,256,512]{2,1,0:T(8,128)S(1)} %get-tuple-element.46, pred[]{:T(512)S(6)} %eq.7), kind=kLoop, calls=%fused_computation | loop fusion | flops 786432 | bytes 2097153 | tf_op jit(solution)/shard_map/jit(_where)/select_n | solution.py:313
  115.2 4.0 %collective-permute-done.8 = f32[2,128,256]{1,2,0:T(8,128)S(1)} collective-permute-done((f32[2,128,256]{1,2,0:T(8,128)S(1)}, f32[2,128,256]{1,2,0:T(8,128)S(1)}, u32[]{:S(2)}, u32[]{:S(2)}) %collective-permute-start.8) | collective-permute-done | bytes 262176 | tf_op jit(solution)/shard_map/ppermute | solution.py:225
  (87 shorter events, 13.8 us)
Async XLA Ops:
  2.0 16.1 %collective-permute-start = (f32[128,1024]{1,0:T(8,128)S(1)}, f32[128,1024]{1,0:T(8,128)S(1)}, u32[]{:S(2)}, u32[]{:S(2)}) collective-permute-start(f32[128,1024]{1,0:T(8,128)S(1)} %get-tuple-element.43), channel_id=1, source_target_pairs={{0,4},{4,8},{8,12},{1,5},{5,9},{9,13},{2,6},{6,10},{10,14},{3,7},{... | collective-permute-start | bytes 1572872 | tf_op jit(solution)/shard_map/ppermute | solution.py:220
  6.9 15.3 %collective-permute-start.1 = (f32[128,1024]{1,0:T(8,128)S(1)}, f32[128,1024]{1,0:T(8,128)S(1)}, u32[]{:S(2)}, u32[]{:S(2)}) collective-permute-start(f32[128,1024]{1,0:T(8,128)S(1)} %get-tuple-element.42), channel_id=1, source_target_pairs={{4,0},{8,4},{12,8},{5,1},{9,5},{13,9},{6,2},{10,6},{14,10},{7,3},{... | collective-permute-start | bytes 1572872 | tf_op jit(solution)/shard_map/ppermute | solution.py:225
  18.1 6.3 %collective-permute-start.2 = (f32[128,1024]{1,0:T(8,128)S(1)}, f32[128,1024]{1,0:T(8,128)S(1)}, u32[]{:S(2)}, u32[]{:S(2)}) collective-permute-start(f32[128,1024]{1,0:T(8,128)S(1)} %collective-permute-done.up_a), channel_id=1, source_target_pairs={{0,1},{1,0},{2,3},{3,2},{4,5},{5,4},{6,7},{7,6},{8,9},{9,8},{10,11... | collective-permute-start | bytes 1572872 | tf_op jit(solution)/shard_map/ppermute | solution.py:272
  49.5 36.8 %collective-permute-start.5 = (f32[2,2,512,128]{3,2,1,0:T(8,128)}, f32[2,2,512,128]{3,2,1,0:T(8,128)S(1)}, u32[]{:S(2)}, u32[]{:S(2)}) collective-permute-start(f32[2,2,512,128]{3,2,1,0:T(8,128)} %get-tuple-element.34), channel_id=1, source_target_pairs={{0,1},{1,0},{2,3},{3,2},{4,5},{5,4},{6,7},{7,6},{8,9},{9,8},{10,11... | collective-permute-start | bytes 3145736 | tf_op jit(solution)/shard_map/ppermute | solution.py:272
  50.0 43.1 %collective-permute-start.4 = (f32[2,2,512,128]{3,2,1,0:T(8,128)}, f32[2,2,512,128]{3,2,1,0:T(8,128)S(1)}, u32[]{:S(2)}, u32[]{:S(2)}) collective-permute-start(f32[2,2,512,128]{3,2,1,0:T(8,128)} %get-tuple-element.32), channel_id=1, source_target_pairs={{0,1},{1,0},{2,3},{3,2},{4,5},{5,4},{6,7},{7,6},{8,9},{9,8},{10,11... | collective-permute-start | bytes 3145736 | tf_op jit(solution)/shard_map/ppermute | solution.py:272
  52.7 5.6 %collective-permute-start.17 = (f32[64,512]{1,0:T(8,128)S(1)}, f32[64,512]{1,0:T(8,128)S(1)}, u32[]{:S(2)}, u32[]{:S(2)}) collective-permute-start(f32[64,512]{1,0:T(8,128)S(1)} %slice.139), channel_id=1, source_target_pairs={{0,2},{2,0},{1,3},{3,1},{4,6},{6,4},{5,7},{7,5},{8,10},{10,8},{9,1... | collective-permute-start | bytes 393224 | tf_op jit(solution)/shard_map/ppermute | solution.py:230
  52.8 7.3 %collective-permute-start.10 = (f32[32,512]{1,0:T(8,128)S(1)}, f32[32,512]{1,0:T(8,128)S(1)}, u32[]{:S(2)}, u32[]{:S(2)}) collective-permute-start(f32[32,512]{1,0:T(8,128)S(1)} %get-tuple-element.50), channel_id=1, source_target_pairs={{0,4},{4,8},{8,12},{12,0},{1,5},{5,9},{9,13},{13,1},{2,6},{6,10},{... | collective-permute-start | bytes 196616 | tf_op jit(solution)/shard_map/ppermute | solution.py:230
  52.9 8.6 %collective-permute-start.11 = (f32[32,512]{1,0:T(8,128)S(1)}, f32[32,512]{1,0:T(8,128)S(1)}, u32[]{:S(2)}, u32[]{:S(2)}) collective-permute-start(f32[32,512]{1,0:T(8,128)S(1)} %get-tuple-element.51), channel_id=1, source_target_pairs={{0,8},{4,12},{8,0},{12,4},{1,9},{5,13},{9,1},{13,5},{2,10},{6,14},... | collective-permute-start | bytes 196616 | tf_op jit(solution)/shard_map/ppermute | solution.py:230
  58.3 5.9 %collective-permute-start.12 = (f32[32,512]{1,0:T(8,128)S(1)}, f32[32,512]{1,0:T(8,128)S(1)}, u32[]{:S(2)}, u32[]{:S(2)}) collective-permute-start(f32[32,512]{1,0:T(8,128)S(1)} %get-tuple-element.52), channel_id=1, source_target_pairs={{0,12},{4,0},{8,4},{12,8},{1,13},{5,1},{9,5},{13,9},{2,14},{6,2},{... | collective-permute-start | bytes 196616 | tf_op jit(solution)/shard_map/ppermute | solution.py:230
  60.2 6.9 %collective-permute-start.18 = (f32[16,512]{1,0:T(8,128)S(1)}, f32[16,512]{1,0:T(8,128)S(1)}, u32[]{:S(2)}, u32[]{:S(2)}) collective-permute-start(f32[16,512]{1,0:T(8,128)S(1)} %get-tuple-element.53), channel_id=1, source_target_pairs={{0,4},{4,8},{8,12},{12,0},{1,5},{5,9},{9,13},{13,1},{2,6},{6,10},{... | collective-permute-start | bytes 98312 | tf_op jit(solution)/shard_map/ppermute | solution.py:230
  61.5 6.2 %collective-permute-start.19 = (f32[16,512]{1,0:T(8,128)S(1)}, f32[16,512]{1,0:T(8,128)S(1)}, u32[]{:S(2)}, u32[]{:S(2)}) collective-permute-start(f32[16,512]{1,0:T(8,128)S(1)} %get-tuple-element.54), channel_id=1, source_target_pairs={{0,8},{4,12},{8,0},{12,4},{1,9},{5,13},{9,1},{13,5},{2,10},{6,14},... | collective-permute-start | bytes 98312 | tf_op jit(solution)/shard_map/ppermute | solution.py:230
  64.1 5.0 %collective-permute-start.20 = (f32[16,512]{1,0:T(8,128)S(1)}, f32[16,512]{1,0:T(8,128)S(1)}, u32[]{:S(2)}, u32[]{:S(2)}) collective-permute-start(f32[16,512]{1,0:T(8,128)S(1)} %get-tuple-element.55), channel_id=1, source_target_pairs={{0,12},{4,0},{8,4},{12,8},{1,13},{5,1},{9,5},{13,9},{2,14},{6,2},{... | collective-permute-start | bytes 98312 | tf_op jit(solution)/shard_map/ppermute | solution.py:230
  67.1 5.7 %collective-permute-start.13 = (f32[32,512]{1,0:T(8,128)S(1)}, f32[32,512]{1,0:T(8,128)S(1)}, u32[]{:S(2)}, u32[]{:S(2)}) collective-permute-start(f32[32,512]{1,0:T(8,128)S(1)} %fusion.9), channel_id=1, source_target_pairs={{0,2},{2,0},{1,3},{3,1},{4,6},{6,4},{5,7},{7,5},{8,10},{10,8},{9,1... | collective-permute-start | bytes 196616 | tf_op jit(solution)/shard_map/ppermute | solution.py:230
  69.2 5.3 %collective-permute-start.21 = (f32[16,512]{1,0:T(8,128)S(1)}, f32[16,512]{1,0:T(8,128)S(1)}, u32[]{:S(2)}, u32[]{:S(2)}) collective-permute-start(f32[16,512]{1,0:T(8,128)S(1)} %get-tuple-element.41), channel_id=1, source_target_pairs={{0,12},{4,0},{8,4},{12,8},{1,13},{5,1},{9,5},{13,9},{2,14},{6,2},{... | collective-permute-start | bytes 98312 | tf_op jit(solution)/shard_map/ppermute | solution.py:230
  72.8 14.2 %collective-permute-start.14 = (f32[32,512]{1,0:T(8,128)S(1)}, f32[32,512]{1,0:T(8,128)S(1)}, u32[]{:S(2)}, u32[]{:S(2)}) collective-permute-start(f32[32,512]{1,0:T(8,128)S(1)} %get-tuple-element.39), channel_id=1, source_target_pairs={{0,12},{4,0},{8,4},{12,8},{1,13},{5,1},{9,5},{13,9},{2,14},{6,2},{... | collective-permute-start | bytes 196616 | tf_op jit(solution)/shard_map/ppermute | solution.py:230
  72.9 15.7 %collective-permute-start.15 = (f32[32,512]{1,0:T(8,128)S(1)}, f32[32,512]{1,0:T(8,128)S(1)}, u32[]{:S(2)}, u32[]{:S(2)}) collective-permute-start(f32[32,512]{1,0:T(8,128)S(1)} %get-tuple-element.39), channel_id=1, source_target_pairs={{0,8},{4,12},{8,0},{12,4},{1,9},{5,13},{9,1},{13,5},{2,10},{6,14},... | collective-permute-start | bytes 196616 | tf_op jit(solution)/shard_map/ppermute | solution.py:230
  74.4 6.1 %collective-permute-start.22 = (f32[16,512]{1,0:T(8,128)S(1)}, f32[16,512]{1,0:T(8,128)S(1)}, u32[]{:S(2)}, u32[]{:S(2)}) collective-permute-start(f32[16,512]{1,0:T(8,128)S(1)} %get-tuple-element.41), channel_id=1, source_target_pairs={{0,8},{4,12},{8,0},{12,4},{1,9},{5,13},{9,1},{13,5},{2,10},{6,14},... | collective-permute-start | bytes 98312 | tf_op jit(solution)/shard_map/ppermute | solution.py:230
  80.5 5.7 %collective-permute-start.23 = (f32[16,512]{1,0:T(8,128)S(1)}, f32[16,512]{1,0:T(8,128)S(1)}, u32[]{:S(2)}, u32[]{:S(2)}) collective-permute-start(f32[16,512]{1,0:T(8,128)S(1)} %get-tuple-element.41), channel_id=1, source_target_pairs={{0,4},{4,8},{8,12},{12,0},{1,5},{5,9},{9,13},{13,1},{2,6},{6,10},{... | collective-permute-start | bytes 98312 | tf_op jit(solution)/shard_map/ppermute | solution.py:230
  86.2 6.1 %collective-permute-start.16 = (f32[32,512]{1,0:T(8,128)S(1)}, f32[32,512]{1,0:T(8,128)S(1)}, u32[]{:S(2)}, u32[]{:S(2)}) collective-permute-start(f32[32,512]{1,0:T(8,128)S(1)} %get-tuple-element.39), channel_id=1, source_target_pairs={{0,4},{4,8},{8,12},{12,0},{1,5},{5,9},{9,13},{13,1},{2,6},{6,10},{... | collective-permute-start | bytes 196616 | tf_op jit(solution)/shard_map/ppermute | solution.py:230
  86.3 6.5 %collective-permute-start.24 = (f32[64,512]{1,0:T(8,128)S(1)}, f32[64,512]{1,0:T(8,128)S(1)}, u32[]{:S(2)}, u32[]{:S(2)}) collective-permute-start(f32[64,512]{1,0:T(8,128)S(1)} %constant_dynamic-slice_fusion), channel_id=1, source_target_pairs={{0,2},{2,0},{1,3},{3,1},{4,6},{6,4},{5,7},{7,5},{8,10},{10,8},{9,1... | collective-permute-start | bytes 393224 | tf_op jit(solution)/shard_map/ppermute | solution.py:230
  87.1 20.3 %collective-permute-start.6 = (f32[2,2,512,128]{3,2,1,0:T(8,128)S(1)}, f32[2,2,512,128]{3,2,1,0:T(8,128)S(1)}, u32[]{:S(2)}, u32[]{:S(2)}) collective-permute-start(f32[2,2,512,128]{3,2,1,0:T(8,128)S(1)} %add.88), channel_id=1, source_target_pairs={{0,2},{2,0},{1,3},{3,1},{4,6},{6,4},{5,7},{7,5},{8,10},{10,8},{9,1... | collective-permute-start | bytes 3145736 | tf_op jit(solution)/shard_map/ppermute | solution.py:301
  93.0 19.3 %collective-permute-start.25 = (f32[256,512]{1,0:T(8,128)S(1)}, f32[256,512]{1,0:T(8,128)}, u32[]{:S(2)}, u32[]{:S(2)}) collective-permute-start(f32[256,512]{1,0:T(8,128)S(1)} %get-tuple-element.47), channel_id=1, source_target_pairs={{0,1},{1,0},{2,3},{3,2},{4,5},{5,4},{6,7},{7,6},{8,9},{9,8},{10,11... | collective-permute-start | bytes 1572872 | tf_op jit(solution)/shard_map/ppermute | solution.py:272
  108.6 6.6 %collective-permute-start.7 = (f32[2,128,256]{1,2,0:T(8,128)}, f32[2,128,256]{1,2,0:T(8,128)S(1)}, u32[]{:S(2)}, u32[]{:S(2)}) collective-permute-start(f32[2,128,256]{1,2,0:T(8,128)} %get-tuple-element.45), channel_id=1, source_target_pairs={{0,4},{4,8},{8,12},{1,5},{5,9},{9,13},{2,6},{6,10},{10,14},{3,7},{... | collective-permute-start | bytes 786440 | tf_op jit(solution)/shard_map/ppermute | solution.py:220
  111.0 8.3 %collective-permute-start.8 = (f32[2,128,256]{1,2,0:T(8,128)S(1)}, f32[2,128,256]{1,2,0:T(8,128)S(1)}, u32[]{:S(2)}, u32[]{:S(2)}) collective-permute-start(f32[2,128,256]{1,2,0:T(8,128)S(1)} %get-tuple-element.44), channel_id=1, source_target_pairs={{4,0},{8,4},{12,8},{5,1},{9,5},{13,9},{6,2},{10,6},{14,10},{7,3},{... | collective-permute-start | bytes 786440 | tf_op jit(solution)/shard_map/ppermute | solution.py:225
  (9 other events, 90.6 us)

commit v2 on v1

--- a/solution.py
+++ b/solution.py
@@ -41,9 +41,8 @@
     *rest,
     owners,
 ):
-    outs = rest[:owners]
-    probe_grad = rest[owners]
-    field, grad, probe_f32, patch, wave, half_buf, far, sems, out_sems = rest[owners + 1 :]
+    keep_obj, give_mine, give_others, keep_probe, give_probe = rest[:5]
+    field, grad, probe_grad, probe_f32, patch, wave, half_buf, far, sems, out_sems = rest[5:]
     strip, sub, mode = place[0], place[1], place[2]
     member = sub * 2 + mode
     side = probe.shape[1]
@@ -165,15 +164,20 @@
 
     width = blocks // owners
     sends = []
-    for step in range(owners // 2):
-        for swap in range(2):
-            owner = 2 * lax.rem(sub + step, owners // 2) + (mode + swap) % 2
-            index = 2 * step + swap
-            sends.append(
-                pltpu.make_async_copy(
-                    grad.at[pl.ds(owner * width, width)], outs[index], out_sems.at[index]
-                )
-            )
+
+    def send(src, dst):
+        sends.append(pltpu.make_async_copy(src, dst, out_sems.at[len(sends)]))
+
+    send(probe_grad.at[1 - mode], give_probe)
+    send(probe_grad.at[mode], keep_probe)
+    for step in list(range(1, owners // 2)) + [0]:
+        owner = 2 * lax.rem(sub + step, owners // 2)
+        target = give_others.at[pl.ds((step - 1) * width, width)] if step else give_mine
+        send(grad.at[pl.ds((owner + 1 - mode) * width, width)], target)
+        send(
+            grad.at[pl.ds((owner + mode) * width, width)],
+            keep_obj.at[pl.ds(step * width, width)],
+        )
     for copy in sends:
         copy.start()
     for copy in sends:
@@ -185,27 +189,32 @@
     side = probe.shape[1]
     blocks = own.shape[2] // LANES
     rows = own.shape[1] + side
-    piece = jax.ShapeDtypeStruct((blocks // owners, 2, rows, LANES), jnp.float32)
+    width = blocks // owners
+
+    def piece(count):
+        return jax.ShapeDtypeStruct((count, 2, rows, LANES), jnp.float32)
+
+    mode_sum = jax.ShapeDtypeStruct((side, 2 * side), jnp.float32)
     smem = pl.BlockSpec(memory_space=pltpu.SMEM)
     vmem = pl.BlockSpec(memory_space=pltpu.VMEM)
     anywhere = pl.BlockSpec(memory_space=pl.ANY)
     slots = inten.shape[0]
     return pl.pallas_call(
         functools.partial(point_kernel, owners=owners),
-        out_shape=[piece] * owners
-        + [jax.ShapeDtypeStruct((2, side, 2 * side), jnp.float32)],
+        out_shape=[piece(blocks // 2), piece(width), piece(blocks // 2 - width), mode_sum, mode_sum],
         in_specs=[smem] * 3 + [anywhere] * 5 + [vmem] * 4,
-        out_specs=[anywhere] * owners + [vmem],
+        out_specs=[anywhere] * 5,
         scratch_shapes=[
             pltpu.VMEM((2, blocks + 1, rows, LANES), jnp.float32),
             pltpu.VMEM((blocks + 1, 2, rows, LANES), jnp.float32),
+            pltpu.VMEM((2, side, 2 * side), jnp.float32),
             pltpu.VMEM((2, side, 2 * side), jnp.float32),
             pltpu.VMEM((2, side, side), jnp.float32),
             pltpu.VMEM((2 * side, 2 * side), jnp.bfloat16),
             pltpu.VMEM((2 * side, 2 * side), jnp.bfloat16),
             pltpu.VMEM((2 * side, 2 * side), jnp.float32),
             pltpu.SemaphoreType.DMA((6 * blocks,)),
-            pltpu.SemaphoreType.DMA((owners,)),
+            pltpu.SemaphoreType.DMA((owners + 2,)),
         ],
         compiler_params=pltpu.CompilerParams(vmem_limit_bytes=60 * 1024 * 1024),
         cost_estimate=pl.CostEstimate(
@@ -225,62 +234,121 @@
     return lax.ppermute(cells, axis, [(i + 1, i) for i in range(count - 1)])
 
 
+def swap(cells):
+    return lax.ppermute(cells, "modes", [(0, 1), (1, 0)])
+
+
 def rotated(cells, axis, step):
     count = lax.axis_size(axis)
     return lax.ppermute(cells, axis, [(i, (i + step) % count) for i in range(count)])
 
 
-def scatter_sum(cells, axis):
-    count = lax.axis_size(axis)
-    share = cells.shape[0] // count
-    index = lax.axis_index(axis)
-    turned = lax.dynamic_slice_in_dim(
-        jnp.concatenate([cells, cells]), index * share, cells.shape[0], 0
-    )
-    total = turned[:share]
-    for step in range(1, count):
-        total = total + rotated(turned[step * share : (step + 1) * share], axis, step)
-    return total
-
-
-def gather_parts(part, axis):
-    count = lax.axis_size(axis)
-    index = lax.axis_index(axis)
-    parts = [part] + [rotated(part, axis, step) for step in range(1, count)]
-    parts = jnp.concatenate(parts[:1] + parts[:0:-1])
-    share = part.shape[0]
-    start = (count - index) % count * share
-    return lax.dynamic_slice_in_dim(jnp.concatenate([parts, parts]), start, count * share, 0)
-
-
-def sum_over_strips(cells):
-    if lax.axis_size("tiles") > 4:
-        return lax.psum(cells, ("tiles", "sub"))
-    middle = cells.shape[0] // 2
-    first = scatter_sum(cells[:middle], "tiles")
-    second = scatter_sum(cells[middle:], "sub")
-    for step in range(1, lax.axis_size("sub")):
-        first = first + rotated(first, "sub", step)
-    second = scatter_sum(second, "tiles")
-    second = gather_parts(second, "tiles")
-    first = gather_parts(first, "tiles")
-    second = gather_parts(second, "sub")
-    return jnp.concatenate([first, second])
-
-
-def swap(cells):
-    return lax.ppermute(cells, "modes", [(0, 1), (1, 0)])
+def small_kernel(body, out_shape, *args, name):
+    return pl.pallas_call(
+        body,
+        out_shape=out_shape,
+        in_specs=[
+            pl.BlockSpec(memory_space=pltpu.SMEM if x.dtype == jnp.int32 else pltpu.VMEM)
+            for x in args
+        ],
+        out_specs=jax.tree.map(lambda _: pl.BlockSpec(memory_space=pltpu.VMEM), out_shape),
+        compiler_params=pltpu.CompilerParams(vmem_limit_bytes=24 * 1024 * 1024),
+        cost_estimate=pl.CostEstimate(flops=0, bytes_accessed=0, transcendentals=0),
+        name=name,
+    )(*args)
+
+
+def shape(*dims):
+    return jax.ShapeDtypeStruct(dims, jnp.float32)
+
+
+def after(cells, *earlier):
+    return lax.optimization_barrier((cells, *earlier))[0]
+
+
+def add_kernel(*refs):
+    total = refs[0][...]
+    for ref in refs[1:-1]:
+        total = total + ref[...]
+    refs[-1][...] = total
+
+
+def others_kernel(kept, got, *outs):
+    width, _, rows = outs[1].shape[:3]
+    rim = outs[0].shape[2] // 2
+    for step in range(len(outs) // 2):
+        rims, core = outs[2 * step : 2 * step + 2]
+        mine = slice((step + 1) * width, (step + 2) * width)
+        theirs = slice(step * width, (step + 1) * width)
+        rims[:, :, :rim] = kept[mine, :, :rim] + got[theirs, :, :rim]
+        rims[:, :, rim:] = kept[mine, :, rim + rows :] + got[theirs, :, rim + rows :]
+        core[...] = kept[mine, :, rim : rim + rows] + got[theirs, :, rim : rim + rows]
+
+
+def mine_kernel(kept, got, *rest):
+    above, core, below = rest[-3:]
+    width = got.shape[0]
+    rim, rows = above.shape[2], core.shape[2]
+    total_above = kept[:width, :, :rim] + got[:, :, :rim]
+    total_below = kept[:width, :, rim + rows :] + got[:, :, rim + rows :]
+    for other in rest[:-3]:
+        total_above = total_above + other[:, :, :rim]
+        total_below = total_below + other[:, :, rim:]
+    above[...] = total_above
+    below[...] = total_below
+    core[...] = kept[:width, :, rim : rim + rows] + got[:, :, rim : rim + rows]
+
+
+def fold_kernel(core, from_below, from_above, out):
+    rim, rows = from_below.shape[2], core.shape[2]
+    out[...] = core[...]
+    out[:, :, :rim] += from_above[...]
+    out[:, :, rows - rim :] += from_below[...]
+
+
+def finish_kernel(core, *rest):
+    out = rest[-1]
+    for block in range(core.shape[0]):
+        total = core[block]
+        for other in rest[:-1]:
+            total = total + other[block]
+        out[:, :, block * LANES : (block + 1) * LANES] = total
+
+
+def share_rows(index, share):
+    return pl.ds(pl.multiple_of(index * share, share), share)
+
+
+def shares_kernel(place, kept, got, *outs):
+    share = outs[0].shape[0]
+    for step, out in enumerate(outs):
+        rows = share_rows(lax.rem(place[0] + step, len(outs)), share)
+        out[...] = kept[rows] + got[rows]
+
+
+def order_kernel(place, *refs):
+    out = refs[-1]
+    share = refs[0].shape[0]
+    tiles = len(refs) - 1
+    for step, part in enumerate(refs[:-1]):
+        out[share_rows(lax.rem(place[0] + tiles - step, tiles), share)] = part[...]
+
+
+def both_kernel(place, mine, other, out):
+    out[place[2]] = mine[...]
+    out[1 - place[2]] = other[...]
 
 
 def on_device(object_field, probe, intensity, centres, counts):
     side = probe.shape[1]
     rim = side // 2
-    strip_rows = object_field.shape[1]
+    strip_rows, cols = object_field.shape[1:]
     strip = lax.axis_index("tiles")
     sub = lax.axis_index("sub")
     mode = lax.axis_index("modes")
-    subs = lax.axis_size("sub")
+    tiles, subs = lax.axis_size("tiles"), lax.axis_size("sub")
     owners = subs * lax.axis_size("modes")
+    width = cols // owners // LANES
     place = jnp.stack([strip, sub, mode]).astype(jnp.int32)
 
     own_plane = lax.dynamic_index_in_dim(object_field, mode, 0, keepdims=False)
@@ -288,30 +356,88 @@
     dn_a = shift_down(own_plane[:rim], "tiles")
     halos = (up_a, dn_a, swap(up_a), swap(dn_a))
 
-    sums = point_sums(
+    keep_obj, give_mine, give_others, keep_probe, give_probe = point_sums(
         place, counts, centres.reshape(-1), object_field, halos, probe, intensity[0], owners
     )
-    probe_grad = sums[owners]
-
-    mine = []
-    for step in range(subs):
-        mine.append(sums[2 * step] + swap(sums[2 * step + 1]))
-    total = mine[0]
-    for step in range(1, subs):
-        total = total + lax.ppermute(
-            mine[step], "sub", [(i, (i + step) % subs) for i in range(subs)]
+    got_probe = swap(give_probe)
+    got_others = swap(give_others)
+    got_mine = swap(give_mine)
+
+    rims_shape = shape(width, 2, 2 * rim, LANES)
+    core_shape = shape(width, 2, strip_rows, LANES)
+    outgoing = list(small_kernel(
+        others_kernel,
+        [rims_shape, core_shape] * (subs - 1),
+        keep_obj,
+        got_others,
+        name="object_others",
+    ))
+
+    def rotate_all(parts):
+        return [rotated(x, "sub", step + 1) for step, x in enumerate(parts)]
+
+    def rotate_strips(parts):
+        return [rotated(x, "tiles", step + 1) for step, x in enumerate(parts)]
+
+    direct = tiles <= 4
+    total_rows, total_cols = keep_probe.shape
+    share = shape(total_rows // tiles, total_cols)
+    if direct:
+        parts = small_kernel(
+            shares_kernel, [share] * tiles, place, keep_probe, got_probe, name="probe_shares"
         )
-    total = total.transpose(1, 2, 0, 3).reshape(2, strip_rows + side, -1)
-    core = total[:, rim : rim + strip_rows]
-    core = core.at[:, :rim].add(shift_up(total[:, rim + strip_rows :], "tiles"))
-    core = core.at[:, strip_rows - rim :].add(shift_down(total[:, :rim], "tiles"))
-
-    kept = lax.dynamic_index_in_dim(probe_grad, mode, 0, keepdims=False)
-    given = lax.dynamic_index_in_dim(probe_grad, 1 - mode, 0, keepdims=False)
-    kept = sum_over_strips(kept + swap(given))
-    other = swap(kept)
-    probe_out = jnp.where(mode == 0, jnp.stack([kept, other]), jnp.stack([other, kept]))
-    return (core, probe_out)
+        parts_in = rotate_strips(parts[1:])
+    rims_in = rotate_all(outgoing[0::2])
+    core_out = outgoing[1::2]
+    above, core, below = small_kernel(
+        mine_kernel,
+        [shape(width, 2, rim, LANES), core_shape, shape(width, 2, rim, LANES)],
+        keep_obj,
+        got_mine,
+        *rims_in,
+        name="object_mine",
+    )
+    if direct:
+        part_sum = small_kernel(add_kernel, share, parts[0], *parts_in, name="probe_strips_sum")
+        part_sum, above, below = lax.optimization_barrier((part_sum, above, below))
+        part_in = [rotated(part_sum, "sub", step) for step in range(1, subs)]
+    from_below = shift_down(above, "tiles")
+    from_above = shift_up(below, "tiles")
+    folded = small_kernel(
+        fold_kernel, core_shape, core, from_below, from_above, name="object_fold"
+    )
+    if direct:
+        part_sum = small_kernel(add_kernel, share, part_sum, *part_in, name="probe_total")
+        part_sum, folded, *core_out = lax.optimization_barrier((part_sum, folded, *core_out))
+        parts_in = rotate_strips([part_sum] * (tiles - 1))
+    core_in = rotate_all(core_out)
+    if direct:
+        probe_mine = small_kernel(
+            order_kernel,
+            shape(total_rows, total_cols),
+            place,
+            part_sum,
+            *parts_in,
+            name="probe_order",
+        )
+    else:
+        probe_mine = lax.psum(keep_probe + got_probe, ("tiles", "sub"))
+    object_grad = small_kernel(
+        finish_kernel,
+        shape(2, strip_rows, width * LANES),
+        folded,
+        *core_in,
+        name="object_finish",
+    )
+    probe_grad = small_kernel(
+        both_kernel,
+        shape(2, *probe_mine.shape),
+        place,
+        probe_mine,
+        swap(probe_mine),
+        name="probe_both",
+    )
+    return (object_grad, probe_grad)
 
 
 def solution(mesh):

time: 121 us -> 99.2 us (0.82)
  waiting for transfers between devices: 51.7 us -> 35 us
  other arithmetic: 4.9 us -> 0.61 us
  Pallas kernels: 23 us -> 26.3 us
  starting transfers between devices: 32.6 us -> 30 us
  local copies, waits for them, and re-layouts: 6.46 us -> 4.69 us
    ppermute x1 -> x0, waiting for transfers between devices: 14.2 us -> none  [on_device(): lax.ppermute(mine[step], 'sub', [(i, (i + step) % subs) for i in range(su...]
    ppermute x2, waiting for transfers between devices: 10.3 us -> 1.63 us  [shift_up(): return lax.ppermute(cells, axis, [(i, i + 1) for i in range(count - 1)])]
    ppermute x15 -> x9, starting transfers between devices: 20.3 us -> 15.1 us  [rotated(): lax.ppermute(cells, axis, [(i, (i + step) % count) for i in range(count)])]
    pallas_call x0 -> x9, Pallas kernels: none -> 4.01 us  [small_kernel(): pl.pallas_call(body, out_shape=out_shape, in_specs=[pl.BlockSpec(memory_s...]
    ppermute x2, starting transfers between devices: 7.4 us -> 11.2 us  [shift_up(): return lax.ppermute(cells, axis, [(i, i + 1) for i in range(count - 1)])]
    ppermute x15 -> x9, waiting for transfers between devices: 17.7 us -> 21.4 us  [rotated(): lax.ppermute(cells, axis, [(i, (i + step) % count) for i in range(count)])]
    select_n x1 -> x0, other arithmetic: 2.33 us -> none  [on_device(): jnp.where(mode == 0, jnp.stack([kept, other]), jnp.stack([other, kept]))]
    ppermute x2, waiting for transfers between devices: 8.19 us -> 9.95 us  [shift_down(): return lax.ppermute(cells, axis, [(i + 1, i) for i in range(count - 1)])]
  transfers between devices with their start and end apart: 26 -> 19, of which waited for: 13 -> 10; matrix products, arithmetic and copies ran while one was open for 6% -> 1% of each run, Pallas kernels for 0% -> 2%
where the time goes in v2:
time: 99.2 us; the launch traced here: 98.1 us
  waiting for transfers between devices  35 us (35%)
  starting transfers between devices  30 us (30%)
  Pallas kernels  26.3 us (27%)
  local copies, waits for them, and re-layouts  4.69 us (5%)
  between operations  1.48 us (1%)
    pallas_call x1, Pallas kernels, point_sums(): pl.pallas_call(functools.partial(point_kernel, owners=owners), out_shape=...  22.3 us
    ppermute x9, waiting for transfers between devices, rotated(): lax.ppermute(cells, axis, [(i, (i + step) % count) for i in range(count)])  21.4 us
    ppermute x9, starting transfers between devices, rotated(): lax.ppermute(cells, axis, [(i, (i + step) % count) for i in range(count)])  15.1 us
    ppermute x2, starting transfers between devices, shift_up(): return lax.ppermute(cells, axis, [(i, i + 1) for i in range(count - 1)])  11.2 us
    ppermute x2, waiting for transfers between devices, shift_down(): return lax.ppermute(cells, axis, [(i + 1, i) for i in range(count - 1)])  9.95 us
    pallas_call x9, Pallas kernels, small_kernel(): pl.pallas_call(body, out_shape=out_shape, in_specs=[pl.BlockSpec(memory_s...  4.01 us
    unnamed x19, local copies, waits for them, and re-layouts  2.7 us
    ppermute x2, starting transfers between devices, shift_down(): return lax.ppermute(cells, axis, [(i + 1, i) for i in range(count - 1)])  2.58 us
  transfers between devices with their start and end apart: 19, of which 10 were waited for; matrix products, arithmetic and copies ran while one was open for 1% of the time, Pallas kernels for 2%

profile of v2, /device:TPU:0, one launch (start us, length us, event | category | flops | bytes accessed | tf_op | source)
XLA Modules:
  0.0 98.1 jit_solution(9216363279019994779)
XLA Ops:
  0.6 1.3 %dynamic-slice_bitcast_fusion = (f32[128,1024]{1,0:T(8,128)S(1)}, f32[128,1024]{1,0:T(8,128)S(1)}) fusion(f32[2,256,1024]{2,1,0:T(8,128)} %own.1, s32[]{:T(128)S(6)} %select_n.4, s32[]{:T(128)S(6)} %add.7), kind=kLoop, calls=%fused_computation | loop fusion | bytes 2097160 | tf_op jit(solution)/shard_map/slice | solution.py:356
  2.0 1.3 %collective-permute-start.1 = (f32[128,1024]{1,0:T(8,128)S(1)}, f32[128,1024]{1,0:T(8,128)S(1)}, u32[]{:S(2)}, u32[]{:S(2)}) collective-permute-start(f32[128,1024]{1,0:T(8,128)S(1)} %get-tuple-element.42), channel_id=1, source_target_pairs={{4,0},{8,4},{12,8},{5,1},{9,5},{13,9},{6,2},{10,6},{14,10},{7,3},{... | collective-permute-start | bytes 1572872 | tf_op jit(solution)/shard_map/ppermute | solution.py:234
  3.3 5.6 %collective-permute-start = (f32[128,1024]{1,0:T(8,128)S(1)}, f32[128,1024]{1,0:T(8,128)S(1)}, u32[]{:S(2)}, u32[]{:S(2)}) collective-permute-start(f32[128,1024]{1,0:T(8,128)S(1)} %get-tuple-element.43), channel_id=1, source_target_pairs={{0,4},{4,8},{8,12},{1,5},{5,9},{9,13},{2,6},{6,10},{10,14},{3,7},{... | collective-permute-start | bytes 1572872 | tf_op jit(solution)/shard_map/ppermute | solution.py:229
  8.9 10.0 %collective-permute-done.1.dn_a = f32[128,1024]{1,0:T(8,128)S(1)} collective-permute-done((f32[128,1024]{1,0:T(8,128)S(1)}, f32[128,1024]{1,0:T(8,128)S(1)}, u32[]{:S(2)}, u32[]{:S(2)}) %collective-permute-start.1) | collective-permute-done | bytes 524320 | tf_op jit(solution)/shard_map/ppermute | solution.py:234
  18.8 1.2 %collective-permute-done.up_a = f32[128,1024]{1,0:T(8,128)S(1)} collective-permute-done((f32[128,1024]{1,0:T(8,128)S(1)}, f32[128,1024]{1,0:T(8,128)S(1)}, u32[]{:S(2)}, u32[]{:S(2)}) %collective-permute-start) | collective-permute-done | bytes 524320 | tf_op jit(solution)/shard_map/ppermute | solution.py:229
  23.1 22.3 %point_sums.1 = (f32[4,2,512,128]{3,2,1,0:T(8,128)}, f32[2,2,512,128]{3,2,1,0:T(8,128)}, f32[2,2,512,128]{3,2,1,0:T(8,128)}, f32[256,512]{1,0:T(8,128)}, f32[256,512]{1,0:T(8,128)}) custom-call(s32[3]{0:T(128)} %pad_add_fusion.place, s32[1]{0:T(128)S(6)} %copy.11.counts, s32[64]{0:T(128)} %reshape.9.spots, f32[2,256,1024]{2,1,0:T(8,128)} %own.1, ...), custom_call_target="tpu_custom_call" | custom-call | flops 8589934592 | bytes 16777216 | tf_op jit(solution)/shard_map/point_sums/pallas_call | solution.py:202
  46.5 2.0 %collective-permute-done.9.got = f32[2,2,512,128]{3,2,1,0:T(8,128)S(1)} collective-permute-done((f32[2,2,512,128]{3,2,1,0:T(8,128)}, f32[2,2,512,128]{3,2,1,0:T(8,128)S(1)}, u32[]{:S(2)}, u32[]{:S(2)}) %collective-permute-start.9) | collective-permute-done | bytes 1048608 | tf_op jit(solution)/shard_map/ppermute | solution.py:238
  48.5 1.6 %copy-done = f32[4,2,512,128]{3,2,1,0:T(8,128)S(1)} copy-done((f32[4,2,512,128]{3,2,1,0:T(8,128)S(1)}, f32[4,2,512,128]{3,2,1,0:T(8,128)}, u32[]{:S(2)}) %copy-start) | copy-done | bytes 2097176
  50.2 1.7 %collective-permute-start.10 = (f32[2,2,256,128]{3,2,1,0:T(8,128)S(1)}, f32[2,2,256,128]{3,2,1,0:T(8,128)S(1)}, u32[]{:S(2)}, u32[]{:S(2)}) collective-permute-start(f32[2,2,256,128]{3,2,1,0:T(8,128)S(1)} %get-tuple-element.31), channel_id=1, source_target_pairs={{0,2},{2,0},{1,3},{3,1},{4,6},{6,4},{5,7},{7,5},{8,10},{10,8},{9,1... | collective-permute-start | bytes 1572872 | tf_op jit(solution)/shard_map/ppermute | solution.py:243
  52.6 3.1 %collective-permute-start.6 = (f32[64,512]{1,0:T(8,128)S(1)}, f32[64,512]{1,0:T(8,128)S(1)}, u32[]{:S(2)}, u32[]{:S(2)}) collective-permute-start(f32[64,512]{1,0:T(8,128)S(1)} %get-tuple-element.26), channel_id=1, source_target_pairs={{0,8},{4,12},{8,0},{12,4},{1,9},{5,13},{9,1},{13,5},{2,10},{6,14},... | collective-permute-start | bytes 393224 | tf_op jit(solution)/shard_map/ppermute | solution.py:243
  55.7 2.8 %collective-permute-start.7 = (f32[64,512]{1,0:T(8,128)S(1)}, f32[64,512]{1,0:T(8,128)S(1)}, u32[]{:S(2)}, u32[]{:S(2)}) collective-permute-start(f32[64,512]{1,0:T(8,128)S(1)} %get-tuple-element.27), channel_id=1, source_target_pairs={{0,12},{4,0},{8,4},{12,8},{1,13},{5,1},{9,5},{13,9},{2,14},{6,2},{... | collective-permute-start | bytes 393224 | tf_op jit(solution)/shard_map/ppermute | solution.py:243
  58.5 2.2 %collective-permute-done.5.refs_1_ = f32[64,512]{1,0:T(8,128)S(1)} collective-permute-done((f32[64,512]{1,0:T(8,128)S(1)}, f32[64,512]{1,0:T(8,128)S(1)}, u32[]{:S(2)}, u32[]{:S(2)}) %collective-permute-start.5) | collective-permute-done | bytes 131104 | tf_op jit(solution)/shard_map/ppermute | solution.py:243
  60.7 4.9 %collective-permute-done.6.refs_2_ = f32[64,512]{1,0:T(8,128)S(1)} collective-permute-done((f32[64,512]{1,0:T(8,128)S(1)}, f32[64,512]{1,0:T(8,128)S(1)}, u32[]{:S(2)}, u32[]{:S(2)}) %collective-permute-start.6) | collective-permute-done | bytes 131104 | tf_op jit(solution)/shard_map/ppermute | solution.py:243
  65.8 1.3 %collective-permute-start.12 = (f32[2,2,128,128]{3,2,1,0:T(8,128)S(1)}, f32[2,2,128,128]{3,2,1,0:T(8,128)S(1)}, u32[]{:S(2)}, u32[]{:S(2)}) collective-permute-start(f32[2,2,128,128]{3,2,1,0:T(8,128)S(1)} %get-tuple-element.36), channel_id=1, source_target_pairs={{4,0},{8,4},{12,8},{5,1},{9,5},{13,9},{6,2},{10,6},{14,10},{7,3},{... | collective-permute-start | bytes 786440 | tf_op jit(solution)/shard_map/ppermute | solution.py:234
  67.1 5.6 %collective-permute-start.13 = (f32[2,2,128,128]{3,2,1,0:T(8,128)S(1)}, f32[2,2,128,128]{3,2,1,0:T(8,128)S(1)}, u32[]{:S(2)}, u32[]{:S(2)}) collective-permute-start(f32[2,2,128,128]{3,2,1,0:T(8,128)S(1)} %get-tuple-element.37), channel_id=1, source_target_pairs={{0,4},{4,8},{8,12},{1,5},{5,9},{9,13},{2,6},{6,10},{10,14},{3,7},{... | collective-permute-start | bytes 786440 | tf_op jit(solution)/shard_map/ppermute | solution.py:229
  72.7 1.0 collective-permute-start.11
  73.7 4.1 %collective-permute-done.11.refs_1_ = f32[64,512]{1,0:T(8,128)S(1)} collective-permute-done((f32[64,512]{1,0:T(8,128)S(1)}, f32[64,512]{1,0:T(8,128)S(1)}, u32[]{:S(2)}, u32[]{:S(2)}) %collective-permute-start.11) | collective-permute-done | bytes 131104 | tf_op jit(solution)/shard_map/ppermute | solution.py:243
  78.3 3.7 %collective-permute-start.17 = (f32[64,512]{1,0:T(8,128)S(1)}, f32[64,512]{1,0:T(8,128)S(1)}, u32[]{:S(2)}, u32[]{:S(2)}) collective-permute-start(f32[64,512]{1,0:T(8,128)S(1)} %probe_total.1.refs_0_), channel_id=1, source_target_pairs={{0,12},{4,0},{8,4},{12,8},{1,13},{5,1},{9,5},{13,9},{2,14},{6,2},{... | collective-permute-start | bytes 393224 | tf_op jit(solution)/shard_map/ppermute | solution.py:243
  82.3 1.7 %collective-permute-start.15 = (f32[64,512]{1,0:T(8,128)S(1)}, f32[64,512]{1,0:T(8,128)S(1)}, u32[]{:S(2)}, u32[]{:S(2)}) collective-permute-start(f32[64,512]{1,0:T(8,128)S(1)} %probe_total.1.refs_0_), channel_id=1, source_target_pairs={{0,4},{4,8},{8,12},{12,0},{1,5},{5,9},{9,13},{13,1},{2,6},{6,10},{... | collective-permute-start | bytes 393224 | tf_op jit(solution)/shard_map/ppermute | solution.py:243
  84.8 1.1 %collective-permute-done.17.refs_3_ = f32[64,512]{1,0:T(8,128)S(1)} collective-permute-done((f32[64,512]{1,0:T(8,128)S(1)}, f32[64,512]{1,0:T(8,128)S(1)}, u32[]{:S(2)}, u32[]{:S(2)}) %collective-permute-start.17) | collective-permute-done | bytes 131104 | tf_op jit(solution)/shard_map/ppermute | solution.py:243
  85.9 7.7 %collective-permute-done.16.refs_2_ = f32[64,512]{1,0:T(8,128)S(1)} collective-permute-done((f32[64,512]{1,0:T(8,128)S(1)}, f32[64,512]{1,0:T(8,128)S(1)}, u32[]{:S(2)}, u32[]{:S(2)}) %collective-permute-start.16) | collective-permute-done | bytes 131104 | tf_op jit(solution)/shard_map/ppermute | solution.py:243
  94.3 1.3 %collective-permute-done.14.rest_0_ = f32[2,2,256,128]{3,2,1,0:T(8,128)S(1)} collective-permute-done((f32[2,2,256,128]{3,2,1,0:T(8,128)S(1)}, f32[2,2,256,128]{3,2,1,0:T(8,128)S(1)}, u32[]{:S(2)}, u32[]{:S(2)}) %collective-permute-start.14) | collective-permute-done | bytes 524320 | tf_op jit(solution)/shard_map/ppermute | solution.py:243
  95.7 0.8 object_finish.1
  96.5 1.6 %probe_both.1 = f32[2,256,512]{2,1,0:T(8,128)} custom-call(s32[3]{0:T(128)S(1)} %copy-done.3, f32[256,512]{1,0:T(8,128)S(1)} %probe_order.1.mine, f32[256,512]{1,0:T(8,128)S(1)} %collective-permute-done.18.other), custom_call_target="tpu_custom_call" | custom-call | tf_op jit(solution)/shard_map/probe_both/pallas_call | solution.py:247
  (46 shorter events, 6.7 us)
Async XLA Ops:
  0.6 20.0 %copy-start.4 = (s32[1,32,2]{1,2,0:T(2,128)S(1)}, s32[1,32,2]{1,2,0:T(2,128)}, u32[]{:S(2)}) copy-start(s32[1,32,2]{1,2,0:T(2,128)} %param.10) | copy-start | bytes 772
  2.0 16.8 %collective-permute-start.1 = (f32[128,1024]{1,0:T(8,128)S(1)}, f32[128,1024]{1,0:T(8,128)S(1)}, u32[]{:S(2)}, u32[]{:S(2)}) collective-permute-start(f32[128,1024]{1,0:T(8,128)S(1)} %get-tuple-element.42), channel_id=1, source_target_pairs={{4,0},{8,4},{12,8},{5,1},{9,5},{13,9},{6,2},{10,6},{14,10},{7,3},{... | collective-permute-start | bytes 1572872 | tf_op jit(solution)/shard_map/ppermute | solution.py:234
  3.3 16.7 %collective-permute-start = (f32[128,1024]{1,0:T(8,128)S(1)}, f32[128,1024]{1,0:T(8,128)S(1)}, u32[]{:S(2)}, u32[]{:S(2)}) collective-permute-start(f32[128,1024]{1,0:T(8,128)S(1)} %get-tuple-element.43), channel_id=1, source_target_pairs={{0,4},{4,8},{8,12},{1,5},{5,9},{9,13},{2,6},{6,10},{10,14},{3,7},{... | collective-permute-start | bytes 1572872 | tf_op jit(solution)/shard_map/ppermute | solution.py:229
  18.8 3.3 %copy-start.5 = (f32[128,1024]{1,0:T(8,128)}, f32[128,1024]{1,0:T(8,128)S(1)}, u32[]{:S(2)}) copy-start(f32[128,1024]{1,0:T(8,128)S(1)} %collective-permute-done.1.dn_a) | copy-start | bytes 1572868
  18.8 3.2 %collective-permute-start.3 = (f32[128,1024]{1,0:T(8,128)S(1)}, f32[128,1024]{1,0:T(8,128)S(1)}, u32[]{:S(2)}, u32[]{:S(2)}) collective-permute-start(f32[128,1024]{1,0:T(8,128)S(1)} %collective-permute-done.1.dn_a), channel_id=1, source_target_pairs={{0,1},{1,0},{2,3},{3,2},{4,5},{5,4},{6,7},{7,6},{8,9},{9,8},{10,11... | collective-permute-start | bytes 1572872 | tf_op jit(solution)/shard_map/ppermute | solution.py:238
  20.0 2.1 %copy-start.6 = (f32[128,1024]{1,0:T(8,128)}, f32[128,1024]{1,0:T(8,128)S(1)}, u32[]{:S(2)}) copy-start(f32[128,1024]{1,0:T(8,128)S(1)} %collective-permute-done.up_a) | copy-start | bytes 1572868
  20.0 2.1 %collective-permute-start.2 = (f32[128,1024]{1,0:T(8,128)S(1)}, f32[128,1024]{1,0:T(8,128)S(1)}, u32[]{:S(2)}, u32[]{:S(2)}) collective-permute-start(f32[128,1024]{1,0:T(8,128)S(1)} %collective-permute-done.up_a), channel_id=1, source_target_pairs={{0,1},{1,0},{2,3},{3,2},{4,5},{5,4},{6,7},{7,6},{8,9},{9,8},{10,11... | collective-permute-start | bytes 1572872 | tf_op jit(solution)/shard_map/ppermute | solution.py:238
  45.4 6.5 %copy-start.3 = (s32[3]{0:T(128)S(1)}, s32[3]{0:T(128)}, u32[]{:S(2)}) copy-start(s32[3]{0:T(128)} %pad_add_fusion.place) | copy-start | bytes 40
  45.4 3.0 %collective-permute-start.9 = (f32[2,2,512,128]{3,2,1,0:T(8,128)}, f32[2,2,512,128]{3,2,1,0:T(8,128)S(1)}, u32[]{:S(2)}, u32[]{:S(2)}) collective-permute-start(f32[2,2,512,128]{3,2,1,0:T(8,128)} %get-tuple-element.30), channel_id=1, source_target_pairs={{0,1},{1,0},{2,3},{3,2},{4,5},{5,4},{6,7},{7,6},{8,9},{9,8},{10,11... | collective-permute-start | bytes 3145736 | tf_op jit(solution)/shard_map/ppermute | solution.py:238
  46.0 19.6 %collective-permute-start.8 = (f32[2,2,512,128]{3,2,1,0:T(8,128)}, f32[2,2,512,128]{3,2,1,0:T(8,128)S(1)}, u32[]{:S(2)}, u32[]{:S(2)}) collective-permute-start(f32[2,2,512,128]{3,2,1,0:T(8,128)} %get-tuple-element.29), channel_id=1, source_target_pairs={{0,1},{1,0},{2,3},{3,2},{4,5},{5,4},{6,7},{7,6},{8,9},{9,8},{10,11... | collective-permute-start | bytes 3145736 | tf_op jit(solution)/shard_map/ppermute | solution.py:238
  46.0 5.8 %collective-permute-start.4 = (f32[256,512]{1,0:T(8,128)}, f32[256,512]{1,0:T(8,128)S(1)}, u32[]{:S(2)}, u32[]{:S(2)}) collective-permute-start(f32[256,512]{1,0:T(8,128)} %get-tuple-element.23), channel_id=1, source_target_pairs={{0,1},{1,0},{2,3},{3,2},{4,5},{5,4},{6,7},{7,6},{8,9},{9,8},{10,11... | collective-permute-start | bytes 1572872 | tf_op jit(solution)/shard_map/ppermute | solution.py:238
  50.1 15.6 %copy-start.1 = (f32[4,2,512,128]{3,2,1,0:T(8,128)S(1)}, f32[4,2,512,128]{3,2,1,0:T(8,128)}, u32[]{:S(2)}) copy-start(f32[4,2,512,128]{3,2,1,0:T(8,128)} %get-tuple-element.28.kept) | copy-start | bytes 6291460
  50.2 15.5 %collective-permute-start.10 = (f32[2,2,256,128]{3,2,1,0:T(8,128)S(1)}, f32[2,2,256,128]{3,2,1,0:T(8,128)S(1)}, u32[]{:S(2)}, u32[]{:S(2)}) collective-permute-start(f32[2,2,256,128]{3,2,1,0:T(8,128)S(1)} %get-tuple-element.31), channel_id=1, source_target_pairs={{0,2},{2,0},{1,3},{3,1},{4,6},{6,4},{5,7},{7,5},{8,10},{10,8},{9,1... | collective-permute-start | bytes 1572872 | tf_op jit(solution)/shard_map/ppermute | solution.py:243
  52.5 8.2 %collective-permute-start.5 = (f32[64,512]{1,0:T(8,128)S(1)}, f32[64,512]{1,0:T(8,128)S(1)}, u32[]{:S(2)}, u32[]{:S(2)}) collective-permute-start(f32[64,512]{1,0:T(8,128)S(1)} %get-tuple-element.25), channel_id=1, source_target_pairs={{0,4},{4,8},{8,12},{12,0},{1,5},{5,9},{9,13},{13,1},{2,6},{6,10},{... | collective-permute-start | bytes 393224 | tf_op jit(solution)/shard_map/ppermute | solution.py:243
  52.6 13.0 %collective-permute-start.6 = (f32[64,512]{1,0:T(8,128)S(1)}, f32[64,512]{1,0:T(8,128)S(1)}, u32[]{:S(2)}, u32[]{:S(2)}) collective-permute-start(f32[64,512]{1,0:T(8,128)S(1)} %get-tuple-element.26), channel_id=1, source_target_pairs={{0,8},{4,12},{8,0},{12,4},{1,9},{5,13},{9,1},{13,5},{2,10},{6,14},... | collective-permute-start | bytes 393224 | tf_op jit(solution)/shard_map/ppermute | solution.py:243
  55.7 9.9 %collective-permute-start.7 = (f32[64,512]{1,0:T(8,128)S(1)}, f32[64,512]{1,0:T(8,128)S(1)}, u32[]{:S(2)}, u32[]{:S(2)}) collective-permute-start(f32[64,512]{1,0:T(8,128)S(1)} %get-tuple-element.27), channel_id=1, source_target_pairs={{0,12},{4,0},{8,4},{12,8},{1,13},{5,1},{9,5},{13,9},{2,14},{6,2},{... | collective-permute-start | bytes 393224 | tf_op jit(solution)/shard_map/ppermute | solution.py:243
  65.8 12.0 %collective-permute-start.12 = (f32[2,2,128,128]{3,2,1,0:T(8,128)S(1)}, f32[2,2,128,128]{3,2,1,0:T(8,128)S(1)}, u32[]{:S(2)}, u32[]{:S(2)}) collective-permute-start(f32[2,2,128,128]{3,2,1,0:T(8,128)S(1)} %get-tuple-element.36), channel_id=1, source_target_pairs={{4,0},{8,4},{12,8},{5,1},{9,5},{13,9},{6,2},{10,6},{14,10},{7,3},{... | collective-permute-start | bytes 786440 | tf_op jit(solution)/shard_map/ppermute | solution.py:234
  67.1 11.2 %collective-permute-start.13 = (f32[2,2,128,128]{3,2,1,0:T(8,128)S(1)}, f32[2,2,128,128]{3,2,1,0:T(8,128)S(1)}, u32[]{:S(2)}, u32[]{:S(2)}) collective-permute-start(f32[2,2,128,128]{3,2,1,0:T(8,128)S(1)} %get-tuple-element.37), channel_id=1, source_target_pairs={{0,4},{4,8},{8,12},{1,5},{5,9},{9,13},{2,6},{6,10},{10,14},{3,7},{... | collective-permute-start | bytes 786440 | tf_op jit(solution)/shard_map/ppermute | solution.py:229
  72.7 5.0 %collective-permute-start.11 = (f32[64,512]{1,0:T(8,128)S(1)}, f32[64,512]{1,0:T(8,128)S(1)}, u32[]{:S(2)}, u32[]{:S(2)}) collective-permute-start(f32[64,512]{1,0:T(8,128)S(1)} %probe_strips_sum.1.refs_0_), channel_id=1, source_target_pairs={{0,2},{2,0},{1,3},{3,1},{4,6},{6,4},{5,7},{7,5},{8,10},{10,8},{9,1... | collective-permute-start | bytes 393224 | tf_op jit(solution)/shard_map/ppermute | solution.py:243
  78.3 7.6 %collective-permute-start.17 = (f32[64,512]{1,0:T(8,128)S(1)}, f32[64,512]{1,0:T(8,128)S(1)}, u32[]{:S(2)}, u32[]{:S(2)}) collective-permute-start(f32[64,512]{1,0:T(8,128)S(1)} %probe_total.1.refs_0_), channel_id=1, source_target_pairs={{0,12},{4,0},{8,4},{12,8},{1,13},{5,1},{9,5},{13,9},{2,14},{6,2},{... | collective-permute-start | bytes 393224 | tf_op jit(solution)/shard_map/ppermute | solution.py:243
  82.0 11.7 %collective-permute-start.16 = (f32[64,512]{1,0:T(8,128)S(1)}, f32[64,512]{1,0:T(8,128)S(1)}, u32[]{:S(2)}, u32[]{:S(2)}) collective-permute-start(f32[64,512]{1,0:T(8,128)S(1)} %probe_total.1.refs_0_), channel_id=1, source_target_pairs={{0,8},{4,12},{8,0},{12,4},{1,9},{5,13},{9,1},{13,5},{2,10},{6,14},... | collective-permute-start | bytes 393224 | tf_op jit(solution)/shard_map/ppermute | solution.py:243
  82.3 11.3 %collective-permute-start.15 = (f32[64,512]{1,0:T(8,128)S(1)}, f32[64,512]{1,0:T(8,128)S(1)}, u32[]{:S(2)}, u32[]{:S(2)}) collective-permute-start(f32[64,512]{1,0:T(8,128)S(1)} %probe_total.1.refs_0_), channel_id=1, source_target_pairs={{0,4},{4,8},{8,12},{12,0},{1,5},{5,9},{9,13},{13,1},{2,6},{6,10},{... | collective-permute-start | bytes 393224 | tf_op jit(solution)/shard_map/ppermute | solution.py:243
  84.1 11.6 %collective-permute-start.14 = (f32[2,2,256,128]{3,2,1,0:T(8,128)S(1)}, f32[2,2,256,128]{3,2,1,0:T(8,128)S(1)}, u32[]{:S(2)}, u32[]{:S(2)}) collective-permute-start(f32[2,2,256,128]{3,2,1,0:T(8,128)S(1)} %get-tuple-element.40), channel_id=1, source_target_pairs={{0,2},{2,0},{1,3},{3,1},{4,6},{6,4},{5,7},{7,5},{8,10},{10,8},{9,1... | collective-permute-start | bytes 1572872 | tf_op jit(solution)/shard_map/ppermute | solution.py:243
  94.3 2.3 %collective-permute-start.18 = (f32[256,512]{1,0:T(8,128)S(1)}, f32[256,512]{1,0:T(8,128)S(1)}, u32[]{:S(2)}, u32[]{:S(2)}) collective-permute-start(f32[256,512]{1,0:T(8,128)S(1)} %probe_order.1.mine), channel_id=1, source_target_pairs={{0,1},{1,0},{2,3},{3,2},{4,5},{5,4},{6,7},{7,6},{8,9},{9,8},{10,11... | collective-permute-start | bytes 1572872 | tf_op jit(solution)/shard_map/ppermute | solution.py:238
  (4 other events, 5.3 us)

commit v3 on v2

v3 whole, which is shorter than its diff:
```python
import functools
import math

import jax
import jax.numpy as jnp
import ml_dtypes
import numpy as np
from jax import lax
from jax.experimental import pallas as pl
from jax.experimental.pallas import tpu as pltpu
from jax.sharding import PartitionSpec as P

LANES = 128
CHUNK = 64


def dft_tables(size):
    index = np.arange(size)
    angle = (index[:, None] * index[None, :] % size) * (2.0 * math.pi / size)
    scale = 1.0 / math.sqrt(size)
    cos_part = (np.cos(angle) * scale).astype(np.float32).astype(ml_dtypes.bfloat16)
    sin_part = (-np.sin(angle) * scale).astype(np.float32).astype(ml_dtypes.bfloat16)
    plain = np.block([[cos_part, -sin_part], [sin_part, cos_part]])
    turned = np.block([[cos_part, sin_part], [-sin_part, cos_part]])
    return plain, turned


def interleave(first, second):
    done = 0
    for index, step in enumerate(first):
        step()
        upto = (index + 1) * len(second) // len(first)
        for other in second[done:upto]:
            other()
        done = upto


def point_kernel(
    place,
    counts,
    spots,
    own,
    first_a,
    second_a,
    first_b,
    second_b,
    probe_f32,
    inten,
    plain,
    turned,
    *rest,
    owners,
):
    keep_mine, give_mine, keep_others, give_others, keep_probe, give_probe = rest[:6]
    field, grad, probe_grad = rest[6:9]
    patches, waves, halves, fars = (rest[9 + 2 * i : 11 + 2 * i] for i in range(4))
    sems, out_sems = rest[17:]
    strip, sub, mode = place[0], place[1], place[2]
    member = sub * 2 + mode
    side = probe_f32.shape[1]
    rim = side // 2
    strip_rows = own.shape[1]
    blocks = own.shape[2] // LANES
    slots = inten.shape[0]
    total = jnp.clip(counts[0] - member * slots, 0, slots)
    far_rows = rim + strip_rows
    near = (strip % 2) * far_rows
    copies = []

    def fetch(src, dst):
        copies.append(pltpu.make_async_copy(src, dst, sems.at[len(copies)]))

    for block in range(blocks):
        cols = pl.ds(block * LANES, LANES)
        for plane in range(2):
            fetch(own.at[plane, :, cols], field.at[plane, block, pl.ds(rim, strip_rows)])
        for first, second, plane in ((first_a, second_a, mode), (first_b, second_b, 1 - mode)):
            fetch(first.at[:, cols], field.at[plane, block, pl.ds(far_rows - near, rim)])
            fetch(second.at[:, cols], field.at[plane, block, pl.ds(near, rim)])
    for copy in copies:
        copy.start()

    probe_grad[...] = jnp.zeros_like(probe_grad)
    patches[1][...] = jnp.zeros_like(patches[1])
    fars[1][...] = jnp.zeros_like(fars[1])

    @pl.loop(0, grad.shape[0])
    def clear(block):
        grad[block] = jnp.zeros(grad.shape[1:], jnp.float32)

    for copy in copies:
        copy.wait()

    lane = lax.broadcasted_iota(jnp.int32, (CHUNK, LANES), 1)
    chunks = range(0, side, CHUNK)

    def spot(slot):
        base = 2 * (member * slots + jnp.clip(slot, 0, slots - 1))
        row = spots[base] - strip * strip_rows
        col = spots[base + 1] - rim
        return row, col // LANES, col % LANES

    def cut(k, slot):
        row, block, off = spot(slot)
        back_shift = (LANES - off) % LANES
        patch, wave = patches[k], waves[k]

        def step(chunk):
            rows = slice(chunk, chunk + CHUNK)
            low = slice(side + chunk, side + chunk + CHUNK)
            source = pl.ds(row + chunk, CHUNK)
            obj = []
            for plane in range(2):
                rolled = [
                    pltpu.roll(field[plane, block + j, source, :], back_shift, 1)
                    for j in range(3)
                ]
                obj.append(
                    [jnp.where(lane < LANES - off, rolled[j], rolled[j + 1]) for j in range(2)]
                )
            for j in range(2):
                cols = slice(j * LANES, (j + 1) * LANES)
                obj_re, obj_im = obj[0][j], obj[1][j]
                patch[0, rows, cols] = obj_re
                patch[1, rows, cols] = obj_im
                for m in range(2):
                    probe_re = probe_f32[m, rows, cols]
                    probe_im = probe_f32[m, rows, side + j * LANES : side + (j + 1) * LANES]
                    out = slice(m * side + j * LANES, m * side + (j + 1) * LANES)
                    wave[rows, out] = (probe_re * obj_re - probe_im * obj_im).astype(jnp.bfloat16)
                    wave[low, out] = (probe_re * obj_im + probe_im * obj_re).astype(jnp.bfloat16)

        return [functools.partial(step, chunk) for chunk in chunks]

    def left(k, table):
        wave, half = waves[k], halves[k]

        def step(m):
            cols = slice(m * side, (m + 1) * side)
            stacked = jnp.dot(table[...], wave[:, cols], preferred_element_type=jnp.float32)
            half[cols, :side] = stacked[:side].astype(jnp.bfloat16)
            half[cols, side:] = stacked[side:].astype(jnp.bfloat16)

        return [functools.partial(step, m) for m in range(2)]

    def right(k, table):
        half, far = halves[k], fars[k]

        def step(m):
            rows = slice(m * side, (m + 1) * side)
            far[rows] = jnp.dot(half[rows], table[...], preferred_element_type=jnp.float32)

        return [functools.partial(step, m) for m in range(2)]

    def compare(k, slot):
        far, wave = fars[k], waves[k]
        valid = jnp.where(slot < total, 1.0, 0.0)

        def step(chunk):
            parts = []
            power = 1.0
            for m in range(2):
                rows = slice(m * side + chunk, m * side + chunk + CHUNK)
                far_re, far_im = far[rows, :side], far[rows, side:]
                power = power + (far_re * far_re + far_im * far_im)
                parts.append((far_re, far_im))
            level = inten[jnp.clip(slot, 0, slots - 1), chunk : chunk + CHUNK]
            level = level.astype(jnp.float32) + 1.0
            ratio = valid - (valid * level) * lax.rsqrt(level * power)
            for m in range(2):
                cols = slice(m * side, (m + 1) * side)
                wave[chunk : chunk + CHUNK, cols] = (parts[m][0] * ratio).astype(jnp.bfloat16)
                wave[side + chunk : side + chunk + CHUNK, cols] = (parts[m][1] * ratio).astype(
                    jnp.bfloat16
                )

        return [functools.partial(step, chunk) for chunk in chunks]

    def gather(k, slot):
        row, block, off = spot(slot)
        far, patch = fars[k], patches[k]

        def step(chunk):
            rows = slice(chunk, chunk + CHUNK)
            obj_re, obj_im = patch[0, rows], patch[1, rows]
            terms = [0.0, 0.0]
            for m in range(2):
                probe_re = probe_f32[m, rows, :side]
                probe_im = probe_f32[m, rows, side:]
                far_rows = slice(m * side + chunk, m * side + chunk + CHUNK)
                back_re, back_im = far[far_rows, :side], far[far_rows, side:]
                terms[0] = terms[0] + (probe_re * back_re + probe_im * back_im)
                terms[1] = terms[1] + (probe_re * back_im - probe_im * back_re)
                probe_grad[m, rows, :side] += obj_re * back_re + obj_im * back_im
                probe_grad[m, rows, side:] += obj_re * back_im - obj_im * back_re
            target = pl.ds(row + chunk, CHUNK)
            for plane in range(2):
                first = pltpu.roll(terms[plane][:, :LANES], off, 1)
                second = pltpu.roll(terms[plane][:, LANES:], off, 1)
                grad[block, plane, target, :] += jnp.where(lane < off, 0.0, first)
                grad[block + 1, plane, target, :] += jnp.where(lane < off, first, second)
                grad[block + 2, plane, target, :] += jnp.where(lane < off, second, 0.0)

        return [functools.partial(step, chunk) for chunk in chunks]

    for step in cut(0, 0):
        step()

    @pl.loop(0, (total + 1) // 2)
    def pair(index):
        slot = 2 * index
        interleave(left(0, plain) + right(0, turned), gather(1, slot - 1) + cut(1, slot + 1))
        interleave(left(1, plain) + right(1, turned), compare(0, slot))
        interleave(left(0, turned) + right(0, plain), compare(1, slot + 1))
        interleave(left(1, turned) + right(1, plain), gather(0, slot) + cut(0, slot + 2))

    for step in gather(1, 2 * ((total + 1) // 2) - 1):
        step()

    width = blocks // owners
    sends = []

    def send(src, dst):
        sends.append(pltpu.make_async_copy(src, dst, out_sems.at[len(sends)]))

    send(probe_grad.at[1 - mode], give_probe)
    send(probe_grad.at[mode], keep_probe)
    for step in list(range(1, owners // 2)) + [0]:
        owner = 2 * lax.rem(sub + step, owners // 2)
        for part, target in (
            (owner + 1 - mode, give_others if step else give_mine),
            (owner + mode, keep_others if step else keep_mine),
        ):
            if step:
                target = target.at[pl.ds((step - 1) * width, width)]
            send(grad.at[pl.ds(part * width, width)], target)
    for copy in sends:
        copy.start()
    for copy in sends:
        copy.wait()


def prepare_kernel(probe, inten, plain, turned, *outs):
    probe_f32 = outs[0]
    probe_f32[...] = probe[...].astype(jnp.float32)
    for source, target in zip((inten, plain, turned), outs[1:]):
        target[...] = source[...]


def prepare(probe, inten):
    tables = [jnp.asarray(x) for x in dft_tables(probe.shape[1])]
    return small_kernel(
        prepare_kernel,
        [shape(*probe.shape)]
        + [jax.ShapeDtypeStruct(x.shape, x.dtype) for x in (inten, *tables)],
        probe,
        inten,
        *tables,
        name="prepare",
    )


def point_sums(place, counts, spots, own, halos, prepared, owners):
    probe, inten, plain, turned = prepared
    side = probe.shape[1]
    blocks = own.shape[2] // LANES
    rows = own.shape[1] + side
    width = blocks // owners

    def piece(count):
        return jax.ShapeDtypeStruct((count, 2, rows, LANES), jnp.float32)

    mode_sum = jax.ShapeDtypeStruct((side, 2 * side), jnp.float32)
    smem = pl.BlockSpec(memory_space=pltpu.SMEM)
    vmem = pl.BlockSpec(memory_space=pltpu.VMEM)
    anywhere = pl.BlockSpec(memory_space=pl.ANY)
    slots = inten.shape[0]
    return pl.pallas_call(
        functools.partial(point_kernel, owners=owners),
        out_shape=[piece(width)] * 2 + [piece(blocks // 2 - width)] * 2 + [mode_sum] * 2,
        in_specs=[smem] * 3 + [anywhere] * 5 + [vmem] * 4,
        out_specs=[anywhere] * 6,
        scratch_shapes=[
            pltpu.VMEM((2, blocks + 1, rows, LANES), jnp.float32),
            pltpu.VMEM((blocks + 1, 2, rows, LANES), jnp.float32),
            pltpu.VMEM((2, side, 2 * side), jnp.float32),
            *[pltpu.VMEM((2, side, side), jnp.float32)] * 2,
            *[pltpu.VMEM((2 * side, 2 * side), jnp.bfloat16)] * 4,
            *[pltpu.VMEM((2 * side, 2 * side), jnp.float32)] * 2,
            pltpu.SemaphoreType.DMA((6 * blocks,)),
            pltpu.SemaphoreType.DMA((owners + 2,)),
        ],
        compiler_params=pltpu.CompilerParams(vmem_limit_bytes=24 * 1024 * 1024),
        cost_estimate=pl.CostEstimate(
            flops=slots * 32 * 2 * side**3, bytes_accessed=16 * 1024 * 1024, transcendentals=0
        ),
        name="point_sums",
    )(place, counts, spots, own, *halos, *prepared)


def with_neighbours(first, second):
    count = lax.axis_size("tiles")
    pairs = [(i, i + 1) for i in range(count - 1)]
    return [
        lax.ppermute(cells, "tiles", [x for a, b in pairs[turn::2] for x in ((a, b), (b, a))])
        for turn, cells in enumerate((first, second))
    ]


def swap(cells):
    return lax.ppermute(cells, "modes", [(0, 1), (1, 0)])


def rotated(cells, axis, step):
    count = lax.axis_size(axis)
    return lax.ppermute(cells, axis, [(i, (i + step) % count) for i in range(count)])


def small_kernel(body, out_shape, *args, name):
    return pl.pallas_call(
        body,
        out_shape=out_shape,
        in_specs=[
            pl.BlockSpec(memory_space=pltpu.SMEM if x.dtype == jnp.int32 else pltpu.VMEM)
            for x in args
        ],
        out_specs=jax.tree.map(lambda _: pl.BlockSpec(memory_space=pltpu.VMEM), out_shape),
        compiler_params=pltpu.CompilerParams(vmem_limit_bytes=24 * 1024 * 1024),
        cost_estimate=pl.CostEstimate(flops=0, bytes_accessed=0, transcendentals=0),
        name=name,
    )(*args)


def shape(*dims):
    return jax.ShapeDtypeStruct(dims, jnp.float32)


def after(cells, *earlier):
    return lax.optimization_barrier((cells, *earlier))[0]


def add_kernel(*refs):
    total = refs[0][...]
    for ref in refs[1:-1]:
        total = total + ref[...]
    refs[-1][...] = total


def others_kernel(kept, got, *outs):
    width, _, rows = outs[1].shape[:3]
    rim = outs[0].shape[2] // 2
    for step in range(len(outs) // 2):
        rims, core = outs[2 * step : 2 * step + 2]
        cut = slice(step * width, (step + 1) * width)
        rims[:, :, :rim] = kept[cut, :, :rim] + got[cut, :, :rim]
        rims[:, :, rim:] = kept[cut, :, rim + rows :] + got[cut, :, rim + rows :]
        core[...] = kept[cut, :, rim : rim + rows] + got[cut, :, rim : rim + rows]


def mine_kernel(place, kept, got, *rest):
    first, core, second = rest[-3:]
    rim, rows = first.shape[2], core.shape[2]
    total_above = kept[:, :, :rim] + got[:, :, :rim]
    total_below = kept[:, :, rim + rows :] + got[:, :, rim + rows :]
    for other in rest[:-3]:
        total_above = total_above + other[:, :, :rim]
        total_below = total_below + other[:, :, rim:]
    even = place[0] % 2 == 0

    @pl.when(even)
    def below_first():
        first[...] = total_below
        second[...] = total_above

    @pl.when(~even)
    def above_first():
        first[...] = total_above
        second[...] = total_below

    core[...] = kept[:, :, rim : rim + rows] + got[:, :, rim : rim + rows]


def fold_kernel(place, core, first, second, out):
    rim, rows = first.shape[2], core.shape[2]
    out[...] = core[...]
    near = pl.multiple_of((place[0] % 2) * (rows - rim), 8)
    far = pl.multiple_of(rows - rim - near, 8)
    out[:, :, pl.ds(far, rim)] += first[...]
    out[:, :, pl.ds(near, rim)] += second[...]


def finish_kernel(core, *rest):
    out = rest[-1]
    for block in range(core.shape[0]):
        total = core[block]
        for other in rest[:-1]:
            total = total + other[block]
        out[:, :, block * LANES : (block + 1) * LANES] = total


def share_rows(index, share):
    return pl.ds(pl.multiple_of(index * share, share), share)


def shares_kernel(place, kept, got, *outs):
    share = outs[0].shape[0]
    for step, out in enumerate(outs):
        rows = share_rows(place[0] ^ step, share)
        out[...] = kept[rows] + got[rows]


def order_kernel(place, *refs):
    out = refs[-1]
    share = refs[0].shape[0]
    for step, part in enumerate(refs[:-1]):
        out[share_rows(place[0] ^ step, share)] = part[...]


def both_kernel(place, mine, other, out):
    out[place[2]] = mine[...]
    out[1 - place[2]] = other[...]


def on_device(object_field, probe, intensity, centres, counts):
    side = probe.shape[1]
    rim = side // 2
    strip_rows, cols = object_field.shape[1:]
    strip = lax.axis_index("tiles")
    sub = lax.axis_index("sub")
    mode = lax.axis_index("modes")
    tiles, subs = lax.axis_size("tiles"), lax.axis_size("sub")
    owners = subs * lax.axis_size("modes")
    width = cols // owners // LANES
    place = jnp.stack([strip, sub, mode]).astype(jnp.int32)

    last = strip_rows - rim
    even = strip % 2 == 0
    ends = [
        lax.dynamic_slice(object_field, (mode, jnp.where(at_end, last, 0), 0), (1, rim, cols))[0]
        for at_end in (even, ~even)
    ]
    first, second = with_neighbours(*ends)
    halos = (first, second, swap(first), swap(second))

    keep_mine, give_mine, keep_others, give_others, keep_probe, give_probe = point_sums(
        place, counts, centres.reshape(-1), object_field, halos, prepare(probe, intensity[0]), owners
    )
    got_probe = swap(give_probe)
    got_others = swap(give_others)
    got_mine = swap(give_mine)

    rims_shape = shape(width, 2, 2 * rim, LANES)
    core_shape = shape(width, 2, strip_rows, LANES)
    outgoing = list(small_kernel(
        others_kernel,
        [rims_shape, core_shape] * (subs - 1),
        keep_others,
        got_others,
        name="object_others",
    ))

    def rotate_all(parts):
        return [rotated(x, "sub", step + 1) for step, x in enumerate(parts)]

    def rotate_strips(parts):
        return [
            lax.ppermute(x, "tiles", [(i, i ^ (step + 1)) for i in range(tiles)])
            for step, x in enumerate(parts)
        ]

    direct = tiles in (1, 2, 4)
    total_rows, total_cols = keep_probe.shape
    share = shape(total_rows // tiles, total_cols)
    if direct:
        parts = small_kernel(
            shares_kernel, [share] * tiles, place, keep_probe, got_probe, name="probe_shares"
        )
        parts_in = rotate_strips(parts[1:])
    rims_in = rotate_all(outgoing[0::2])
    core_out = outgoing[1::2]
    first, core, second = small_kernel(
        mine_kernel,
        [shape(width, 2, rim, LANES), core_shape, shape(width, 2, rim, LANES)],
        place,
        keep_mine,
        got_mine,
        *rims_in,
        name="object_mine",
    )
    if direct:
        part_sum = small_kernel(add_kernel, share, parts[0], *parts_in, name="probe_strips_sum")
        part_sum, first, second = lax.optimization_barrier((part_sum, first, second))
        part_in = [rotated(part_sum, "sub", step) for step in range(1, subs)]
    first, second = with_neighbours(first, second)
    folded = small_kernel(
        fold_kernel, core_shape, place, core, first, second, name="object_fold"
    )
    if direct:
        part_sum = small_kernel(add_kernel, share, part_sum, *part_in, name="probe_total")
        part_sum, folded, *core_out = lax.optimization_barrier((part_sum, folded, *core_out))
        parts_in = rotate_strips([part_sum] * (tiles - 1))
    core_in = rotate_all(core_out)
    if direct:
        probe_mine = small_kernel(
            order_kernel,
            shape(total_rows, total_cols),
            place,
            part_sum,
            *parts_in,
            name="probe_order",
        )
    else:
        probe_mine = lax.psum(keep_probe + got_probe, ("tiles", "sub"))
    object_grad = small_kernel(
        finish_kernel,
        shape(2, strip_rows, width * LANES),
        folded,
        *core_in,
        name="object_finish",
    )
    probe_grad = small_kernel(
        both_kernel,
        shape(2, *probe_mine.shape),
        place,
        probe_mine,
        swap(probe_mine),
        name="probe_both",
    )
    return (object_grad, probe_grad)


def solution(mesh):
    return jax.shard_map(
        on_device,
        mesh=mesh,
        in_specs=(
            P(None, ("groups", "tiles"), None),
            P("groups", None, None),
            P(("groups", "tiles"), ("sub", "modes"), None, None),
            P(("groups", "tiles"), None, None),
            P(("groups", "tiles")),
        ),
        out_specs=(P(None, ("groups", "tiles"), ("sub", "modes")), P("groups", None, None)),
        check_vma=False,
    )
```

time: 99.2 us -> 89.6 us (0.903)
  Pallas kernels: 26.3 us -> 11.8 us
  waiting for transfers between devices: 35 us -> 40.3 us
  starting transfers between devices: 30 us -> 31.3 us
    ppermute x4 -> x10, waiting for transfers between devices: 11.6 us -> 30.5 us  [the longest x6 18.8 us: rotate_strips(): lax.ppermute(x, 'tiles', [(i, i ^ step + 1) for i in range(tiles)])]
    pallas_call x1, Pallas kernels: 22.3 us -> 6.52 us  [point_sums(): pl.pallas_call(functools.partial(point_kernel, owners=owners), out_shape=...]
    ppermute x9 -> x3, waiting for transfers between devices: 21.4 us -> 5.61 us  [rotated(): lax.ppermute(cells, axis, [(i, (i + step) % count) for i in range(count)])]
    ppermute x4 -> x10, starting transfers between devices: 13.8 us -> 28.5 us  [the longest x6 18.6 us: rotate_strips(): lax.ppermute(x, 'tiles', [(i, i ^ step + 1) for i in range(tiles)])]
    ppermute x9 -> x3, starting transfers between devices: 15.1 us -> 2.09 us  [rotated(): lax.ppermute(cells, axis, [(i, (i + step) % count) for i in range(count)])]
    ppermute x6, waiting for transfers between devices: 2 us -> 4.14 us  [swap(): return lax.ppermute(cells, 'modes', [(0, 1), (1, 0)])]
    squeeze x0 -> x1, local copies, waits for them, and re-layouts: none -> 1.44 us  [on_device(): lax.dynamic_slice(object_field, (mode, jnp.where(at_end, last, 0), 0), (1...]
    pallas_call x9 -> x10, Pallas kernels: 4.01 us -> 5.32 us  [small_kernel(): pl.pallas_call(body, out_shape=out_shape, in_specs=[pl.BlockSpec(memory_s...]
  transfers between devices with their start and end apart: 19 -> 19, of which waited for: 10 -> 10; matrix products, arithmetic and copies ran while one was open for 1% -> 0% of each run, Pallas kernels for 2% -> 3%
where the time goes in v3:
time: 89.6 us; the launch traced here: 89 us
  waiting for transfers between devices  40.3 us (45%)
  starting transfers between devices  31.3 us (35%)
  Pallas kernels  11.8 us (13%)
  local copies, waits for them, and re-layouts  3.99 us (4%)
  between operations  1.51 us (2%)
    ppermute x6, waiting for transfers between devices, rotate_strips(): lax.ppermute(x, 'tiles', [(i, i ^ step + 1) for i in range(tiles)])  18.8 us
    ppermute x6, starting transfers between devices, rotate_strips(): lax.ppermute(x, 'tiles', [(i, i ^ step + 1) for i in range(tiles)])  18.6 us
    ppermute x4, waiting for transfers between devices, with_neighbours(): lax.ppermute(cells, 'tiles', [x for a, b in pairs[turn::2] for x in ((a,...  11.8 us
    ppermute x4, starting transfers between devices, with_neighbours(): lax.ppermute(cells, 'tiles', [x for a, b in pairs[turn::2] for x in ((a,...  9.93 us
    pallas_call x1, Pallas kernels, point_sums(): pl.pallas_call(functools.partial(point_kernel, owners=owners), out_shape=...  6.52 us
    ppermute x3, waiting for transfers between devices, rotated(): lax.ppermute(cells, axis, [(i, (i + step) % count) for i in range(count)])  5.61 us
    pallas_call x10, Pallas kernels, small_kernel(): pl.pallas_call(body, out_shape=out_shape, in_specs=[pl.BlockSpec(memory_s...  5.32 us
    ppermute x6, waiting for transfers between devices, swap(): return lax.ppermute(cells, 'modes', [(0, 1), (1, 0)])  4.14 us
  transfers between devices with their start and end apart: 19, of which 10 were waited for; matrix products, arithmetic and copies ran while one was open for 0% of the time, Pallas kernels for 3%

profile of v3, /device:TPU:0, one launch (start us, length us, event | category | flops | bytes accessed | tf_op | source)
XLA Modules:
  0.0 89.0 jit_solution(7268633079471175029)
XLA Ops:
  0.7 1.4 %dynamic-slice_bitcast_fusion = (f32[128,1024]{1,0:T(8,128)S(1)}, f32[128,1024]{1,0:T(8,128)S(1)}) fusion(f32[2,256,1024]{2,1,0:T(8,128)} %own.1, s32[]{:T(128)S(6)} %select_n.20, s32[]{:T(128)S(6)} %select_n.23, s32[]{:T(128)S(6)} %select_n.22), kind=kLoop, calls=%fused_computation | loop fusion | bytes 2097164 | tf_op jit(solution)/shard_map/squeeze | solution.py:439
  2.8 5.9 %collective-permute-start = (f32[128,1024]{1,0:T(8,128)S(1)}, f32[128,1024]{1,0:T(8,128)S(1)}, u32[]{:S(2)}, u32[]{:S(2)}) collective-permute-start(f32[128,1024]{1,0:T(8,128)S(1)} %get-tuple-element.53), channel_id=1, source_target_pairs={{0,4},{4,0},{8,12},{12,8},{1,5},{5,1},{9,13},{13,9},{2,6},{6,2},{1... | collective-permute-start | bytes 1572872 | tf_op jit(solution)/shard_map/ppermute | solution.py:305
  8.7 11.6 %collective-permute-done.first_a = f32[128,1024]{1,0:T(8,128)S(1)} collective-permute-done((f32[128,1024]{1,0:T(8,128)S(1)}, f32[128,1024]{1,0:T(8,128)S(1)}, u32[]{:S(2)}, u32[]{:S(2)}) %collective-permute-start) | collective-permute-done | bytes 524320 | tf_op jit(solution)/shard_map/ppermute | solution.py:305
  21.3 1.0 %copy-done.3 = bf16[512,512]{1,0:T(8,128)(2,1)S(1)} copy-done((bf16[512,512]{1,0:T(8,128)(2,1)S(1)}, bf16[512,512]{1,0:T(8,128)(2,1)}, u32[]{:S(2)}) %copy-start.3) | copy-done | bytes 524312
  22.6 1.3 %copy-done.4 = f32[2,256,1024]{2,1,0:T(8,128)S(1)} copy-done((f32[2,256,1024]{2,1,0:T(8,128)S(1)}, f32[2,256,1024]{2,1,0:T(8,128)}, u32[]{:S(2)}) %copy-start.4) | copy-done | bytes 2097176
  23.9 6.5 %point_sums.1 = (f32[2,2,512,128]{3,2,1,0:T(8,128)S(1)}, f32[2,2,512,128]{3,2,1,0:T(8,128)S(1)}, f32[2,2,512,128]{3,2,1,0:T(8,128)S(1)}, f32[2,2,512,128]{3,2,1,...) custom-call(s32[3]{0:T(128)S(1)} %pad_add_fusion.place, s32[1]{0:T(128)S(6)} %copy.11.counts, ...), custom_call_target="tpu_custom_call" | custom-call | flops 8589934592 | bytes 16777216 | tf_op jit(solution)/shard_map/point_sums/pallas_call | solution.py:278
  31.1 2.1 %collective-permute-done.9.got = f32[2,2,512,128]{3,2,1,0:T(8,128)S(1)} collective-permute-done((f32[2,2,512,128]{3,2,1,0:T(8,128)S(1)}, f32[2,2,512,128]{3,2,1,0:T(8,128)S(1)}, u32[]{:S(2)}, u32[]{:S(2)}) %collective-permute-start.9) | collective-permute-done | bytes 1048608 | tf_op jit(solution)/shard_map/ppermute | solution.py:311
  33.3 2.1 %collective-permute-done.4.got = f32[256,512]{1,0:T(8,128)S(1)} collective-permute-done((f32[256,512]{1,0:T(8,128)S(1)}, f32[256,512]{1,0:T(8,128)S(1)}, u32[]{:S(2)}, u32[]{:S(2)}) %collective-permute-start.4) | collective-permute-done | bytes 524320 | tf_op jit(solution)/shard_map/ppermute | solution.py:311
  36.0 11.0 %collective-permute-start.5 = (f32[64,512]{1,0:T(8,128)S(1)}, f32[64,512]{1,0:T(8,128)S(1)}, u32[]{:S(2)}, u32[]{:S(2)}) collective-permute-start(f32[64,512]{1,0:T(8,128)S(1)} %get-tuple-element.34), channel_id=1, source_target_pairs={{0,4},{4,0},{8,12},{12,8},{1,5},{5,1},{9,13},{13,9},{2,6},{6,2},{1... | collective-permute-start | bytes 393224 | tf_op jit(solution)/shard_map/ppermute | solution.py:467
  47.1 2.4 %collective-permute-start.7 = (f32[64,512]{1,0:T(8,128)S(1)}, f32[64,512]{1,0:T(8,128)S(1)}, u32[]{:S(2)}, u32[]{:S(2)}) collective-permute-start(f32[64,512]{1,0:T(8,128)S(1)} %get-tuple-element.36), channel_id=1, source_target_pairs={{0,12},{4,8},{8,4},{12,0},{1,13},{5,9},{9,5},{13,1},{2,14},{6,10},... | collective-permute-start | bytes 393224 | tf_op jit(solution)/shard_map/ppermute | solution.py:467
  49.4 2.7 %collective-permute-done.5.refs_1_ = f32[64,512]{1,0:T(8,128)S(1)} collective-permute-done((f32[64,512]{1,0:T(8,128)S(1)}, f32[64,512]{1,0:T(8,128)S(1)}, u32[]{:S(2)}, u32[]{:S(2)}) %collective-permute-start.5) | collective-permute-done | bytes 131104 | tf_op jit(solution)/shard_map/ppermute | solution.py:467
  52.1 7.6 %collective-permute-done.6.refs_2_ = f32[64,512]{1,0:T(8,128)S(1)} collective-permute-done((f32[64,512]{1,0:T(8,128)S(1)}, f32[64,512]{1,0:T(8,128)S(1)}, u32[]{:S(2)}, u32[]{:S(2)}) %collective-permute-start.6) | collective-permute-done | bytes 131104 | tf_op jit(solution)/shard_map/ppermute | solution.py:467
  59.8 0.7 object_mine.1
  60.5 2.7 %collective-permute-start.12 = (f32[2,2,128,128]{3,2,1,0:T(8,128)S(1)}, f32[2,2,128,128]{3,2,1,0:T(8,128)S(1)}, u32[]{:S(2)}, u32[]{:S(2)}) collective-permute-start(f32[2,2,128,128]{3,2,1,0:T(8,128)S(1)} %get-tuple-element.46), channel_id=1, source_target_pairs={{0,4},{4,0},{8,12},{12,8},{1,5},{5,1},{9,13},{13,9},{2,6},{6,2},{1... | collective-permute-start | bytes 786440 | tf_op jit(solution)/shard_map/ppermute | solution.py:305
  63.9 1.2 %collective-permute-start.11 = (f32[64,512]{1,0:T(8,128)S(1)}, f32[64,512]{1,0:T(8,128)S(1)}, u32[]{:S(2)}, u32[]{:S(2)}) collective-permute-start(f32[64,512]{1,0:T(8,128)S(1)} %probe_strips_sum.1.refs_0_), channel_id=1, source_target_pairs={{0,2},{2,0},{1,3},{3,1},{4,6},{6,4},{5,7},{7,5},{8,10},{10,8},{9,1... | collective-permute-start | bytes 393224 | tf_op jit(solution)/shard_map/ppermute | solution.py:316
  65.1 3.8 %collective-permute-done.11.refs_1_ = f32[64,512]{1,0:T(8,128)S(1)} collective-permute-done((f32[64,512]{1,0:T(8,128)S(1)}, f32[64,512]{1,0:T(8,128)S(1)}, u32[]{:S(2)}, u32[]{:S(2)}) %collective-permute-start.11) | collective-permute-done | bytes 131104 | tf_op jit(solution)/shard_map/ppermute | solution.py:316
  69.7 1.3 %collective-permute-start.17 = (f32[64,512]{1,0:T(8,128)S(1)}, f32[64,512]{1,0:T(8,128)S(1)}, u32[]{:S(2)}, u32[]{:S(2)}) collective-permute-start(f32[64,512]{1,0:T(8,128)S(1)} %probe_total.1.refs_0_), channel_id=1, source_target_pairs={{0,12},{4,8},{8,4},{12,0},{1,13},{5,9},{9,5},{13,1},{2,14},{6,10},... | collective-permute-start | bytes 393224 | tf_op jit(solution)/shard_map/ppermute | solution.py:467
  71.0 3.9 %collective-permute-start.16 = (f32[64,512]{1,0:T(8,128)S(1)}, f32[64,512]{1,0:T(8,128)S(1)}, u32[]{:S(2)}, u32[]{:S(2)}) collective-permute-start(f32[64,512]{1,0:T(8,128)S(1)} %probe_total.1.refs_0_), channel_id=1, source_target_pairs={{0,8},{4,12},{8,0},{12,4},{1,9},{5,13},{9,1},{13,5},{2,10},{6,14},... | collective-permute-start | bytes 393224 | tf_op jit(solution)/shard_map/ppermute | solution.py:467
  74.9 0.8 collective-permute-start.14
  75.7 2.3 %collective-permute-done.17.refs_3_ = f32[64,512]{1,0:T(8,128)S(1)} collective-permute-done((f32[64,512]{1,0:T(8,128)S(1)}, f32[64,512]{1,0:T(8,128)S(1)}, u32[]{:S(2)}, u32[]{:S(2)}) %collective-permute-start.17) | collective-permute-done | bytes 131104 | tf_op jit(solution)/shard_map/ppermute | solution.py:467
  78.0 6.2 %collective-permute-done.16.refs_2_ = f32[64,512]{1,0:T(8,128)S(1)} collective-permute-done((f32[64,512]{1,0:T(8,128)S(1)}, f32[64,512]{1,0:T(8,128)S(1)}, u32[]{:S(2)}, u32[]{:S(2)}) %collective-permute-start.16) | collective-permute-done | bytes 131104 | tf_op jit(solution)/shard_map/ppermute | solution.py:467
  84.8 1.8 %collective-permute-done.14.rest_0_ = f32[2,2,256,128]{3,2,1,0:T(8,128)S(1)} collective-permute-done((f32[2,2,256,128]{3,2,1,0:T(8,128)S(1)}, f32[2,2,256,128]{3,2,1,0:T(8,128)S(1)}, u32[]{:S(2)}, u32[]{:S(2)}) %collective-permute-start.14) | collective-permute-done | bytes 524320 | tf_op jit(solution)/shard_map/ppermute | solution.py:316
  86.6 0.8 object_finish.1
  87.5 1.6 %probe_both.1 = f32[2,256,512]{2,1,0:T(8,128)} custom-call(s32[3]{0:T(128)S(1)} %pad_add_fusion.place, f32[256,512]{1,0:T(8,128)S(1)} %probe_order.1.mine, f32[256,512]{1,0:T(8,128)S(1)} %collective-permute-done.18.other), custom_call_target="tpu_custom_call" | custom-call | tf_op jit(solution)/shard_map/probe_both/pallas_call | solution.py:320
  (41 shorter events, 4.8 us)
Async XLA Ops:
  0.6 20.6 %copy-start.2 = (bf16[512,512]{1,0:T(8,128)(2,1)S(1)}, bf16[512,512]{1,0:T(8,128)(2,1)}, u32[]{:S(2)}) copy-start(bf16[512,512]{1,0:T(8,128)(2,1)} %constant.35.clone.turned) | copy-start | bytes 1572868
  0.6 20.4 %copy-start.5 = (s32[1,32,2]{1,2,0:T(2,128)S(1)}, s32[1,32,2]{1,2,0:T(2,128)}, u32[]{:S(2)}) copy-start(s32[1,32,2]{1,2,0:T(2,128)} %param.10) | copy-start | bytes 772
  0.7 20.6 %copy-start = (bf16[1,8,256,256]{3,2,1,0:T(8,128)(2,1)S(1)}, bf16[1,8,256,256]{3,2,1,0:T(8,128)(2,1)}, u32[]{:S(2)}) copy-start(bf16[1,8,256,256]{3,2,1,0:T(8,128)(2,1)} %param.9) | copy-start | bytes 3145732
  0.7 20.6 %copy-start.1 = (bf16[2,256,512]{2,1,0:T(8,128)(2,1)S(1)}, bf16[2,256,512]{2,1,0:T(8,128)(2,1)}, u32[]{:S(2)}) copy-start(bf16[2,256,512]{2,1,0:T(8,128)(2,1)} %probe.1) | copy-start | bytes 1572868
  2.1 6.6 %collective-permute-start.1 = (f32[128,1024]{1,0:T(8,128)S(1)}, f32[128,1024]{1,0:T(8,128)S(1)}, u32[]{:S(2)}, u32[]{:S(2)}) collective-permute-start(f32[128,1024]{1,0:T(8,128)S(1)} %get-tuple-element.52), channel_id=1, source_target_pairs={{4,8},{8,4},{5,9},{9,5},{6,10},{10,6},{7,11},{11,7},{20,24},{24,20... | collective-permute-start | bytes 1572872 | tf_op jit(solution)/shard_map/ppermute | solution.py:305
  2.8 17.5 %collective-permute-start = (f32[128,1024]{1,0:T(8,128)S(1)}, f32[128,1024]{1,0:T(8,128)S(1)}, u32[]{:S(2)}, u32[]{:S(2)}) collective-permute-start(f32[128,1024]{1,0:T(8,128)S(1)} %get-tuple-element.53), channel_id=1, source_target_pairs={{0,4},{4,0},{8,12},{12,8},{1,5},{5,1},{9,13},{13,9},{2,6},{6,2},{1... | collective-permute-start | bytes 1572872 | tf_op jit(solution)/shard_map/ppermute | solution.py:305
  8.7 13.9 %collective-permute-start.3 = (f32[128,1024]{1,0:T(8,128)S(1)}, f32[128,1024]{1,0:T(8,128)}, u32[]{:S(2)}, u32[]{:S(2)}) collective-permute-start(f32[128,1024]{1,0:T(8,128)S(1)} %collective-permute-done.1.second_a), channel_id=1, source_target_pairs={{0,1},{1,0},{2,3},{3,2},{4,5},{5,4},{6,7},{7,6},{8,9},{9,8},{10,11... | collective-permute-start | bytes 1572872 | tf_op jit(solution)/shard_map/ppermute | solution.py:311
  20.4 2.2 %collective-permute-start.2 = (f32[128,1024]{1,0:T(8,128)S(1)}, f32[128,1024]{1,0:T(8,128)}, u32[]{:S(2)}, u32[]{:S(2)}) collective-permute-start(f32[128,1024]{1,0:T(8,128)S(1)} %collective-permute-done.first_a), channel_id=1, source_target_pairs={{0,1},{1,0},{2,3},{3,2},{4,5},{5,4},{6,7},{7,6},{8,9},{9,8},{10,11... | collective-permute-start | bytes 1572872 | tf_op jit(solution)/shard_map/ppermute | solution.py:311
  22.3 1.6 %copy-start.4 = (f32[2,256,1024]{2,1,0:T(8,128)S(1)}, f32[2,256,1024]{2,1,0:T(8,128)}, u32[]{:S(2)}) copy-start(f32[2,256,1024]{2,1,0:T(8,128)} %own.1) | copy-start | bytes 6291460
  30.4 2.7 %collective-permute-start.9 = (f32[2,2,512,128]{3,2,1,0:T(8,128)S(1)}, f32[2,2,512,128]{3,2,1,0:T(8,128)S(1)}, u32[]{:S(2)}, u32[]{:S(2)}) collective-permute-start(f32[2,2,512,128]{3,2,1,0:T(8,128)S(1)} %get-tuple-element.40), channel_id=1, source_target_pairs={{0,1},{1,0},{2,3},{3,2},{4,5},{5,4},{6,7},{7,6},{8,9},{9,8},{10,11... | collective-permute-start | bytes 3145736 | tf_op jit(solution)/shard_map/ppermute | solution.py:311
  30.5 29.3 %collective-permute-start.8 = (f32[2,2,512,128]{3,2,1,0:T(8,128)S(1)}, f32[2,2,512,128]{3,2,1,0:T(8,128)S(1)}, u32[]{:S(2)}, u32[]{:S(2)}) collective-permute-start(f32[2,2,512,128]{3,2,1,0:T(8,128)S(1)} %get-tuple-element.38), channel_id=1, source_target_pairs={{0,1},{1,0},{2,3},{3,2},{4,5},{5,4},{6,7},{7,6},{8,9},{9,8},{10,11... | collective-permute-start | bytes 3145736 | tf_op jit(solution)/shard_map/ppermute | solution.py:311
  31.0 4.4 %collective-permute-start.4 = (f32[256,512]{1,0:T(8,128)S(1)}, f32[256,512]{1,0:T(8,128)S(1)}, u32[]{:S(2)}, u32[]{:S(2)}) collective-permute-start(f32[256,512]{1,0:T(8,128)S(1)} %get-tuple-element.32), channel_id=1, source_target_pairs={{0,1},{1,0},{2,3},{3,2},{4,5},{5,4},{6,7},{7,6},{8,9},{9,8},{10,11... | collective-permute-start | bytes 1572872 | tf_op jit(solution)/shard_map/ppermute | solution.py:311
  33.3 26.5 %collective-permute-start.10 = (f32[2,2,256,128]{3,2,1,0:T(8,128)S(1)}, f32[2,2,256,128]{3,2,1,0:T(8,128)S(1)}, u32[]{:S(2)}, u32[]{:S(2)}) collective-permute-start(f32[2,2,256,128]{3,2,1,0:T(8,128)S(1)} %get-tuple-element.41), channel_id=1, source_target_pairs={{0,2},{2,0},{1,3},{3,1},{4,6},{6,4},{5,7},{7,5},{8,10},{10,8},{9,1... | collective-permute-start | bytes 1572872 | tf_op jit(solution)/shard_map/ppermute | solution.py:316
  36.0 16.1 %collective-permute-start.5 = (f32[64,512]{1,0:T(8,128)S(1)}, f32[64,512]{1,0:T(8,128)S(1)}, u32[]{:S(2)}, u32[]{:S(2)}) collective-permute-start(f32[64,512]{1,0:T(8,128)S(1)} %get-tuple-element.34), channel_id=1, source_target_pairs={{0,4},{4,0},{8,12},{12,8},{1,5},{5,1},{9,13},{13,9},{2,6},{6,2},{1... | collective-permute-start | bytes 393224 | tf_op jit(solution)/shard_map/ppermute | solution.py:467
  47.0 12.7 %collective-permute-start.6 = (f32[64,512]{1,0:T(8,128)S(1)}, f32[64,512]{1,0:T(8,128)S(1)}, u32[]{:S(2)}, u32[]{:S(2)}) collective-permute-start(f32[64,512]{1,0:T(8,128)S(1)} %get-tuple-element.35), channel_id=1, source_target_pairs={{0,8},{4,12},{8,0},{12,4},{1,9},{5,13},{9,1},{13,5},{2,10},{6,14},... | collective-permute-start | bytes 393224 | tf_op jit(solution)/shard_map/ppermute | solution.py:467
  47.1 12.7 %collective-permute-start.7 = (f32[64,512]{1,0:T(8,128)S(1)}, f32[64,512]{1,0:T(8,128)S(1)}, u32[]{:S(2)}, u32[]{:S(2)}) collective-permute-start(f32[64,512]{1,0:T(8,128)S(1)} %get-tuple-element.36), channel_id=1, source_target_pairs={{0,12},{4,8},{8,4},{12,0},{1,13},{5,9},{9,5},{13,1},{2,14},{6,10},... | collective-permute-start | bytes 393224 | tf_op jit(solution)/shard_map/ppermute | solution.py:467
  60.5 8.5 %collective-permute-start.12 = (f32[2,2,128,128]{3,2,1,0:T(8,128)S(1)}, f32[2,2,128,128]{3,2,1,0:T(8,128)S(1)}, u32[]{:S(2)}, u32[]{:S(2)}) collective-permute-start(f32[2,2,128,128]{3,2,1,0:T(8,128)S(1)} %get-tuple-element.46), channel_id=1, source_target_pairs={{0,4},{4,0},{8,12},{12,8},{1,5},{5,1},{9,13},{13,9},{2,6},{6,2},{1... | collective-permute-start | bytes 786440 | tf_op jit(solution)/shard_map/ppermute | solution.py:305
  63.2 5.8 %collective-permute-start.13 = (f32[2,2,128,128]{3,2,1,0:T(8,128)S(1)}, f32[2,2,128,128]{3,2,1,0:T(8,128)S(1)}, u32[]{:S(2)}, u32[]{:S(2)}) collective-permute-start(f32[2,2,128,128]{3,2,1,0:T(8,128)S(1)} %get-tuple-element.47), channel_id=1, source_target_pairs={{4,8},{8,4},{5,9},{9,5},{6,10},{10,6},{7,11},{11,7},{20,24},{24,20... | collective-permute-start | bytes 786440 | tf_op jit(solution)/shard_map/ppermute | solution.py:305
  63.9 5.0 %collective-permute-start.11 = (f32[64,512]{1,0:T(8,128)S(1)}, f32[64,512]{1,0:T(8,128)S(1)}, u32[]{:S(2)}, u32[]{:S(2)}) collective-permute-start(f32[64,512]{1,0:T(8,128)S(1)} %probe_strips_sum.1.refs_0_), channel_id=1, source_target_pairs={{0,2},{2,0},{1,3},{3,1},{4,6},{6,4},{5,7},{7,5},{8,10},{10,8},{9,1... | collective-permute-start | bytes 393224 | tf_op jit(solution)/shard_map/ppermute | solution.py:316
  69.7 8.3 %collective-permute-start.17 = (f32[64,512]{1,0:T(8,128)S(1)}, f32[64,512]{1,0:T(8,128)S(1)}, u32[]{:S(2)}, u32[]{:S(2)}) collective-permute-start(f32[64,512]{1,0:T(8,128)S(1)} %probe_total.1.refs_0_), channel_id=1, source_target_pairs={{0,12},{4,8},{8,4},{12,0},{1,13},{5,9},{9,5},{13,1},{2,14},{6,10},... | collective-permute-start | bytes 393224 | tf_op jit(solution)/shard_map/ppermute | solution.py:467
  71.0 13.2 %collective-permute-start.16 = (f32[64,512]{1,0:T(8,128)S(1)}, f32[64,512]{1,0:T(8,128)S(1)}, u32[]{:S(2)}, u32[]{:S(2)}) collective-permute-start(f32[64,512]{1,0:T(8,128)S(1)} %probe_total.1.refs_0_), channel_id=1, source_target_pairs={{0,8},{4,12},{8,0},{12,4},{1,9},{5,13},{9,1},{13,5},{2,10},{6,14},... | collective-permute-start | bytes 393224 | tf_op jit(solution)/shard_map/ppermute | solution.py:467
  74.9 9.3 %collective-permute-start.15 = (f32[64,512]{1,0:T(8,128)S(1)}, f32[64,512]{1,0:T(8,128)S(1)}, u32[]{:S(2)}, u32[]{:S(2)}) collective-permute-start(f32[64,512]{1,0:T(8,128)S(1)} %probe_total.1.refs_0_), channel_id=1, source_target_pairs={{0,4},{4,0},{8,12},{12,8},{1,5},{5,1},{9,13},{13,9},{2,6},{6,2},{1... | collective-permute-start | bytes 393224 | tf_op jit(solution)/shard_map/ppermute | solution.py:467
  74.9 11.7 %collective-permute-start.14 = (f32[2,2,256,128]{3,2,1,0:T(8,128)S(1)}, f32[2,2,256,128]{3,2,1,0:T(8,128)S(1)}, u32[]{:S(2)}, u32[]{:S(2)}) collective-permute-start(f32[2,2,256,128]{3,2,1,0:T(8,128)S(1)} %get-tuple-element.50), channel_id=1, source_target_pairs={{0,2},{2,0},{1,3},{3,1},{4,6},{6,4},{5,7},{7,5},{8,10},{10,8},{9,1... | collective-permute-start | bytes 1572872 | tf_op jit(solution)/shard_map/ppermute | solution.py:316
  84.7 2.7 %collective-permute-start.18 = (f32[256,512]{1,0:T(8,128)S(1)}, f32[256,512]{1,0:T(8,128)S(1)}, u32[]{:S(2)}, u32[]{:S(2)}) collective-permute-start(f32[256,512]{1,0:T(8,128)S(1)} %probe_order.1.mine), channel_id=1, source_target_pairs={{0,1},{1,0},{2,3},{3,2},{4,5},{5,4},{6,7},{7,6},{8,9},{9,8},{10,11... | collective-permute-start | bytes 1572872 | tf_op jit(solution)/shard_map/ppermute | solution.py:311
  (1 other events, 1.0 us)

commit v4 on v3

--- a/solution.py
+++ b/solution.py
@@ -20,9 +20,7 @@
     scale = 1.0 / math.sqrt(size)
     cos_part = (np.cos(angle) * scale).astype(np.float32).astype(ml_dtypes.bfloat16)
     sin_part = (-np.sin(angle) * scale).astype(np.float32).astype(ml_dtypes.bfloat16)
-    plain = np.block([[cos_part, -sin_part], [sin_part, cos_part]])
-    turned = np.block([[cos_part, sin_part], [-sin_part, cos_part]])
-    return plain, turned
+    return np.concatenate([cos_part, sin_part])
 
 
 def interleave(first, second):
@@ -240,22 +238,28 @@
         copy.wait()
 
 
-def prepare_kernel(probe, inten, plain, turned, *outs):
-    probe_f32 = outs[0]
+def prepare_kernel(probe, inten_in, table, probe_f32, inten, plain, turned):
+    side = table.shape[1]
+    cos_part, sin_part = table[:side], table[side:]
     probe_f32[...] = probe[...].astype(jnp.float32)
-    for source, target in zip((inten, plain, turned), outs[1:]):
-        target[...] = source[...]
+    inten[...] = inten_in[...]
+    for target, first, second in ((plain, -sin_part, sin_part), (turned, sin_part, -sin_part)):
+        target[:side, :side] = cos_part
+        target[side:, side:] = cos_part
+        target[:side, side:] = first
+        target[side:, :side] = second
 
 
 def prepare(probe, inten):
-    tables = [jnp.asarray(x) for x in dft_tables(probe.shape[1])]
+    side = probe.shape[1]
+    table = jnp.asarray(dft_tables(side))
+    square = jax.ShapeDtypeStruct((2 * side, 2 * side), table.dtype)
     return small_kernel(
         prepare_kernel,
-        [shape(*probe.shape)]
-        + [jax.ShapeDtypeStruct(x.shape, x.dtype) for x in (inten, *tables)],
+        [shape(*probe.shape), jax.ShapeDtypeStruct(inten.shape, inten.dtype), square, square],
         probe,
         inten,
-        *tables,
+        table,
         name="prepare",
     )
 
@@ -325,7 +329,7 @@
             for x in args
         ],
         out_specs=jax.tree.map(lambda _: pl.BlockSpec(memory_space=pltpu.VMEM), out_shape),
-        compiler_params=pltpu.CompilerParams(vmem_limit_bytes=24 * 1024 * 1024),
+        compiler_params=pltpu.CompilerParams(vmem_limit_bytes=4 * 1024 * 1024),
         cost_estimate=pl.CostEstimate(flops=0, bytes_accessed=0, transcendentals=0),
         name=name,
     )(*args)
@@ -380,22 +384,19 @@
     core[...] = kept[:, :, rim : rim + rows] + got[:, :, rim : rim + rows]
 
 
-def fold_kernel(place, core, first, second, out):
+def finish_kernel(place, core, first, second, *rest):
+    out = rest[-1]
     rim, rows = first.shape[2], core.shape[2]
-    out[...] = core[...]
     near = pl.multiple_of((place[0] % 2) * (rows - rim), 8)
     far = pl.multiple_of(rows - rim - near, 8)
-    out[:, :, pl.ds(far, rim)] += first[...]
-    out[:, :, pl.ds(near, rim)] += second[...]
-
-
-def finish_kernel(core, *rest):
-    out = rest[-1]
     for block in range(core.shape[0]):
         total = core[block]
         for other in rest[:-1]:
             total = total + other[block]
-        out[:, :, block * LANES : (block + 1) * LANES] = total
+        cols = slice(block * LANES, (block + 1) * LANES)
+        out[:, :, cols] = total
+        out[:, pl.ds(far, rim), cols] += first[block]
+        out[:, pl.ds(near, rim), cols] += second[block]
 
 
 def share_rows(index, share):
@@ -409,16 +410,36 @@
         out[...] = kept[rows] + got[rows]
 
 
-def order_kernel(place, *refs):
-    out = refs[-1]
-    share = refs[0].shape[0]
-    for step, part in enumerate(refs[:-1]):
-        out[share_rows(place[0] ^ step, share)] = part[...]
-
-
-def both_kernel(place, mine, other, out):
-    out[place[2]] = mine[...]
-    out[1 - place[2]] = other[...]
+def gather_kernel(place, *refs):
+    out, sems = refs[-2:]
+    parts = refs[:-2]
+    tiles = len(parts) // 2
+    share = parts[0].shape[0]
+    copies = []
+    for index, part in enumerate(parts):
+        swapped, step = divmod(index, tiles)
+        mode = place[2] if swapped == 0 else 1 - place[2]
+        target = out.at[mode, share_rows(place[0] ^ step, share)]
+        copies.append(pltpu.make_async_copy(part, target, sems.at[index]))
+    for copy in copies:
+        copy.start()
+    for copy in copies:
+        copy.wait()
+
+
+def gather_parts(place, parts):
+    tiles = len(parts) // 2
+    share, width = parts[0].shape
+    return pl.pallas_call(
+        gather_kernel,
+        out_shape=shape(2, tiles * share, width),
+        in_specs=[pl.BlockSpec(memory_space=pltpu.SMEM)]
+        + [pl.BlockSpec(memory_space=pltpu.VMEM)] * len(parts),
+        out_specs=pl.BlockSpec(memory_space=pl.ANY),
+        scratch_shapes=[pltpu.SemaphoreType.DMA((len(parts),))],
+        compiler_params=pltpu.CompilerParams(vmem_limit_bytes=4 * 1024 * 1024),
+        name="probe_gather",
+    )(place, *parts)
 
 
 def on_device(object_field, probe, intensity, centres, counts):
@@ -451,6 +472,14 @@
 
     rims_shape = shape(width, 2, 2 * rim, LANES)
     core_shape = shape(width, 2, strip_rows, LANES)
+    direct = tiles in (1, 2, 4)
+    total_rows, total_cols = keep_probe.shape
+    share = shape(total_rows // tiles, total_cols)
+    if direct:
+        parts = small_kernel(
+            shares_kernel, [share] * tiles, place, keep_probe, got_probe, name="probe_shares"
+        )
+        got_others, *parts = lax.optimization_barrier((got_others, *parts))
     outgoing = list(small_kernel(
         others_kernel,
         [rims_shape, core_shape] * (subs - 1),
@@ -468,13 +497,7 @@
             for step, x in enumerate(parts)
         ]
 
-    direct = tiles in (1, 2, 4)
-    total_rows, total_cols = keep_probe.shape
-    share = shape(total_rows // tiles, total_cols)
     if direct:
-        parts = small_kernel(
-            shares_kernel, [share] * tiles, place, keep_probe, got_probe, name="probe_shares"
-        )
         parts_in = rotate_strips(parts[1:])
     rims_in = rotate_all(outgoing[0::2])
     core_out = outgoing[1::2]
@@ -492,40 +515,27 @@
         part_sum, first, second = lax.optimization_barrier((part_sum, first, second))
         part_in = [rotated(part_sum, "sub", step) for step in range(1, subs)]
     first, second = with_neighbours(first, second)
-    folded = small_kernel(
-        fold_kernel, core_shape, place, core, first, second, name="object_fold"
-    )
     if direct:
         part_sum = small_kernel(add_kernel, share, part_sum, *part_in, name="probe_total")
-        part_sum, folded, *core_out = lax.optimization_barrier((part_sum, folded, *core_out))
+        part_sum, core, *core_out = lax.optimization_barrier((part_sum, core, *core_out))
         parts_in = rotate_strips([part_sum] * (tiles - 1))
     core_in = rotate_all(core_out)
-    if direct:
-        probe_mine = small_kernel(
-            order_kernel,
-            shape(total_rows, total_cols),
-            place,
-            part_sum,
-            *parts_in,
-            name="probe_order",
-        )
-    else:
-        probe_mine = lax.psum(keep_probe + got_probe, ("tiles", "sub"))
     object_grad = small_kernel(
         finish_kernel,
         shape(2, strip_rows, width * LANES),
-        folded,
+        place,
+        core,
+        first,
+        second,
         *core_in,
         name="object_finish",
     )
-    probe_grad = small_kernel(
-        both_kernel,
-        shape(2, *probe_mine.shape),
-        place,
-        probe_mine,
-        swap(probe_mine),
-        name="probe_both",
-    )
+    if direct:
+        parts = [part_sum, *parts_in]
+    else:
+        parts = [lax.psum(keep_probe + got_probe, ("tiles", "sub"))]
+    spot = place if direct else place * jnp.array([0, 0, 1], jnp.int32)
+    probe_grad = gather_parts(spot, [*parts, *[swap(x) for x in parts]])
     return (object_grad, probe_grad)
 
 

time: 89.6 us -> 87.9 us (0.981)
  Pallas kernels: 11.8 us -> 20 us
  starting transfers between devices: 31.3 us -> 25 us
  waiting for transfers between devices: 40.3 us -> 37 us
    pallas_call x1, Pallas kernels: 6.52 us -> 15.3 us  [point_sums(): pl.pallas_call(functools.partial(point_kernel, owners=owners), out_shape=...]
    ppermute x6, starting transfers between devices: 18.6 us -> 10.2 us  [rotate_strips(): lax.ppermute(x, 'tiles', [(i, i ^ step + 1) for i in range(tiles)])]
    ppermute x6, waiting for transfers between devices: 18.8 us -> 14.9 us  [rotate_strips(): lax.ppermute(x, 'tiles', [(i, i ^ step + 1) for i in range(tiles)])]
    pallas_call x10 -> x7, Pallas kernels: 5.32 us -> 3.15 us  [small_kernel(): pl.pallas_call(body, out_shape=out_shape, in_specs=[pl.BlockSpec(memory_s...]
    ppermute x4, waiting for transfers between devices: 11.8 us -> 13.4 us  [with_neighbours(): lax.ppermute(cells, 'tiles', [x for a, b in pairs[turn::2] for x in ((a,...]
    ppermute x3, waiting for transfers between devices: 5.61 us -> 4.02 us  [rotated(): lax.ppermute(cells, axis, [(i, (i + step) % count) for i in range(count)])]
    pallas_call x0 -> x1, Pallas kernels: none -> 1.57 us  [gather_parts(): pl.pallas_call(gather_kernel, out_shape=shape(2, tiles * share, width), i...]
    ppermute x4, starting transfers between devices: 9.93 us -> 11 us  [with_neighbours(): lax.ppermute(cells, 'tiles', [x for a, b in pairs[turn::2] for x in ((a,...]
  transfers between devices with their start and end apart: 19 -> 22, of which waited for: 10 -> 11; matrix products, arithmetic and copies ran while one was open for 0% -> 0% of each run, Pallas kernels for 3% -> 3%
where the time goes in v4:
time: 87.9 us; the launch traced here: 86.9 us
  waiting for transfers between devices  37 us (42%)
  starting transfers between devices  25 us (28%)
  Pallas kernels  20 us (23%)
  local copies, waits for them, and re-layouts  3.23 us (4%)
  between operations  1.53 us (2%)
    pallas_call x1, Pallas kernels, point_sums(): pl.pallas_call(functools.partial(point_kernel, owners=owners), out_shape=...  15.3 us
    ppermute x6, waiting for transfers between devices, rotate_strips(): lax.ppermute(x, 'tiles', [(i, i ^ step + 1) for i in range(tiles)])  14.9 us
    ppermute x4, waiting for transfers between devices, with_neighbours(): lax.ppermute(cells, 'tiles', [x for a, b in pairs[turn::2] for x in ((a,...  13.4 us
    ppermute x4, starting transfers between devices, with_neighbours(): lax.ppermute(cells, 'tiles', [x for a, b in pairs[turn::2] for x in ((a,...  11 us
    ppermute x6, starting transfers between devices, rotate_strips(): lax.ppermute(x, 'tiles', [(i, i ^ step + 1) for i in range(tiles)])  10.2 us
    ppermute x9, waiting for transfers between devices, swap(): return lax.ppermute(cells, 'modes', [(0, 1), (1, 0)])  4.71 us
    ppermute x3, waiting for transfers between devices, rotated(): lax.ppermute(cells, axis, [(i, (i + step) % count) for i in range(count)])  4.02 us
    pallas_call x7, Pallas kernels, small_kernel(): pl.pallas_call(body, out_shape=out_shape, in_specs=[pl.BlockSpec(memory_s...  3.15 us
  transfers between devices with their start and end apart: 22, of which 11 were waited for; matrix products, arithmetic and copies ran while one was open for 0% of the time, Pallas kernels for 3%

profile of v4, /device:TPU:0, one launch (start us, length us, event | category | flops | bytes accessed | tf_op | source)
XLA Modules:
  0.0 86.9 jit_solution(3516921697482170802)
XLA Ops:
  0.7 1.4 %dynamic-slice_bitcast_fusion = (f32[128,1024]{1,0:T(8,128)S(1)}, f32[128,1024]{1,0:T(8,128)S(1)}) fusion(f32[2,256,1024]{2,1,0:T(8,128)} %own.1, s32[]{:T(128)S(6)} %select_n.20, s32[]{:T(128)S(6)} %select_n.23, s32[]{:T(128)S(6)} %select_n.22), kind=kLoop, calls=%fused_computation | loop fusion | bytes 2097164 | tf_op jit(solution)/shard_map/squeeze | solution.py:460
  2.8 5.9 %collective-permute-start = (f32[128,1024]{1,0:T(8,128)S(1)}, f32[128,1024]{1,0:T(8,128)S(1)}, u32[]{:S(2)}, u32[]{:S(2)}) collective-permute-start(f32[128,1024]{1,0:T(8,128)S(1)} %get-tuple-element.63), channel_id=1, source_target_pairs={{0,4},{4,0},{8,12},{12,8},{1,5},{5,1},{9,13},{13,9},{2,6},{6,2},{1... | collective-permute-start | bytes 1572872 | tf_op jit(solution)/shard_map/ppermute | solution.py:309
  8.7 11.6 %collective-permute-done.first_a = f32[128,1024]{1,0:T(8,128)S(1)} collective-permute-done((f32[128,1024]{1,0:T(8,128)S(1)}, f32[128,1024]{1,0:T(8,128)S(1)}, u32[]{:S(2)}, u32[]{:S(2)}) %collective-permute-start) | collective-permute-done | bytes 524320 | tf_op jit(solution)/shard_map/ppermute | solution.py:309
  21.5 0.9 collective-permute-done.2.first_b
  22.4 1.6 %copy-done.2 = f32[2,256,1024]{2,1,0:T(8,128)S(1)} copy-done((f32[2,256,1024]{2,1,0:T(8,128)S(1)}, f32[2,256,1024]{2,1,0:T(8,128)}, u32[]{:S(2)}) %copy-start.2) | copy-done | bytes 2097176
  24.0 15.3 %point_sums.1 = (f32[2,2,512,128]{3,2,1,0:T(8,128)S(1)}, f32[2,2,512,128]{3,2,1,0:T(8,128)S(1)}, f32[2,2,512,128]{3,2,1,0:T(8,128)S(1)}, f32[2,2,512,128]{3,2,1,...) custom-call(s32[3]{0:T(128)S(1)} %pad_add_fusion.place, s32[1]{0:T(128)S(6)} %copy.10.counts, ...), custom_call_target="tpu_custom_call" | custom-call | flops 8589934592 | bytes 16777216 | tf_op jit(solution)/shard_map/point_sums/pallas_call | solution.py:282
  39.9 2.8 %collective-permute-done.5.got = f32[256,512]{1,0:T(8,128)S(1)} collective-permute-done((f32[256,512]{1,0:T(8,128)S(1)}, f32[256,512]{1,0:T(8,128)S(1)}, u32[]{:S(2)}, u32[]{:S(2)}) %collective-permute-start.5) | collective-permute-done | bytes 524320 | tf_op jit(solution)/shard_map/ppermute | solution.py:315
  43.6 3.5 %collective-permute-start.6 = (f32[64,512]{1,0:T(8,128)S(1)}, f32[64,512]{1,0:T(8,128)S(1)}, u32[]{:S(2)}, u32[]{:S(2)}) collective-permute-start(f32[64,512]{1,0:T(8,128)S(1)} %get-tuple-element.44), channel_id=1, source_target_pairs={{0,4},{4,0},{8,12},{12,8},{1,5},{5,1},{9,13},{13,9},{2,6},{6,2},{1... | collective-permute-start | bytes 393224 | tf_op jit(solution)/shard_map/ppermute | solution.py:496
  47.0 2.4 %collective-permute-start.8 = (f32[64,512]{1,0:T(8,128)S(1)}, f32[64,512]{1,0:T(8,128)S(1)}, u32[]{:S(2)}, u32[]{:S(2)}) collective-permute-start(f32[64,512]{1,0:T(8,128)S(1)} %get-tuple-element.46), channel_id=1, source_target_pairs={{0,12},{4,8},{8,4},{12,0},{1,13},{5,9},{9,5},{13,1},{2,14},{6,10},... | collective-permute-start | bytes 393224 | tf_op jit(solution)/shard_map/ppermute | solution.py:496
  49.4 1.6 %collective-permute-done.6.refs_1_ = f32[64,512]{1,0:T(8,128)S(1)} collective-permute-done((f32[64,512]{1,0:T(8,128)S(1)}, f32[64,512]{1,0:T(8,128)S(1)}, u32[]{:S(2)}, u32[]{:S(2)}) %collective-permute-start.6) | collective-permute-done | bytes 131104 | tf_op jit(solution)/shard_map/ppermute | solution.py:496
  51.0 8.3 %collective-permute-done.7.refs_2_ = f32[64,512]{1,0:T(8,128)S(1)} collective-permute-done((f32[64,512]{1,0:T(8,128)S(1)}, f32[64,512]{1,0:T(8,128)S(1)}, u32[]{:S(2)}, u32[]{:S(2)}) %collective-permute-start.7) | collective-permute-done | bytes 131104 | tf_op jit(solution)/shard_map/ppermute | solution.py:496
  59.3 0.7 object_mine.1
  60.1 1.0 %collective-permute-start.11 = (f32[64,512]{1,0:T(8,128)S(1)}, f32[64,512]{1,0:T(8,128)S(1)}, u32[]{:S(2)}, u32[]{:S(2)}) collective-permute-start(f32[64,512]{1,0:T(8,128)S(1)} %probe_strips_sum.1.refs_0_), channel_id=1, source_target_pairs={{0,2},{2,0},{1,3},{3,1},{4,6},{6,4},{5,7},{7,5},{8,10},{10,8},{9,1... | collective-permute-start | bytes 393224 | tf_op jit(solution)/shard_map/ppermute | solution.py:320
  61.1 4.0 %collective-permute-done.11.refs_1_ = f32[64,512]{1,0:T(8,128)S(1)} collective-permute-done((f32[64,512]{1,0:T(8,128)S(1)}, f32[64,512]{1,0:T(8,128)S(1)}, u32[]{:S(2)}, u32[]{:S(2)}) %collective-permute-start.11) | collective-permute-done | bytes 131104 | tf_op jit(solution)/shard_map/ppermute | solution.py:320
  65.1 1.6 %collective-permute-start.14 = (f32[2,2,256,128]{3,2,1,0:T(8,128)S(1)}, f32[2,2,256,128]{3,2,1,0:T(8,128)S(1)}, u32[]{:S(2)}, u32[]{:S(2)}) collective-permute-start(f32[2,2,256,128]{3,2,1,0:T(8,128)S(1)} %get-tuple-element.60), channel_id=1, source_target_pairs={{0,2},{2,0},{1,3},{3,1},{4,6},{6,4},{5,7},{7,5},{8,10},{10,8},{9,1... | collective-permute-start | bytes 1572872 | tf_op jit(solution)/shard_map/ppermute | solution.py:320
  66.7 2.7 %collective-permute-start.17 = (f32[64,512]{1,0:T(8,128)S(1)}, f32[64,512]{1,0:T(8,128)S(1)}, u32[]{:S(2)}, u32[]{:S(2)}) collective-permute-start(f32[64,512]{1,0:T(8,128)S(1)} %probe_total.1.refs_0_), channel_id=1, source_target_pairs={{0,12},{4,8},{8,4},{12,0},{1,13},{5,9},{9,5},{13,1},{2,14},{6,10},... | collective-permute-start | bytes 393224 | tf_op jit(solution)/shard_map/ppermute | solution.py:496
  69.8 1.3 %collective-permute-start.15 = (f32[64,512]{1,0:T(8,128)S(1)}, f32[64,512]{1,0:T(8,128)S(1)}, u32[]{:S(2)}, u32[]{:S(2)}) collective-permute-start(f32[64,512]{1,0:T(8,128)S(1)} %probe_total.1.refs_0_), channel_id=1, source_target_pairs={{0,4},{4,0},{8,12},{12,8},{1,5},{5,1},{9,13},{13,9},{2,6},{6,2},{1... | collective-permute-start | bytes 393224 | tf_op jit(solution)/shard_map/ppermute | solution.py:496
  71.1 3.3 %collective-permute-done.17.refs_3_ = f32[64,512]{1,0:T(8,128)S(1)} collective-permute-done((f32[64,512]{1,0:T(8,128)S(1)}, f32[64,512]{1,0:T(8,128)S(1)}, u32[]{:S(2)}, u32[]{:S(2)}) %collective-permute-start.17) | collective-permute-done | bytes 131104 | tf_op jit(solution)/shard_map/ppermute | solution.py:496
  74.4 3.7 %collective-permute-start.12 = (f32[2,2,128,128]{3,2,1,0:T(8,128)S(1)}, f32[2,2,128,128]{3,2,1,0:T(8,128)S(1)}, u32[]{:S(2)}, u32[]{:S(2)}) collective-permute-start(f32[2,2,128,128]{3,2,1,0:T(8,128)S(1)} %get-tuple-element.58), channel_id=1, source_target_pairs={{0,4},{4,0},{8,12},{12,8},{1,5},{5,1},{9,13},{13,9},{2,6},{6,2},{1... | collective-permute-start | bytes 786440 | tf_op jit(solution)/shard_map/ppermute | solution.py:309
  78.1 1.7 %collective-permute-done.16.refs_2_ = f32[64,512]{1,0:T(8,128)S(1)} collective-permute-done((f32[64,512]{1,0:T(8,128)S(1)}, f32[64,512]{1,0:T(8,128)S(1)}, u32[]{:S(2)}, u32[]{:S(2)}) %collective-permute-start.16) | collective-permute-done | bytes 131104 | tf_op jit(solution)/shard_map/ppermute | solution.py:496
  81.1 0.8 collective-permute-done.20.refs_6_
  82.1 1.6 %probe_gather.1 = f32[2,256,512]{2,1,0:T(8,128)} custom-call(s32[3]{0:T(128)S(1)} %pad_add_fusion.place, f32[64,512]{1,0:T(8,128)S(1)} %probe_total.1.refs_0_, f32[64,512]{1,0:T(8,128)S(1)} %collective-permute-done.15.refs_1_, f32[64,512]{1,0:T(8,128)S(1)} %collective-permute-done.16.refs_2_, f32[64,512]{1,0:T(8,128)S(1)} %collective-permute-done.17.refs_3_, ...), custom_call_target="tpu_custom_call" | custom-call | tf_op jit(solution)/shard_map/probe_gather/pallas_call | solution.py:433
  83.7 1.7 %collective-permute-done.12.first = f32[2,2,128,128]{3,2,1,0:T(8,128)S(1)} collective-permute-done((f32[2,2,128,128]{3,2,1,0:T(8,128)S(1)}, f32[2,2,128,128]{3,2,1,0:T(8,128)S(1)}, u32[]{:S(2)}, u32[]{:S(2)}) %collective-permute-start.12) | collective-permute-done | bytes 262176 | tf_op jit(solution)/shard_map/ppermute | solution.py:309
  85.4 1.5 %object_finish.1 = f32[2,256,256]{2,1,0:T(8,128)} custom-call(s32[3]{0:T(128)S(1)} %pad_add_fusion.place, f32[2,2,256,128]{3,2,1,0:T(8,128)S(1)} %get-tuple-element.57.core, f32[2,2,128,128]{3,2,1,0:T(8,128)S(1)} %collective-permute-done.12.first, f32[2,2,128,128]{3,2,1,0:T(8,128)S(1)} %collective-permute-done.13.second, ...), custom_call_target="tpu_custom_call" | custom-call | tf_op jit(solution)/shard_map/object_finish/pallas_call | solution.py:324
  (43 shorter events, 4.6 us)
Async XLA Ops:
  0.6 20.6 %copy-start.3 = (bf16[512,256]{1,0:T(8,128)(2,1)S(1)}, bf16[512,256]{1,0:T(8,128)(2,1)}, u32[]{:S(2)}) copy-start(bf16[512,256]{1,0:T(8,128)(2,1)} %constant.32.clone.table) | copy-start | bytes 786436
  0.7 20.6 %copy-start = (bf16[1,8,256,256]{3,2,1,0:T(8,128)(2,1)S(1)}, bf16[1,8,256,256]{3,2,1,0:T(8,128)(2,1)}, u32[]{:S(2)}) copy-start(bf16[1,8,256,256]{3,2,1,0:T(8,128)(2,1)} %param.8) | copy-start | bytes 3145732
  2.1 6.6 %collective-permute-start.1 = (f32[128,1024]{1,0:T(8,128)S(1)}, f32[128,1024]{1,0:T(8,128)S(1)}, u32[]{:S(2)}, u32[]{:S(2)}) collective-permute-start(f32[128,1024]{1,0:T(8,128)S(1)} %get-tuple-element.62), channel_id=1, source_target_pairs={{4,8},{8,4},{5,9},{9,5},{6,10},{10,6},{7,11},{11,7},{20,24},{24,20... | collective-permute-start | bytes 1572872 | tf_op jit(solution)/shard_map/ppermute | solution.py:309
  2.8 17.5 %collective-permute-start = (f32[128,1024]{1,0:T(8,128)S(1)}, f32[128,1024]{1,0:T(8,128)S(1)}, u32[]{:S(2)}, u32[]{:S(2)}) collective-permute-start(f32[128,1024]{1,0:T(8,128)S(1)} %get-tuple-element.63), channel_id=1, source_target_pairs={{0,4},{4,0},{8,12},{12,8},{1,5},{5,1},{9,13},{13,9},{2,6},{6,2},{1... | collective-permute-start | bytes 1572872 | tf_op jit(solution)/shard_map/ppermute | solution.py:309
  8.7 12.8 %collective-permute-start.3 = (f32[128,1024]{1,0:T(8,128)S(1)}, f32[128,1024]{1,0:T(8,128)S(1)}, u32[]{:S(2)}, u32[]{:S(2)}) collective-permute-start(f32[128,1024]{1,0:T(8,128)S(1)} %collective-permute-done.1.second_a), channel_id=1, source_target_pairs={{0,1},{1,0},{2,3},{3,2},{4,5},{5,4},{6,7},{7,6},{8,9},{9,8},{10,11... | collective-permute-start | bytes 1572872 | tf_op jit(solution)/shard_map/ppermute | solution.py:315
  20.4 2.0 %collective-permute-start.2 = (f32[128,1024]{1,0:T(8,128)S(1)}, f32[128,1024]{1,0:T(8,128)}, u32[]{:S(2)}, u32[]{:S(2)}) collective-permute-start(f32[128,1024]{1,0:T(8,128)S(1)} %collective-permute-done.first_a), channel_id=1, source_target_pairs={{0,1},{1,0},{2,3},{3,2},{4,5},{5,4},{6,7},{7,6},{8,9},{9,8},{10,11... | collective-permute-start | bytes 1572872 | tf_op jit(solution)/shard_map/ppermute | solution.py:315
  39.3 4.1 %collective-permute-start.4 = (f32[2,2,512,128]{3,2,1,0:T(8,128)S(1)}, f32[2,2,512,128]{3,2,1,0:T(8,128)S(1)}, u32[]{:S(2)}, u32[]{:S(2)}) collective-permute-start(f32[2,2,512,128]{3,2,1,0:T(8,128)S(1)} %get-tuple-element.36), channel_id=1, source_target_pairs={{0,1},{1,0},{2,3},{3,2},{4,5},{5,4},{6,7},{7,6},{8,9},{9,8},{10,11... | collective-permute-start | bytes 3145736 | tf_op jit(solution)/shard_map/ppermute | solution.py:315
  39.4 3.4 %collective-permute-start.5 = (f32[256,512]{1,0:T(8,128)S(1)}, f32[256,512]{1,0:T(8,128)S(1)}, u32[]{:S(2)}, u32[]{:S(2)}) collective-permute-start(f32[256,512]{1,0:T(8,128)S(1)} %get-tuple-element.38), channel_id=1, source_target_pairs={{0,1},{1,0},{2,3},{3,2},{4,5},{5,4},{6,7},{7,6},{8,9},{9,8},{10,11... | collective-permute-start | bytes 1572872 | tf_op jit(solution)/shard_map/ppermute | solution.py:315
  39.9 19.5 %collective-permute-start.9 = (f32[2,2,512,128]{3,2,1,0:T(8,128)S(1)}, f32[2,2,512,128]{3,2,1,0:T(8,128)S(1)}, u32[]{:S(2)}, u32[]{:S(2)}) collective-permute-start(f32[2,2,512,128]{3,2,1,0:T(8,128)S(1)} %get-tuple-element.48), channel_id=1, source_target_pairs={{0,1},{1,0},{2,3},{3,2},{4,5},{5,4},{6,7},{7,6},{8,9},{9,8},{10,11... | collective-permute-start | bytes 3145736 | tf_op jit(solution)/shard_map/ppermute | solution.py:315
  43.5 15.8 %collective-permute-start.10 = (f32[2,2,256,128]{3,2,1,0:T(8,128)S(1)}, f32[2,2,256,128]{3,2,1,0:T(8,128)S(1)}, u32[]{:S(2)}, u32[]{:S(2)}) collective-permute-start(f32[2,2,256,128]{3,2,1,0:T(8,128)S(1)} %get-tuple-element.51), channel_id=1, source_target_pairs={{0,2},{2,0},{1,3},{3,1},{4,6},{6,4},{5,7},{7,5},{8,10},{10,8},{9,1... | collective-permute-start | bytes 1572872 | tf_op jit(solution)/shard_map/ppermute | solution.py:320
  43.6 7.4 %collective-permute-start.6 = (f32[64,512]{1,0:T(8,128)S(1)}, f32[64,512]{1,0:T(8,128)S(1)}, u32[]{:S(2)}, u32[]{:S(2)}) collective-permute-start(f32[64,512]{1,0:T(8,128)S(1)} %get-tuple-element.44), channel_id=1, source_target_pairs={{0,4},{4,0},{8,12},{12,8},{1,5},{5,1},{9,13},{13,9},{2,6},{6,2},{1... | collective-permute-start | bytes 393224 | tf_op jit(solution)/shard_map/ppermute | solution.py:496
  47.0 12.2 %collective-permute-start.7 = (f32[64,512]{1,0:T(8,128)S(1)}, f32[64,512]{1,0:T(8,128)S(1)}, u32[]{:S(2)}, u32[]{:S(2)}) collective-permute-start(f32[64,512]{1,0:T(8,128)S(1)} %get-tuple-element.45), channel_id=1, source_target_pairs={{0,8},{4,12},{8,0},{12,4},{1,9},{5,13},{9,1},{13,5},{2,10},{6,14},... | collective-permute-start | bytes 393224 | tf_op jit(solution)/shard_map/ppermute | solution.py:496
  47.0 12.2 %collective-permute-start.8 = (f32[64,512]{1,0:T(8,128)S(1)}, f32[64,512]{1,0:T(8,128)S(1)}, u32[]{:S(2)}, u32[]{:S(2)}) collective-permute-start(f32[64,512]{1,0:T(8,128)S(1)} %get-tuple-element.46), channel_id=1, source_target_pairs={{0,12},{4,8},{8,4},{12,0},{1,13},{5,9},{9,5},{13,1},{2,14},{6,10},... | collective-permute-start | bytes 393224 | tf_op jit(solution)/shard_map/ppermute | solution.py:496
  60.1 5.0 %collective-permute-start.11 = (f32[64,512]{1,0:T(8,128)S(1)}, f32[64,512]{1,0:T(8,128)S(1)}, u32[]{:S(2)}, u32[]{:S(2)}) collective-permute-start(f32[64,512]{1,0:T(8,128)S(1)} %probe_strips_sum.1.refs_0_), channel_id=1, source_target_pairs={{0,2},{2,0},{1,3},{3,1},{4,6},{6,4},{5,7},{7,5},{8,10},{10,8},{9,1... | collective-permute-start | bytes 393224 | tf_op jit(solution)/shard_map/ppermute | solution.py:320
  65.1 20.3 %collective-permute-start.14 = (f32[2,2,256,128]{3,2,1,0:T(8,128)S(1)}, f32[2,2,256,128]{3,2,1,0:T(8,128)S(1)}, u32[]{:S(2)}, u32[]{:S(2)}) collective-permute-start(f32[2,2,256,128]{3,2,1,0:T(8,128)S(1)} %get-tuple-element.60), channel_id=1, source_target_pairs={{0,2},{2,0},{1,3},{3,1},{4,6},{6,4},{5,7},{7,5},{8,10},{10,8},{9,1... | collective-permute-start | bytes 1572872 | tf_op jit(solution)/shard_map/ppermute | solution.py:320
  66.7 7.7 %collective-permute-start.17 = (f32[64,512]{1,0:T(8,128)S(1)}, f32[64,512]{1,0:T(8,128)S(1)}, u32[]{:S(2)}, u32[]{:S(2)}) collective-permute-start(f32[64,512]{1,0:T(8,128)S(1)} %probe_total.1.refs_0_), channel_id=1, source_target_pairs={{0,12},{4,8},{8,4},{12,0},{1,13},{5,9},{9,5},{13,1},{2,14},{6,10},... | collective-permute-start | bytes 393224 | tf_op jit(solution)/shard_map/ppermute | solution.py:496
  69.4 5.0 %collective-permute-start.18 = (f32[64,512]{1,0:T(8,128)S(1)}, f32[64,512]{1,0:T(8,128)S(1)}, u32[]{:S(2)}, u32[]{:S(2)}) collective-permute-start(f32[64,512]{1,0:T(8,128)S(1)} %probe_total.1.refs_0_), channel_id=1, source_target_pairs={{0,1},{1,0},{2,3},{3,2},{4,5},{5,4},{6,7},{7,6},{8,9},{9,8},{10,11... | collective-permute-start | bytes 393224 | tf_op jit(solution)/shard_map/ppermute | solution.py:315
  69.4 10.4 %collective-permute-start.16 = (f32[64,512]{1,0:T(8,128)S(1)}, f32[64,512]{1,0:T(8,128)S(1)}, u32[]{:S(2)}, u32[]{:S(2)}) collective-permute-start(f32[64,512]{1,0:T(8,128)S(1)} %probe_total.1.refs_0_), channel_id=1, source_target_pairs={{0,8},{4,12},{8,0},{12,4},{1,9},{5,13},{9,1},{13,5},{2,10},{6,14},... | collective-permute-start | bytes 393224 | tf_op jit(solution)/shard_map/ppermute | solution.py:496
  69.8 10.7 %collective-permute-start.15 = (f32[64,512]{1,0:T(8,128)S(1)}, f32[64,512]{1,0:T(8,128)S(1)}, u32[]{:S(2)}, u32[]{:S(2)}) collective-permute-start(f32[64,512]{1,0:T(8,128)S(1)} %probe_total.1.refs_0_), channel_id=1, source_target_pairs={{0,4},{4,0},{8,12},{12,8},{1,5},{5,1},{9,13},{13,9},{2,6},{6,2},{1... | collective-permute-start | bytes 393224 | tf_op jit(solution)/shard_map/ppermute | solution.py:496
  74.3 6.2 %collective-permute-start.21 = (f32[64,512]{1,0:T(8,128)S(1)}, f32[64,512]{1,0:T(8,128)S(1)}, u32[]{:S(2)}, u32[]{:S(2)}) collective-permute-start(f32[64,512]{1,0:T(8,128)S(1)} %collective-permute-done.17.refs_3_), channel_id=1, source_target_pairs={{0,1},{1,0},{2,3},{3,2},{4,5},{5,4},{6,7},{7,6},{8,9},{9,8},{10,11... | collective-permute-start | bytes 393224 | tf_op jit(solution)/shard_map/ppermute | solution.py:315
  74.4 11.0 %collective-permute-start.12 = (f32[2,2,128,128]{3,2,1,0:T(8,128)S(1)}, f32[2,2,128,128]{3,2,1,0:T(8,128)S(1)}, u32[]{:S(2)}, u32[]{:S(2)}) collective-permute-start(f32[2,2,128,128]{3,2,1,0:T(8,128)S(1)} %get-tuple-element.58), channel_id=1, source_target_pairs={{0,4},{4,0},{8,12},{12,8},{1,5},{5,1},{9,13},{13,9},{2,6},{6,2},{1... | collective-permute-start | bytes 786440 | tf_op jit(solution)/shard_map/ppermute | solution.py:309
  79.8 5.6 %collective-permute-start.13 = (f32[2,2,128,128]{3,2,1,0:T(8,128)S(1)}, f32[2,2,128,128]{3,2,1,0:T(8,128)S(1)}, u32[]{:S(2)}, u32[]{:S(2)}) collective-permute-start(f32[2,2,128,128]{3,2,1,0:T(8,128)S(1)} %get-tuple-element.59), channel_id=1, source_target_pairs={{4,8},{8,4},{5,9},{9,5},{6,10},{10,6},{7,11},{11,7},{20,24},{24,20... | collective-permute-start | bytes 786440 | tf_op jit(solution)/shard_map/ppermute | solution.py:309
  80.5 1.4 %collective-permute-start.20 = (f32[64,512]{1,0:T(8,128)S(1)}, f32[64,512]{1,0:T(8,128)S(1)}, u32[]{:S(2)}, u32[]{:S(2)}) collective-permute-start(f32[64,512]{1,0:T(8,128)S(1)} %collective-permute-done.16.refs_2_), channel_id=1, source_target_pairs={{0,1},{1,0},{2,3},{3,2},{4,5},{5,4},{6,7},{7,6},{8,9},{9,8},{10,11... | collective-permute-start | bytes 393224 | tf_op jit(solution)/shard_map/ppermute | solution.py:315
  80.6 1.5 %collective-permute-start.19 = (f32[64,512]{1,0:T(8,128)S(1)}, f32[64,512]{1,0:T(8,128)S(1)}, u32[]{:S(2)}, u32[]{:S(2)}) collective-permute-start(f32[64,512]{1,0:T(8,128)S(1)} %collective-permute-done.15.refs_1_), channel_id=1, source_target_pairs={{0,1},{1,0},{2,3},{3,2},{4,5},{5,4},{6,7},{7,6},{8,9},{9,8},{10,11... | collective-permute-start | bytes 393224 | tf_op jit(solution)/shard_map/ppermute | solution.py:315
  (3 other events, 42.5 us)

commit v5 on v4

--- a/solution.py
+++ b/solution.py
@@ -302,12 +302,12 @@
     )(place, counts, spots, own, *halos, *prepared)
 
 
-def with_neighbours(first, second):
+def with_neighbours(first, second, turns=(0, 1)):
     count = lax.axis_size("tiles")
     pairs = [(i, i + 1) for i in range(count - 1)]
     return [
         lax.ppermute(cells, "tiles", [x for a, b in pairs[turn::2] for x in ((a, b), (b, a))])
-        for turn, cells in enumerate((first, second))
+        for turn, cells in zip(turns, (first, second))
     ]
 
 
@@ -384,19 +384,22 @@
     core[...] = kept[:, :, rim : rim + rows] + got[:, :, rim : rim + rows]
 
 
-def finish_kernel(place, core, first, second, *rest):
-    out = rest[-1]
+def fold_kernel(place, core, second, first, out):
     rim, rows = first.shape[2], core.shape[2]
+    out[...] = core[...]
     near = pl.multiple_of((place[0] % 2) * (rows - rim), 8)
     far = pl.multiple_of(rows - rim - near, 8)
+    out[:, :, pl.ds(far, rim)] += first[...]
+    out[:, :, pl.ds(near, rim)] += second[...]
+
+
+def finish_kernel(core, *rest):
+    out = rest[-1]
     for block in range(core.shape[0]):
         total = core[block]
         for other in rest[:-1]:
             total = total + other[block]
-        cols = slice(block * LANES, (block + 1) * LANES)
-        out[:, :, cols] = total
-        out[:, pl.ds(far, rim), cols] += first[block]
-        out[:, pl.ds(near, rim), cols] += second[block]
+        out[:, :, block * LANES : (block + 1) * LANES] = total
 
 
 def share_rows(index, share):
@@ -514,19 +517,21 @@
         part_sum = small_kernel(add_kernel, share, parts[0], *parts_in, name="probe_strips_sum")
         part_sum, first, second = lax.optimization_barrier((part_sum, first, second))
         part_in = [rotated(part_sum, "sub", step) for step in range(1, subs)]
-    first, second = with_neighbours(first, second)
+    second, first = with_neighbours(second, first, (1, 0))
     if direct:
         part_sum = small_kernel(add_kernel, share, part_sum, *part_in, name="probe_total")
         part_sum, core, *core_out = lax.optimization_barrier((part_sum, core, *core_out))
         parts_in = rotate_strips([part_sum] * (tiles - 1))
+    folded = small_kernel(
+        fold_kernel, core_shape, place, core, second, first, name="object_fold"
+    )
+    if direct:
+        parts_in[1], folded = lax.optimization_barrier((parts_in[1], folded))
     core_in = rotate_all(core_out)
     object_grad = small_kernel(
         finish_kernel,
         shape(2, strip_rows, width * LANES),
-        place,
-        core,
-        first,
-        second,
+        folded,
         *core_in,
         name="object_finish",
     )

time: 87.9 us -> 86.1 us (0.980)
  waiting for transfers between devices: 37 us -> 33.3 us
  starting transfers between devices: 25 us -> 27.8 us
    ppermute x6, starting transfers between devices: 10.2 us -> 14 us  [rotate_strips(): lax.ppermute(x, 'tiles', [(i, i ^ step + 1) for i in range(tiles)])]
    ppermute x4, starting transfers between devices: 11 us -> 8.12 us  [with_neighbours(): lax.ppermute(cells, 'tiles', [x for a, b in pairs[turn::2] for x in ((a,...]
    ppermute x3, starting transfers between devices: 2.65 us -> 4.51 us  [rotated(): lax.ppermute(cells, axis, [(i, (i + step) % count) for i in range(count)])]
    ppermute x6, waiting for transfers between devices: 14.9 us -> 13.3 us  [rotate_strips(): lax.ppermute(x, 'tiles', [(i, i ^ step + 1) for i in range(tiles)])]
    ppermute x4, waiting for transfers between devices: 13.4 us -> 12.2 us  [with_neighbours(): lax.ppermute(cells, 'tiles', [x for a, b in pairs[turn::2] for x in ((a,...]
    ppermute x3, waiting for transfers between devices: 4.02 us -> 3.14 us  [rotated(): lax.ppermute(cells, axis, [(i, (i + step) % count) for i in range(count)])]
    pallas_call x7 -> x8, Pallas kernels: 3.15 us -> 3.15 us  [small_kernel(): pl.pallas_call(body, out_shape=out_shape, in_specs=[pl.BlockSpec(memory_s...]
  transfers between devices with their start and end apart: 22 -> 22, of which waited for: 11 -> 12; matrix products, arithmetic and copies ran while one was open for 0% -> 0% of each run, Pallas kernels for 3% -> 4%
where the time goes in v5:
time: 86.1 us; the launch traced here: 85.9 us
  waiting for transfers between devices  33.3 us (39%)
  starting transfers between devices  27.8 us (32%)
  Pallas kernels  19.9 us (23%)
  local copies, waits for them, and re-layouts  3.23 us (4%)
  between operations  1.52 us (2%)
    pallas_call x1, Pallas kernels, point_sums(): pl.pallas_call(functools.partial(point_kernel, owners=owners), out_shape=...  15.2 us
    ppermute x6, starting transfers between devices, rotate_strips(): lax.ppermute(x, 'tiles', [(i, i ^ step + 1) for i in range(tiles)])  14 us
    ppermute x6, waiting for transfers between devices, rotate_strips(): lax.ppermute(x, 'tiles', [(i, i ^ step + 1) for i in range(tiles)])  13.3 us
    ppermute x4, waiting for transfers between devices, with_neighbours(): lax.ppermute(cells, 'tiles', [x for a, b in pairs[turn::2] for x in ((a,...  12.2 us
    ppermute x4, starting transfers between devices, with_neighbours(): lax.ppermute(cells, 'tiles', [x for a, b in pairs[turn::2] for x in ((a,...  8.12 us
    ppermute x9, waiting for transfers between devices, swap(): return lax.ppermute(cells, 'modes', [(0, 1), (1, 0)])  4.71 us
    ppermute x3, starting transfers between devices, rotated(): lax.ppermute(cells, axis, [(i, (i + step) % count) for i in range(count)])  4.51 us
    pallas_call x8, Pallas kernels, small_kernel(): pl.pallas_call(body, out_shape=out_shape, in_specs=[pl.BlockSpec(memory_s...  3.15 us
  transfers between devices with their start and end apart: 22, of which 12 were waited for; matrix products, arithmetic and copies ran while one was open for 0% of the time, Pallas kernels for 4%

profile of v5, /device:TPU:0, one launch (start us, length us, event | category | flops | bytes accessed | tf_op | source)
XLA Modules:
  0.0 85.9 jit_solution(779979584735417376)
XLA Ops:
  0.7 1.4 %dynamic-slice_bitcast_fusion = (f32[128,1024]{1,0:T(8,128)S(1)}, f32[128,1024]{1,0:T(8,128)S(1)}) fusion(f32[2,256,1024]{2,1,0:T(8,128)} %own.1, s32[]{:T(128)S(6)} %select_n.20, s32[]{:T(128)S(6)} %select_n.23, s32[]{:T(128)S(6)} %select_n.22), kind=kLoop, calls=%fused_computation | loop fusion | bytes 2097164 | tf_op jit(solution)/shard_map/squeeze | solution.py:463
  2.1 0.7 collective-permute-start.1
  2.8 5.9 %collective-permute-start = (f32[128,1024]{1,0:T(8,128)S(1)}, f32[128,1024]{1,0:T(8,128)S(1)}, u32[]{:S(2)}, u32[]{:S(2)}) collective-permute-start(f32[128,1024]{1,0:T(8,128)S(1)} %get-tuple-element.67), channel_id=1, source_target_pairs={{0,4},{4,0},{8,12},{12,8},{1,5},{5,1},{9,13},{13,9},{2,6},{6,2},{1... | collective-permute-start | bytes 1572872 | tf_op jit(solution)/shard_map/ppermute | solution.py:309
  8.7 11.6 %collective-permute-done.first_a = f32[128,1024]{1,0:T(8,128)S(1)} collective-permute-done((f32[128,1024]{1,0:T(8,128)S(1)}, f32[128,1024]{1,0:T(8,128)S(1)}, u32[]{:S(2)}, u32[]{:S(2)}) %collective-permute-start) | collective-permute-done | bytes 524320 | tf_op jit(solution)/shard_map/ppermute | solution.py:309
  21.5 0.9 collective-permute-done.2.first_b
  22.4 1.6 %copy-done.2 = f32[2,256,1024]{2,1,0:T(8,128)S(1)} copy-done((f32[2,256,1024]{2,1,0:T(8,128)S(1)}, f32[2,256,1024]{2,1,0:T(8,128)}, u32[]{:S(2)}) %copy-start.2) | copy-done | bytes 2097176
  24.0 15.2 %point_sums.1 = (f32[2,2,512,128]{3,2,1,0:T(8,128)S(1)}, f32[2,2,512,128]{3,2,1,0:T(8,128)S(1)}, f32[2,2,512,128]{3,2,1,0:T(8,128)S(1)}, f32[2,2,512,128]{3,2,1,...) custom-call(s32[3]{0:T(128)S(1)} %pad_add_fusion.place, s32[1]{0:T(128)S(6)} %copy.10.counts, ...), custom_call_target="tpu_custom_call" | custom-call | flops 8589934592 | bytes 16777216 | tf_op jit(solution)/shard_map/point_sums/pallas_call | solution.py:282
  39.9 2.8 %collective-permute-done.5.got = f32[256,512]{1,0:T(8,128)S(1)} collective-permute-done((f32[256,512]{1,0:T(8,128)S(1)}, f32[256,512]{1,0:T(8,128)S(1)}, u32[]{:S(2)}, u32[]{:S(2)}) %collective-permute-start.5) | collective-permute-done | bytes 524320 | tf_op jit(solution)/shard_map/ppermute | solution.py:315
  43.5 2.1 %collective-permute-start.6 = (f32[64,512]{1,0:T(8,128)S(1)}, f32[64,512]{1,0:T(8,128)S(1)}, u32[]{:S(2)}, u32[]{:S(2)}) collective-permute-start(f32[64,512]{1,0:T(8,128)S(1)} %get-tuple-element.46), channel_id=1, source_target_pairs={{0,4},{4,0},{8,12},{12,8},{1,5},{5,1},{9,13},{13,9},{2,6},{6,2},{1... | collective-permute-start | bytes 393224 | tf_op jit(solution)/shard_map/ppermute | solution.py:499
  45.6 1.8 %collective-permute-start.7 = (f32[64,512]{1,0:T(8,128)S(1)}, f32[64,512]{1,0:T(8,128)S(1)}, u32[]{:S(2)}, u32[]{:S(2)}) collective-permute-start(f32[64,512]{1,0:T(8,128)S(1)} %get-tuple-element.47), channel_id=1, source_target_pairs={{0,8},{4,12},{8,0},{12,4},{1,9},{5,13},{9,1},{13,5},{2,10},{6,14},... | collective-permute-start | bytes 393224 | tf_op jit(solution)/shard_map/ppermute | solution.py:499
  47.4 1.5 %collective-permute-start.8 = (f32[64,512]{1,0:T(8,128)S(1)}, f32[64,512]{1,0:T(8,128)S(1)}, u32[]{:S(2)}, u32[]{:S(2)}) collective-permute-start(f32[64,512]{1,0:T(8,128)S(1)} %get-tuple-element.48), channel_id=1, source_target_pairs={{0,12},{4,8},{8,4},{12,0},{1,13},{5,9},{9,5},{13,1},{2,14},{6,10},... | collective-permute-start | bytes 393224 | tf_op jit(solution)/shard_map/ppermute | solution.py:499
  48.9 2.6 %collective-permute-done.6.refs_1_ = f32[64,512]{1,0:T(8,128)S(1)} collective-permute-done((f32[64,512]{1,0:T(8,128)S(1)}, f32[64,512]{1,0:T(8,128)S(1)}, u32[]{:S(2)}, u32[]{:S(2)}) %collective-permute-start.6) | collective-permute-done | bytes 131104 | tf_op jit(solution)/shard_map/ppermute | solution.py:499
  51.5 7.0 %collective-permute-done.7.refs_2_ = f32[64,512]{1,0:T(8,128)S(1)} collective-permute-done((f32[64,512]{1,0:T(8,128)S(1)}, f32[64,512]{1,0:T(8,128)S(1)}, u32[]{:S(2)}, u32[]{:S(2)}) %collective-permute-start.7) | collective-permute-done | bytes 131104 | tf_op jit(solution)/shard_map/ppermute | solution.py:499
  58.6 0.7 object_mine.1
  59.3 1.9 %collective-permute-start.11 = (f32[64,512]{1,0:T(8,128)S(1)}, f32[64,512]{1,0:T(8,128)S(1)}, u32[]{:S(2)}, u32[]{:S(2)}) collective-permute-start(f32[64,512]{1,0:T(8,128)S(1)} %probe_strips_sum.1.refs_0_), channel_id=1, source_target_pairs={{0,2},{2,0},{1,3},{3,1},{4,6},{6,4},{5,7},{7,5},{8,10},{10,8},{9,1... | collective-permute-start | bytes 393224 | tf_op jit(solution)/shard_map/ppermute | solution.py:320
  61.8 3.1 %collective-permute-done.11.refs_1_ = f32[64,512]{1,0:T(8,128)S(1)} collective-permute-done((f32[64,512]{1,0:T(8,128)S(1)}, f32[64,512]{1,0:T(8,128)S(1)}, u32[]{:S(2)}, u32[]{:S(2)}) %collective-permute-start.11) | collective-permute-done | bytes 131104 | tf_op jit(solution)/shard_map/ppermute | solution.py:320
  65.0 2.5 %collective-permute-start.15 = (f32[2,2,256,128]{3,2,1,0:T(8,128)S(1)}, f32[2,2,256,128]{3,2,1,0:T(8,128)S(1)}, u32[]{:S(2)}, u32[]{:S(2)}) collective-permute-start(f32[2,2,256,128]{3,2,1,0:T(8,128)S(1)} %get-tuple-element.64), channel_id=1, source_target_pairs={{0,2},{2,0},{1,3},{3,1},{4,6},{6,4},{5,7},{7,5},{8,10},{10,8},{9,1... | collective-permute-start | bytes 1572872 | tf_op jit(solution)/shard_map/ppermute | solution.py:320
  67.5 0.9 %collective-permute-start.14 = (f32[2,2,128,128]{3,2,1,0:T(8,128)S(1)}, f32[2,2,128,128]{3,2,1,0:T(8,128)S(1)}, u32[]{:S(2)}, u32[]{:S(2)}) collective-permute-start(f32[2,2,128,128]{3,2,1,0:T(8,128)S(1)} %get-tuple-element.62), channel_id=1, source_target_pairs={{0,4},{4,0},{8,12},{12,8},{1,5},{5,1},{9,13},{13,9},{2,6},{6,2},{1... | collective-permute-start | bytes 786440 | tf_op jit(solution)/shard_map/ppermute | solution.py:309
  68.4 0.9 %collective-permute-start.12 = (f32[64,512]{1,0:T(8,128)S(1)}, f32[64,512]{1,0:T(8,128)S(1)}, u32[]{:S(2)}, u32[]{:S(2)}) collective-permute-start(f32[64,512]{1,0:T(8,128)S(1)} %probe_total.1.refs_0_), channel_id=1, source_target_pairs={{0,8},{4,12},{8,0},{12,4},{1,9},{5,13},{9,1},{13,5},{2,10},{6,14},... | collective-permute-start | bytes 393224 | tf_op jit(solution)/shard_map/ppermute | solution.py:499
  69.3 2.6 %collective-permute-start.17 = (f32[64,512]{1,0:T(8,128)S(1)}, f32[64,512]{1,0:T(8,128)S(1)}, u32[]{:S(2)}, u32[]{:S(2)}) collective-permute-start(f32[64,512]{1,0:T(8,128)S(1)} %probe_total.1.refs_0_), channel_id=1, source_target_pairs={{0,12},{4,8},{8,4},{12,0},{1,13},{5,9},{9,5},{13,1},{2,14},{6,10},... | collective-permute-start | bytes 393224 | tf_op jit(solution)/shard_map/ppermute | solution.py:499
  71.9 5.1 %collective-permute-start.16 = (f32[64,512]{1,0:T(8,128)S(1)}, f32[64,512]{1,0:T(8,128)S(1)}, u32[]{:S(2)}, u32[]{:S(2)}) collective-permute-start(f32[64,512]{1,0:T(8,128)S(1)} %probe_total.1.refs_0_), channel_id=1, source_target_pairs={{0,4},{4,0},{8,12},{12,8},{1,5},{5,1},{9,13},{13,9},{2,6},{6,2},{1... | collective-permute-start | bytes 393224 | tf_op jit(solution)/shard_map/ppermute | solution.py:499
  78.3 3.2 %collective-permute-done.12.refs_2_ = f32[64,512]{1,0:T(8,128)S(1)} collective-permute-done((f32[64,512]{1,0:T(8,128)S(1)}, f32[64,512]{1,0:T(8,128)S(1)}, u32[]{:S(2)}, u32[]{:S(2)}) %collective-permute-start.12) | collective-permute-done | bytes 131104 | tf_op jit(solution)/shard_map/ppermute | solution.py:499
  83.5 1.6 %probe_gather.1 = f32[2,256,512]{2,1,0:T(8,128)} custom-call(s32[3]{0:T(128)S(1)} %pad_add_fusion.place, f32[64,512]{1,0:T(8,128)S(1)} %probe_total.1.refs_0_, f32[64,512]{1,0:T(8,128)S(1)} %collective-permute-done.16.refs_1_, f32[64,512]{1,0:T(8,128)S(1)} %collective-permute-done.12.refs_2_, f32[64,512]{1,0:T(8,128)S(1)} %collective-permute-done.17.refs_3_, ...), custom_call_target="tpu_custom_call" | custom-call | tf_op jit(solution)/shard_map/probe_gather/pallas_call | solution.py:436
  85.1 0.8 object_finish.1
  (44 shorter events, 5.8 us)
Async XLA Ops:
  0.6 20.6 %copy-start.3 = (bf16[512,256]{1,0:T(8,128)(2,1)S(1)}, bf16[512,256]{1,0:T(8,128)(2,1)}, u32[]{:S(2)}) copy-start(bf16[512,256]{1,0:T(8,128)(2,1)} %constant.32.clone.table) | copy-start | bytes 786436
  0.7 20.6 %copy-start = (bf16[1,8,256,256]{3,2,1,0:T(8,128)(2,1)S(1)}, bf16[1,8,256,256]{3,2,1,0:T(8,128)(2,1)}, u32[]{:S(2)}) copy-start(bf16[1,8,256,256]{3,2,1,0:T(8,128)(2,1)} %param.8) | copy-start | bytes 3145732
  2.1 6.6 %collective-permute-start.1 = (f32[128,1024]{1,0:T(8,128)S(1)}, f32[128,1024]{1,0:T(8,128)S(1)}, u32[]{:S(2)}, u32[]{:S(2)}) collective-permute-start(f32[128,1024]{1,0:T(8,128)S(1)} %get-tuple-element.66), channel_id=1, source_target_pairs={{4,8},{8,4},{5,9},{9,5},{6,10},{10,6},{7,11},{11,7},{20,24},{24,20... | collective-permute-start | bytes 1572872 | tf_op jit(solution)/shard_map/ppermute | solution.py:309
  2.8 17.5 %collective-permute-start = (f32[128,1024]{1,0:T(8,128)S(1)}, f32[128,1024]{1,0:T(8,128)S(1)}, u32[]{:S(2)}, u32[]{:S(2)}) collective-permute-start(f32[128,1024]{1,0:T(8,128)S(1)} %get-tuple-element.67), channel_id=1, source_target_pairs={{0,4},{4,0},{8,12},{12,8},{1,5},{5,1},{9,13},{13,9},{2,6},{6,2},{1... | collective-permute-start | bytes 1572872 | tf_op jit(solution)/shard_map/ppermute | solution.py:309
  8.7 12.8 %collective-permute-start.3 = (f32[128,1024]{1,0:T(8,128)S(1)}, f32[128,1024]{1,0:T(8,128)S(1)}, u32[]{:S(2)}, u32[]{:S(2)}) collective-permute-start(f32[128,1024]{1,0:T(8,128)S(1)} %collective-permute-done.1.second_a), channel_id=1, source_target_pairs={{0,1},{1,0},{2,3},{3,2},{4,5},{5,4},{6,7},{7,6},{8,9},{9,8},{10,11... | collective-permute-start | bytes 1572872 | tf_op jit(solution)/shard_map/ppermute | solution.py:315
  20.4 2.0 %collective-permute-start.2 = (f32[128,1024]{1,0:T(8,128)S(1)}, f32[128,1024]{1,0:T(8,128)}, u32[]{:S(2)}, u32[]{:S(2)}) collective-permute-start(f32[128,1024]{1,0:T(8,128)S(1)} %collective-permute-done.first_a), channel_id=1, source_target_pairs={{0,1},{1,0},{2,3},{3,2},{4,5},{5,4},{6,7},{7,6},{8,9},{9,8},{10,11... | collective-permute-start | bytes 1572872 | tf_op jit(solution)/shard_map/ppermute | solution.py:315
  39.2 4.1 %collective-permute-start.4 = (f32[2,2,512,128]{3,2,1,0:T(8,128)S(1)}, f32[2,2,512,128]{3,2,1,0:T(8,128)S(1)}, u32[]{:S(2)}, u32[]{:S(2)}) collective-permute-start(f32[2,2,512,128]{3,2,1,0:T(8,128)S(1)} %get-tuple-element.38), channel_id=1, source_target_pairs={{0,1},{1,0},{2,3},{3,2},{4,5},{5,4},{6,7},{7,6},{8,9},{9,8},{10,11... | collective-permute-start | bytes 3145736 | tf_op jit(solution)/shard_map/ppermute | solution.py:315
  39.3 3.4 %collective-permute-start.5 = (f32[256,512]{1,0:T(8,128)S(1)}, f32[256,512]{1,0:T(8,128)S(1)}, u32[]{:S(2)}, u32[]{:S(2)}) collective-permute-start(f32[256,512]{1,0:T(8,128)S(1)} %get-tuple-element.40), channel_id=1, source_target_pairs={{0,1},{1,0},{2,3},{3,2},{4,5},{5,4},{6,7},{7,6},{8,9},{9,8},{10,11... | collective-permute-start | bytes 1572872 | tf_op jit(solution)/shard_map/ppermute | solution.py:315
  39.8 18.7 %collective-permute-start.9 = (f32[2,2,512,128]{3,2,1,0:T(8,128)S(1)}, f32[2,2,512,128]{3,2,1,0:T(8,128)S(1)}, u32[]{:S(2)}, u32[]{:S(2)}) collective-permute-start(f32[2,2,512,128]{3,2,1,0:T(8,128)S(1)} %get-tuple-element.50), channel_id=1, source_target_pairs={{0,1},{1,0},{2,3},{3,2},{4,5},{5,4},{6,7},{7,6},{8,9},{9,8},{10,11... | collective-permute-start | bytes 3145736 | tf_op jit(solution)/shard_map/ppermute | solution.py:315
  43.4 15.1 %collective-permute-start.10 = (f32[2,2,256,128]{3,2,1,0:T(8,128)S(1)}, f32[2,2,256,128]{3,2,1,0:T(8,128)S(1)}, u32[]{:S(2)}, u32[]{:S(2)}) collective-permute-start(f32[2,2,256,128]{3,2,1,0:T(8,128)S(1)} %get-tuple-element.53), channel_id=1, source_target_pairs={{0,2},{2,0},{1,3},{3,1},{4,6},{6,4},{5,7},{7,5},{8,10},{10,8},{9,1... | collective-permute-start | bytes 1572872 | tf_op jit(solution)/shard_map/ppermute | solution.py:320
  43.5 8.0 %collective-permute-start.6 = (f32[64,512]{1,0:T(8,128)S(1)}, f32[64,512]{1,0:T(8,128)S(1)}, u32[]{:S(2)}, u32[]{:S(2)}) collective-permute-start(f32[64,512]{1,0:T(8,128)S(1)} %get-tuple-element.46), channel_id=1, source_target_pairs={{0,4},{4,0},{8,12},{12,8},{1,5},{5,1},{9,13},{13,9},{2,6},{6,2},{1... | collective-permute-start | bytes 393224 | tf_op jit(solution)/shard_map/ppermute | solution.py:499
  45.6 12.9 %collective-permute-start.7 = (f32[64,512]{1,0:T(8,128)S(1)}, f32[64,512]{1,0:T(8,128)S(1)}, u32[]{:S(2)}, u32[]{:S(2)}) collective-permute-start(f32[64,512]{1,0:T(8,128)S(1)} %get-tuple-element.47), channel_id=1, source_target_pairs={{0,8},{4,12},{8,0},{12,4},{1,9},{5,13},{9,1},{13,5},{2,10},{6,14},... | collective-permute-start | bytes 393224 | tf_op jit(solution)/shard_map/ppermute | solution.py:499
  47.4 11.1 %collective-permute-start.8 = (f32[64,512]{1,0:T(8,128)S(1)}, f32[64,512]{1,0:T(8,128)S(1)}, u32[]{:S(2)}, u32[]{:S(2)}) collective-permute-start(f32[64,512]{1,0:T(8,128)S(1)} %get-tuple-element.48), channel_id=1, source_target_pairs={{0,12},{4,8},{8,4},{12,0},{1,13},{5,9},{9,5},{13,1},{2,14},{6,10},... | collective-permute-start | bytes 393224 | tf_op jit(solution)/shard_map/ppermute | solution.py:499
  59.3 5.7 %collective-permute-start.11 = (f32[64,512]{1,0:T(8,128)S(1)}, f32[64,512]{1,0:T(8,128)S(1)}, u32[]{:S(2)}, u32[]{:S(2)}) collective-permute-start(f32[64,512]{1,0:T(8,128)S(1)} %probe_strips_sum.1.refs_0_), channel_id=1, source_target_pairs={{0,2},{2,0},{1,3},{3,1},{4,6},{6,4},{5,7},{7,5},{8,10},{10,8},{9,1... | collective-permute-start | bytes 393224 | tf_op jit(solution)/shard_map/ppermute | solution.py:320
  61.2 10.8 %collective-permute-start.13 = (f32[2,2,128,128]{3,2,1,0:T(8,128)S(1)}, f32[2,2,128,128]{3,2,1,0:T(8,128)S(1)}, u32[]{:S(2)}, u32[]{:S(2)}) collective-permute-start(f32[2,2,128,128]{3,2,1,0:T(8,128)S(1)} %get-tuple-element.61), channel_id=1, source_target_pairs={{4,8},{8,4},{5,9},{9,5},{6,10},{10,6},{7,11},{11,7},{20,24},{24,20... | collective-permute-start | bytes 786440 | tf_op jit(solution)/shard_map/ppermute | solution.py:309
  65.0 20.1 %collective-permute-start.15 = (f32[2,2,256,128]{3,2,1,0:T(8,128)S(1)}, f32[2,2,256,128]{3,2,1,0:T(8,128)S(1)}, u32[]{:S(2)}, u32[]{:S(2)}) collective-permute-start(f32[2,2,256,128]{3,2,1,0:T(8,128)S(1)} %get-tuple-element.64), channel_id=1, source_target_pairs={{0,2},{2,0},{1,3},{3,1},{4,6},{6,4},{5,7},{7,5},{8,10},{10,8},{9,1... | collective-permute-start | bytes 1572872 | tf_op jit(solution)/shard_map/ppermute | solution.py:320
  67.5 10.1 %collective-permute-start.14 = (f32[2,2,128,128]{3,2,1,0:T(8,128)S(1)}, f32[2,2,128,128]{3,2,1,0:T(8,128)S(1)}, u32[]{:S(2)}, u32[]{:S(2)}) collective-permute-start(f32[2,2,128,128]{3,2,1,0:T(8,128)S(1)} %get-tuple-element.62), channel_id=1, source_target_pairs={{0,4},{4,0},{8,12},{12,8},{1,5},{5,1},{9,13},{13,9},{2,6},{6,2},{1... | collective-permute-start | bytes 786440 | tf_op jit(solution)/shard_map/ppermute | solution.py:309
  68.4 13.1 %collective-permute-start.12 = (f32[64,512]{1,0:T(8,128)S(1)}, f32[64,512]{1,0:T(8,128)S(1)}, u32[]{:S(2)}, u32[]{:S(2)}) collective-permute-start(f32[64,512]{1,0:T(8,128)S(1)} %probe_total.1.refs_0_), channel_id=1, source_target_pairs={{0,8},{4,12},{8,0},{12,4},{1,9},{5,13},{9,1},{13,5},{2,10},{6,14},... | collective-permute-start | bytes 393224 | tf_op jit(solution)/shard_map/ppermute | solution.py:499
  69.3 12.2 %collective-permute-start.17 = (f32[64,512]{1,0:T(8,128)S(1)}, f32[64,512]{1,0:T(8,128)S(1)}, u32[]{:S(2)}, u32[]{:S(2)}) collective-permute-start(f32[64,512]{1,0:T(8,128)S(1)} %probe_total.1.refs_0_), channel_id=1, source_target_pairs={{0,12},{4,8},{8,4},{12,0},{1,13},{5,9},{9,5},{13,1},{2,14},{6,10},... | collective-permute-start | bytes 393224 | tf_op jit(solution)/shard_map/ppermute | solution.py:499
  71.9 10.0 %collective-permute-start.16 = (f32[64,512]{1,0:T(8,128)S(1)}, f32[64,512]{1,0:T(8,128)S(1)}, u32[]{:S(2)}, u32[]{:S(2)}) collective-permute-start(f32[64,512]{1,0:T(8,128)S(1)} %probe_total.1.refs_0_), channel_id=1, source_target_pairs={{0,4},{4,0},{8,12},{12,8},{1,5},{5,1},{9,13},{13,9},{2,6},{6,2},{1... | collective-permute-start | bytes 393224 | tf_op jit(solution)/shard_map/ppermute | solution.py:499
  77.6 4.8 %collective-permute-start.18 = (f32[64,512]{1,0:T(8,128)S(1)}, f32[64,512]{1,0:T(8,128)S(1)}, u32[]{:S(2)}, u32[]{:S(2)}) collective-permute-start(f32[64,512]{1,0:T(8,128)S(1)} %probe_total.1.refs_0_), channel_id=1, source_target_pairs={{0,1},{1,0},{2,3},{3,2},{4,5},{5,4},{6,7},{7,6},{8,9},{9,8},{10,11... | collective-permute-start | bytes 393224 | tf_op jit(solution)/shard_map/ppermute | solution.py:315
  81.5 1.3 %collective-permute-start.21 = (f32[64,512]{1,0:T(8,128)S(1)}, f32[64,512]{1,0:T(8,128)S(1)}, u32[]{:S(2)}, u32[]{:S(2)}) collective-permute-start(f32[64,512]{1,0:T(8,128)S(1)} %collective-permute-done.17.refs_3_), channel_id=1, source_target_pairs={{0,1},{1,0},{2,3},{3,2},{4,5},{5,4},{6,7},{7,6},{8,9},{9,8},{10,11... | collective-permute-start | bytes 393224 | tf_op jit(solution)/shard_map/ppermute | solution.py:315
  81.9 1.3 %collective-permute-start.19 = (f32[64,512]{1,0:T(8,128)S(1)}, f32[64,512]{1,0:T(8,128)S(1)}, u32[]{:S(2)}, u32[]{:S(2)}) collective-permute-start(f32[64,512]{1,0:T(8,128)S(1)} %collective-permute-done.16.refs_1_), channel_id=1, source_target_pairs={{0,1},{1,0},{2,3},{3,2},{4,5},{5,4},{6,7},{7,6},{8,9},{9,8},{10,11... | collective-permute-start | bytes 393224 | tf_op jit(solution)/shard_map/ppermute | solution.py:315
  82.0 1.5 %collective-permute-start.20 = (f32[64,512]{1,0:T(8,128)S(1)}, f32[64,512]{1,0:T(8,128)S(1)}, u32[]{:S(2)}, u32[]{:S(2)}) collective-permute-start(f32[64,512]{1,0:T(8,128)S(1)} %collective-permute-done.12.refs_2_), channel_id=1, source_target_pairs={{0,1},{1,0},{2,3},{3,2},{4,5},{5,4},{6,7},{7,6},{8,9},{9,8},{10,11... | collective-permute-start | bytes 393224 | tf_op jit(solution)/shard_map/ppermute | solution.py:315
  (3 other events, 42.5 us)

commit v6 on v5

--- a/solution.py
+++ b/solution.py
@@ -11,7 +11,7 @@
 from jax.sharding import PartitionSpec as P
 
 LANES = 128
-CHUNK = 64
+CHUNK = 16
 
 
 def dft_tables(size):

time: 86.1 us -> 85.7 us (level)
  waiting for transfers between devices: 33.3 us -> 36.2 us
  starting transfers between devices: 27.8 us -> 25.5 us
    ppermute x4, waiting for transfers between devices: 12.2 us -> 15.4 us  [with_neighbours(): lax.ppermute(cells, 'tiles', [x for a, b in pairs[turn::2] for x in ((a,...]
    ppermute x3, starting transfers between devices: 4.51 us -> 1.48 us  [rotated(): lax.ppermute(cells, axis, [(i, (i + step) % count) for i in range(count)])]
    ppermute x4, starting transfers between devices: 8.12 us -> 10.6 us  [with_neighbours(): lax.ppermute(cells, 'tiles', [x for a, b in pairs[turn::2] for x in ((a,...]
    ppermute x6, starting transfers between devices: 14 us -> 12.2 us  [rotate_strips(): lax.ppermute(x, 'tiles', [(i, i ^ step + 1) for i in range(tiles)])]
    ppermute x6, waiting for transfers between devices: 13.3 us -> 12.1 us  [rotate_strips(): lax.ppermute(x, 'tiles', [(i, i ^ step + 1) for i in range(tiles)])]
where the time goes in v6:
time: 85.7 us; the launch traced here: 85.9 us
  waiting for transfers between devices  36.2 us (42%)
  starting transfers between devices  25.5 us (30%)
  Pallas kernels  19.3 us (23%)
  local copies, waits for them, and re-layouts  3.23 us (4%)
  between operations  1.52 us (2%)
    ppermute x4, waiting for transfers between devices, with_neighbours(): lax.ppermute(cells, 'tiles', [x for a, b in pairs[turn::2] for x in ((a,...  15.4 us
    pallas_call x1, Pallas kernels, point_sums(): pl.pallas_call(functools.partial(point_kernel, owners=owners), out_shape=...  14.6 us
    ppermute x6, starting transfers between devices, rotate_strips(): lax.ppermute(x, 'tiles', [(i, i ^ step + 1) for i in range(tiles)])  12.2 us
    ppermute x6, waiting for transfers between devices, rotate_strips(): lax.ppermute(x, 'tiles', [(i, i ^ step + 1) for i in range(tiles)])  12.1 us
    ppermute x4, starting transfers between devices, with_neighbours(): lax.ppermute(cells, 'tiles', [x for a, b in pairs[turn::2] for x in ((a,...  10.6 us
    ppermute x9, waiting for transfers between devices, swap(): return lax.ppermute(cells, 'modes', [(0, 1), (1, 0)])  4.77 us
    ppermute x3, waiting for transfers between devices, rotated(): lax.ppermute(cells, axis, [(i, (i + step) % count) for i in range(count)])  3.95 us
    pallas_call x8, Pallas kernels, small_kernel(): pl.pallas_call(body, out_shape=out_shape, in_specs=[pl.BlockSpec(memory_s...  3.15 us
  transfers between devices with their start and end apart: 22, of which 12 were waited for; matrix products, arithmetic and copies ran while one was open for 0% of the time, Pallas kernels for 4%

profile of v6, /device:TPU:0, one launch (start us, length us, event | category | flops | bytes accessed | tf_op | source)
XLA Modules:
  0.0 85.9 jit_solution(13079507063750416526)
XLA Ops:
  0.7 1.4 %dynamic-slice_bitcast_fusion = (f32[128,1024]{1,0:T(8,128)S(1)}, f32[128,1024]{1,0:T(8,128)S(1)}) fusion(f32[2,256,1024]{2,1,0:T(8,128)} %own.1, s32[]{:T(128)S(6)} %select_n.20, s32[]{:T(128)S(6)} %select_n.23, s32[]{:T(128)S(6)} %select_n.22), kind=kLoop, calls=%fused_computation | loop fusion | bytes 2097164 | tf_op jit(solution)/shard_map/squeeze | solution.py:463
  2.1 0.7 collective-permute-start.1
  2.8 5.9 %collective-permute-start = (f32[128,1024]{1,0:T(8,128)S(1)}, f32[128,1024]{1,0:T(8,128)S(1)}, u32[]{:S(2)}, u32[]{:S(2)}) collective-permute-start(f32[128,1024]{1,0:T(8,128)S(1)} %get-tuple-element.67), channel_id=1, source_target_pairs={{0,4},{4,0},{8,12},{12,8},{1,5},{5,1},{9,13},{13,9},{2,6},{6,2},{1... | collective-permute-start | bytes 1572872 | tf_op jit(solution)/shard_map/ppermute | solution.py:309
  8.7 11.6 %collective-permute-done.first_a = f32[128,1024]{1,0:T(8,128)S(1)} collective-permute-done((f32[128,1024]{1,0:T(8,128)S(1)}, f32[128,1024]{1,0:T(8,128)S(1)}, u32[]{:S(2)}, u32[]{:S(2)}) %collective-permute-start) | collective-permute-done | bytes 524320 | tf_op jit(solution)/shard_map/ppermute | solution.py:309
  21.5 0.9 collective-permute-done.2.first_b
  22.4 1.6 %copy-done.2 = f32[2,256,1024]{2,1,0:T(8,128)S(1)} copy-done((f32[2,256,1024]{2,1,0:T(8,128)S(1)}, f32[2,256,1024]{2,1,0:T(8,128)}, u32[]{:S(2)}) %copy-start.2) | copy-done | bytes 2097176
  24.0 14.6 %point_sums.1 = (f32[2,2,512,128]{3,2,1,0:T(8,128)S(1)}, f32[2,2,512,128]{3,2,1,0:T(8,128)S(1)}, f32[2,2,512,128]{3,2,1,0:T(8,128)S(1)}, f32[2,2,512,128]{3,2,1,...) custom-call(s32[3]{0:T(128)S(1)} %pad_add_fusion.place, s32[1]{0:T(128)S(6)} %copy.10.counts, ...), custom_call_target="tpu_custom_call" | custom-call | flops 8589934592 | bytes 16777216 | tf_op jit(solution)/shard_map/point_sums/pallas_call | solution.py:282
  39.3 2.8 %collective-permute-done.5.got = f32[256,512]{1,0:T(8,128)S(1)} collective-permute-done((f32[256,512]{1,0:T(8,128)S(1)}, f32[256,512]{1,0:T(8,128)S(1)}, u32[]{:S(2)}, u32[]{:S(2)}) %collective-permute-start.5) | collective-permute-done | bytes 524320 | tf_op jit(solution)/shard_map/ppermute | solution.py:315
  42.9 3.5 %collective-permute-start.6 = (f32[64,512]{1,0:T(8,128)S(1)}, f32[64,512]{1,0:T(8,128)S(1)}, u32[]{:S(2)}, u32[]{:S(2)}) collective-permute-start(f32[64,512]{1,0:T(8,128)S(1)} %get-tuple-element.46), channel_id=1, source_target_pairs={{0,4},{4,0},{8,12},{12,8},{1,5},{5,1},{9,13},{13,9},{2,6},{6,2},{1... | collective-permute-start | bytes 393224 | tf_op jit(solution)/shard_map/ppermute | solution.py:499
  46.4 2.4 %collective-permute-start.8 = (f32[64,512]{1,0:T(8,128)S(1)}, f32[64,512]{1,0:T(8,128)S(1)}, u32[]{:S(2)}, u32[]{:S(2)}) collective-permute-start(f32[64,512]{1,0:T(8,128)S(1)} %get-tuple-element.48), channel_id=1, source_target_pairs={{0,12},{4,8},{8,4},{12,0},{1,13},{5,9},{9,5},{13,1},{2,14},{6,10},... | collective-permute-start | bytes 393224 | tf_op jit(solution)/shard_map/ppermute | solution.py:499
  48.7 1.5 %collective-permute-done.6.refs_1_ = f32[64,512]{1,0:T(8,128)S(1)} collective-permute-done((f32[64,512]{1,0:T(8,128)S(1)}, f32[64,512]{1,0:T(8,128)S(1)}, u32[]{:S(2)}, u32[]{:S(2)}) %collective-permute-start.6) | collective-permute-done | bytes 131104 | tf_op jit(solution)/shard_map/ppermute | solution.py:499
  50.3 7.6 %collective-permute-done.7.refs_2_ = f32[64,512]{1,0:T(8,128)S(1)} collective-permute-done((f32[64,512]{1,0:T(8,128)S(1)}, f32[64,512]{1,0:T(8,128)S(1)}, u32[]{:S(2)}, u32[]{:S(2)}) %collective-permute-start.7) | collective-permute-done | bytes 131104 | tf_op jit(solution)/shard_map/ppermute | solution.py:499
  58.0 0.7 object_mine.1
  58.7 0.7 collective-permute-start.11
  59.4 0.7 collective-permute-start.13
  60.1 3.9 %collective-permute-done.11.refs_1_ = f32[64,512]{1,0:T(8,128)S(1)} collective-permute-done((f32[64,512]{1,0:T(8,128)S(1)}, f32[64,512]{1,0:T(8,128)S(1)}, u32[]{:S(2)}, u32[]{:S(2)}) %collective-permute-start.11) | collective-permute-done | bytes 131104 | tf_op jit(solution)/shard_map/ppermute | solution.py:320
  64.0 0.7 collective-permute-start.15
  64.7 3.4 %collective-permute-start.14 = (f32[2,2,128,128]{3,2,1,0:T(8,128)S(1)}, f32[2,2,128,128]{3,2,1,0:T(8,128)S(1)}, u32[]{:S(2)}, u32[]{:S(2)}) collective-permute-start(f32[2,2,128,128]{3,2,1,0:T(8,128)S(1)} %get-tuple-element.62), channel_id=1, source_target_pairs={{0,4},{4,0},{8,12},{12,8},{1,5},{5,1},{9,13},{13,9},{2,6},{6,2},{1... | collective-permute-start | bytes 786440 | tf_op jit(solution)/shard_map/ppermute | solution.py:309
  68.1 2.4 %collective-permute-start.17 = (f32[64,512]{1,0:T(8,128)S(1)}, f32[64,512]{1,0:T(8,128)S(1)}, u32[]{:S(2)}, u32[]{:S(2)}) collective-permute-start(f32[64,512]{1,0:T(8,128)S(1)} %probe_total.1.refs_0_), channel_id=1, source_target_pairs={{0,12},{4,8},{8,4},{12,0},{1,13},{5,9},{9,5},{13,1},{2,14},{6,10},... | collective-permute-start | bytes 393224 | tf_op jit(solution)/shard_map/ppermute | solution.py:499
  70.5 4.0 %collective-permute-start.16 = (f32[64,512]{1,0:T(8,128)S(1)}, f32[64,512]{1,0:T(8,128)S(1)}, u32[]{:S(2)}, u32[]{:S(2)}) collective-permute-start(f32[64,512]{1,0:T(8,128)S(1)} %probe_total.1.refs_0_), channel_id=1, source_target_pairs={{0,4},{4,0},{8,12},{12,8},{1,5},{5,1},{9,13},{13,9},{2,6},{6,2},{1... | collective-permute-start | bytes 393224 | tf_op jit(solution)/shard_map/ppermute | solution.py:499
  74.5 3.8 %collective-permute-done.14.first = f32[2,2,128,128]{3,2,1,0:T(8,128)S(1)} collective-permute-done((f32[2,2,128,128]{3,2,1,0:T(8,128)S(1)}, f32[2,2,128,128]{3,2,1,0:T(8,128)S(1)}, u32[]{:S(2)}, u32[]{:S(2)}) %collective-permute-start.14) | collective-permute-done | bytes 262176 | tf_op jit(solution)/shard_map/ppermute | solution.py:309
  78.9 2.7 %collective-permute-done.12.refs_2_ = f32[64,512]{1,0:T(8,128)S(1)} collective-permute-done((f32[64,512]{1,0:T(8,128)S(1)}, f32[64,512]{1,0:T(8,128)S(1)}, u32[]{:S(2)}, u32[]{:S(2)}) %collective-permute-start.12) | collective-permute-done | bytes 131104 | tf_op jit(solution)/shard_map/ppermute | solution.py:499
  83.4 1.6 %probe_gather.1 = f32[2,256,512]{2,1,0:T(8,128)} custom-call(s32[3]{0:T(128)S(1)} %pad_add_fusion.place, f32[64,512]{1,0:T(8,128)S(1)} %probe_total.1.refs_0_, f32[64,512]{1,0:T(8,128)S(1)} %collective-permute-done.16.refs_1_, f32[64,512]{1,0:T(8,128)S(1)} %collective-permute-done.12.refs_2_, f32[64,512]{1,0:T(8,128)S(1)} %collective-permute-done.17.refs_3_, ...), custom_call_target="tpu_custom_call" | custom-call | tf_op jit(solution)/shard_map/probe_gather/pallas_call | solution.py:436
  85.0 0.8 object_finish.1
  (44 shorter events, 4.5 us)
Async XLA Ops:
  0.6 20.6 %copy-start.3 = (bf16[512,256]{1,0:T(8,128)(2,1)S(1)}, bf16[512,256]{1,0:T(8,128)(2,1)}, u32[]{:S(2)}) copy-start(bf16[512,256]{1,0:T(8,128)(2,1)} %constant.32.clone.table) | copy-start | bytes 786436
  0.7 20.6 %copy-start = (bf16[1,8,256,256]{3,2,1,0:T(8,128)(2,1)S(1)}, bf16[1,8,256,256]{3,2,1,0:T(8,128)(2,1)}, u32[]{:S(2)}) copy-start(bf16[1,8,256,256]{3,2,1,0:T(8,128)(2,1)} %param.8) | copy-start | bytes 3145732
  2.1 6.6 %collective-permute-start.1 = (f32[128,1024]{1,0:T(8,128)S(1)}, f32[128,1024]{1,0:T(8,128)S(1)}, u32[]{:S(2)}, u32[]{:S(2)}) collective-permute-start(f32[128,1024]{1,0:T(8,128)S(1)} %get-tuple-element.66), channel_id=1, source_target_pairs={{4,8},{8,4},{5,9},{9,5},{6,10},{10,6},{7,11},{11,7},{20,24},{24,20... | collective-permute-start | bytes 1572872 | tf_op jit(solution)/shard_map/ppermute | solution.py:309
  2.8 17.5 %collective-permute-start = (f32[128,1024]{1,0:T(8,128)S(1)}, f32[128,1024]{1,0:T(8,128)S(1)}, u32[]{:S(2)}, u32[]{:S(2)}) collective-permute-start(f32[128,1024]{1,0:T(8,128)S(1)} %get-tuple-element.67), channel_id=1, source_target_pairs={{0,4},{4,0},{8,12},{12,8},{1,5},{5,1},{9,13},{13,9},{2,6},{6,2},{1... | collective-permute-start | bytes 1572872 | tf_op jit(solution)/shard_map/ppermute | solution.py:309
  8.7 12.8 %collective-permute-start.3 = (f32[128,1024]{1,0:T(8,128)S(1)}, f32[128,1024]{1,0:T(8,128)S(1)}, u32[]{:S(2)}, u32[]{:S(2)}) collective-permute-start(f32[128,1024]{1,0:T(8,128)S(1)} %collective-permute-done.1.second_a), channel_id=1, source_target_pairs={{0,1},{1,0},{2,3},{3,2},{4,5},{5,4},{6,7},{7,6},{8,9},{9,8},{10,11... | collective-permute-start | bytes 1572872 | tf_op jit(solution)/shard_map/ppermute | solution.py:315
  20.4 2.0 %collective-permute-start.2 = (f32[128,1024]{1,0:T(8,128)S(1)}, f32[128,1024]{1,0:T(8,128)}, u32[]{:S(2)}, u32[]{:S(2)}) collective-permute-start(f32[128,1024]{1,0:T(8,128)S(1)} %collective-permute-done.first_a), channel_id=1, source_target_pairs={{0,1},{1,0},{2,3},{3,2},{4,5},{5,4},{6,7},{7,6},{8,9},{9,8},{10,11... | collective-permute-start | bytes 1572872 | tf_op jit(solution)/shard_map/ppermute | solution.py:315
  38.6 4.1 %collective-permute-start.4 = (f32[2,2,512,128]{3,2,1,0:T(8,128)S(1)}, f32[2,2,512,128]{3,2,1,0:T(8,128)S(1)}, u32[]{:S(2)}, u32[]{:S(2)}) collective-permute-start(f32[2,2,512,128]{3,2,1,0:T(8,128)S(1)} %get-tuple-element.38), channel_id=1, source_target_pairs={{0,1},{1,0},{2,3},{3,2},{4,5},{5,4},{6,7},{7,6},{8,9},{9,8},{10,11... | collective-permute-start | bytes 3145736 | tf_op jit(solution)/shard_map/ppermute | solution.py:315
  38.7 3.4 %collective-permute-start.5 = (f32[256,512]{1,0:T(8,128)S(1)}, f32[256,512]{1,0:T(8,128)S(1)}, u32[]{:S(2)}, u32[]{:S(2)}) collective-permute-start(f32[256,512]{1,0:T(8,128)S(1)} %get-tuple-element.40), channel_id=1, source_target_pairs={{0,1},{1,0},{2,3},{3,2},{4,5},{5,4},{6,7},{7,6},{8,9},{9,8},{10,11... | collective-permute-start | bytes 1572872 | tf_op jit(solution)/shard_map/ppermute | solution.py:315
  39.2 18.7 %collective-permute-start.9 = (f32[2,2,512,128]{3,2,1,0:T(8,128)S(1)}, f32[2,2,512,128]{3,2,1,0:T(8,128)S(1)}, u32[]{:S(2)}, u32[]{:S(2)}) collective-permute-start(f32[2,2,512,128]{3,2,1,0:T(8,128)S(1)} %get-tuple-element.50), channel_id=1, source_target_pairs={{0,1},{1,0},{2,3},{3,2},{4,5},{5,4},{6,7},{7,6},{8,9},{9,8},{10,11... | collective-permute-start | bytes 3145736 | tf_op jit(solution)/shard_map/ppermute | solution.py:315
  42.8 15.1 %collective-permute-start.10 = (f32[2,2,256,128]{3,2,1,0:T(8,128)S(1)}, f32[2,2,256,128]{3,2,1,0:T(8,128)S(1)}, u32[]{:S(2)}, u32[]{:S(2)}) collective-permute-start(f32[2,2,256,128]{3,2,1,0:T(8,128)S(1)} %get-tuple-element.53), channel_id=1, source_target_pairs={{0,2},{2,0},{1,3},{3,1},{4,6},{6,4},{5,7},{7,5},{8,10},{10,8},{9,1... | collective-permute-start | bytes 1572872 | tf_op jit(solution)/shard_map/ppermute | solution.py:320
  42.9 7.4 %collective-permute-start.6 = (f32[64,512]{1,0:T(8,128)S(1)}, f32[64,512]{1,0:T(8,128)S(1)}, u32[]{:S(2)}, u32[]{:S(2)}) collective-permute-start(f32[64,512]{1,0:T(8,128)S(1)} %get-tuple-element.46), channel_id=1, source_target_pairs={{0,4},{4,0},{8,12},{12,8},{1,5},{5,1},{9,13},{13,9},{2,6},{6,2},{1... | collective-permute-start | bytes 393224 | tf_op jit(solution)/shard_map/ppermute | solution.py:499
  46.4 11.5 %collective-permute-start.7 = (f32[64,512]{1,0:T(8,128)S(1)}, f32[64,512]{1,0:T(8,128)S(1)}, u32[]{:S(2)}, u32[]{:S(2)}) collective-permute-start(f32[64,512]{1,0:T(8,128)S(1)} %get-tuple-element.47), channel_id=1, source_target_pairs={{0,8},{4,12},{8,0},{12,4},{1,9},{5,13},{9,1},{13,5},{2,10},{6,14},... | collective-permute-start | bytes 393224 | tf_op jit(solution)/shard_map/ppermute | solution.py:499
  46.4 11.5 %collective-permute-start.8 = (f32[64,512]{1,0:T(8,128)S(1)}, f32[64,512]{1,0:T(8,128)S(1)}, u32[]{:S(2)}, u32[]{:S(2)}) collective-permute-start(f32[64,512]{1,0:T(8,128)S(1)} %get-tuple-element.48), channel_id=1, source_target_pairs={{0,12},{4,8},{8,4},{12,0},{1,13},{5,9},{9,5},{13,1},{2,14},{6,10},... | collective-permute-start | bytes 393224 | tf_op jit(solution)/shard_map/ppermute | solution.py:499
  58.7 5.3 %collective-permute-start.11 = (f32[64,512]{1,0:T(8,128)S(1)}, f32[64,512]{1,0:T(8,128)S(1)}, u32[]{:S(2)}, u32[]{:S(2)}) collective-permute-start(f32[64,512]{1,0:T(8,128)S(1)} %probe_strips_sum.1.refs_0_), channel_id=1, source_target_pairs={{0,2},{2,0},{1,3},{3,1},{4,6},{6,4},{5,7},{7,5},{8,10},{10,8},{9,1... | collective-permute-start | bytes 393224 | tf_op jit(solution)/shard_map/ppermute | solution.py:320
  59.4 11.1 %collective-permute-start.13 = (f32[2,2,128,128]{3,2,1,0:T(8,128)S(1)}, f32[2,2,128,128]{3,2,1,0:T(8,128)S(1)}, u32[]{:S(2)}, u32[]{:S(2)}) collective-permute-start(f32[2,2,128,128]{3,2,1,0:T(8,128)S(1)} %get-tuple-element.61), channel_id=1, source_target_pairs={{4,8},{8,4},{5,9},{9,5},{6,10},{10,6},{7,11},{11,7},{20,24},{24,20... | collective-permute-start | bytes 786440 | tf_op jit(solution)/shard_map/ppermute | solution.py:309
  64.0 21.0 %collective-permute-start.15 = (f32[2,2,256,128]{3,2,1,0:T(8,128)S(1)}, f32[2,2,256,128]{3,2,1,0:T(8,128)S(1)}, u32[]{:S(2)}, u32[]{:S(2)}) collective-permute-start(f32[2,2,256,128]{3,2,1,0:T(8,128)S(1)} %get-tuple-element.64), channel_id=1, source_target_pairs={{0,2},{2,0},{1,3},{3,1},{4,6},{6,4},{5,7},{7,5},{8,10},{10,8},{9,1... | collective-permute-start | bytes 1572872 | tf_op jit(solution)/shard_map/ppermute | solution.py:320
  64.7 13.5 %collective-permute-start.14 = (f32[2,2,128,128]{3,2,1,0:T(8,128)S(1)}, f32[2,2,128,128]{3,2,1,0:T(8,128)S(1)}, u32[]{:S(2)}, u32[]{:S(2)}) collective-permute-start(f32[2,2,128,128]{3,2,1,0:T(8,128)S(1)} %get-tuple-element.62), channel_id=1, source_target_pairs={{0,4},{4,0},{8,12},{12,8},{1,5},{5,1},{9,13},{13,9},{2,6},{6,2},{1... | collective-permute-start | bytes 786440 | tf_op jit(solution)/shard_map/ppermute | solution.py:309
  68.1 13.5 %collective-permute-start.12 = (f32[64,512]{1,0:T(8,128)S(1)}, f32[64,512]{1,0:T(8,128)S(1)}, u32[]{:S(2)}, u32[]{:S(2)}) collective-permute-start(f32[64,512]{1,0:T(8,128)S(1)} %probe_total.1.refs_0_), channel_id=1, source_target_pairs={{0,8},{4,12},{8,0},{12,4},{1,9},{5,13},{9,1},{13,5},{2,10},{6,14},... | collective-permute-start | bytes 393224 | tf_op jit(solution)/shard_map/ppermute | solution.py:499
  68.1 13.5 %collective-permute-start.17 = (f32[64,512]{1,0:T(8,128)S(1)}, f32[64,512]{1,0:T(8,128)S(1)}, u32[]{:S(2)}, u32[]{:S(2)}) collective-permute-start(f32[64,512]{1,0:T(8,128)S(1)} %probe_total.1.refs_0_), channel_id=1, source_target_pairs={{0,12},{4,8},{8,4},{12,0},{1,13},{5,9},{9,5},{13,1},{2,14},{6,10},... | collective-permute-start | bytes 393224 | tf_op jit(solution)/shard_map/ppermute | solution.py:499
  70.5 11.4 %collective-permute-start.16 = (f32[64,512]{1,0:T(8,128)S(1)}, f32[64,512]{1,0:T(8,128)S(1)}, u32[]{:S(2)}, u32[]{:S(2)}) collective-permute-start(f32[64,512]{1,0:T(8,128)S(1)} %probe_total.1.refs_0_), channel_id=1, source_target_pairs={{0,4},{4,0},{8,12},{12,8},{1,5},{5,1},{9,13},{13,9},{2,6},{6,2},{1... | collective-permute-start | bytes 393224 | tf_op jit(solution)/shard_map/ppermute | solution.py:499
  78.3 4.1 %collective-permute-start.18 = (f32[64,512]{1,0:T(8,128)S(1)}, f32[64,512]{1,0:T(8,128)S(1)}, u32[]{:S(2)}, u32[]{:S(2)}) collective-permute-start(f32[64,512]{1,0:T(8,128)S(1)} %probe_total.1.refs_0_), channel_id=1, source_target_pairs={{0,1},{1,0},{2,3},{3,2},{4,5},{5,4},{6,7},{7,6},{8,9},{9,8},{10,11... | collective-permute-start | bytes 393224 | tf_op jit(solution)/shard_map/ppermute | solution.py:315
  81.6 1.3 %collective-permute-start.21 = (f32[64,512]{1,0:T(8,128)S(1)}, f32[64,512]{1,0:T(8,128)S(1)}, u32[]{:S(2)}, u32[]{:S(2)}) collective-permute-start(f32[64,512]{1,0:T(8,128)S(1)} %collective-permute-done.17.refs_3_), channel_id=1, source_target_pairs={{0,1},{1,0},{2,3},{3,2},{4,5},{5,4},{6,7},{7,6},{8,9},{9,8},{10,11... | collective-permute-start | bytes 393224 | tf_op jit(solution)/shard_map/ppermute | solution.py:315
  81.8 1.3 %collective-permute-start.19 = (f32[64,512]{1,0:T(8,128)S(1)}, f32[64,512]{1,0:T(8,128)S(1)}, u32[]{:S(2)}, u32[]{:S(2)}) collective-permute-start(f32[64,512]{1,0:T(8,128)S(1)} %collective-permute-done.16.refs_1_), channel_id=1, source_target_pairs={{0,1},{1,0},{2,3},{3,2},{4,5},{5,4},{6,7},{7,6},{8,9},{9,8},{10,11... | collective-permute-start | bytes 393224 | tf_op jit(solution)/shard_map/ppermute | solution.py:315
  82.1 1.3 %collective-permute-start.20 = (f32[64,512]{1,0:T(8,128)S(1)}, f32[64,512]{1,0:T(8,128)S(1)}, u32[]{:S(2)}, u32[]{:S(2)}) collective-permute-start(f32[64,512]{1,0:T(8,128)S(1)} %collective-permute-done.12.refs_2_), channel_id=1, source_target_pairs={{0,1},{1,0},{2,3},{3,2},{4,5},{5,4},{6,7},{7,6},{8,9},{9,8},{10,11... | collective-permute-start | bytes 393224 | tf_op jit(solution)/shard_map/ppermute | solution.py:315
  (3 other events, 42.5 us)

commit v7 on v6

--- a/solution.py
+++ b/solution.py
@@ -413,6 +413,47 @@
         out[...] = kept[rows] + got[rows]
 
 
+def end_kernel(place, *refs, others, tiles):
+    folded, *core_in = refs[: 1 + others]
+    parts = refs[1 + others : 1 + others + 2 * tiles]
+    object_out, probe_out, whole, sems = refs[1 + others + 2 * tiles :]
+    share = parts[0].shape[0]
+    copies = []
+    for index, part in enumerate(parts):
+        swapped, step = divmod(index, tiles)
+        mode = place[2] if swapped == 0 else 1 - place[2]
+        target = probe_out.at[mode, share_rows(place[0] ^ step, share)]
+        copies.append(pltpu.make_async_copy(part, target, sems.at[index]))
+    for copy in copies:
+        copy.start()
+    finish_kernel(folded, *core_in, whole)
+    copies.append(pltpu.make_async_copy(whole, object_out, sems.at[len(parts)]))
+    copies[-1].start()
+    for copy in copies:
+        copy.wait()
+
+
+def end_sums(place, folded, core_in, parts):
+    width, planes, rows, lanes = folded.shape
+    share, probe_cols = parts[0].shape
+    tiles = len(parts) // 2
+    grad = (planes, rows, width * lanes)
+    args = [folded, *core_in, *parts]
+    return pl.pallas_call(
+        functools.partial(end_kernel, others=len(core_in), tiles=tiles),
+        out_shape=[shape(*grad), shape(2, tiles * share, probe_cols)],
+        in_specs=[pl.BlockSpec(memory_space=pltpu.SMEM)]
+        + [pl.BlockSpec(memory_space=pltpu.VMEM)] * len(args),
+        out_specs=[pl.BlockSpec(memory_space=pl.ANY)] * 2,
+        scratch_shapes=[
+            pltpu.VMEM(grad, jnp.float32),
+            pltpu.SemaphoreType.DMA((len(parts) + 1,)),
+        ],
+        compiler_params=pltpu.CompilerParams(vmem_limit_bytes=4 * 1024 * 1024),
+        name="end_sums",
+    )(place, *args)
+
+
 def gather_kernel(place, *refs):
     out, sems = refs[-2:]
     parts = refs[:-2]
@@ -528,6 +569,9 @@
     if direct:
         parts_in[1], folded = lax.optimization_barrier((parts_in[1], folded))
     core_in = rotate_all(core_out)
+    if direct:
+        parts = [part_sum, *parts_in]
+        return tuple(end_sums(place, folded, core_in, [*parts, *[swap(x) for x in parts]]))
     object_grad = small_kernel(
         finish_kernel,
         shape(2, strip_rows, width * LANES),
@@ -535,11 +579,8 @@
         *core_in,
         name="object_finish",
     )
-    if direct:
-        parts = [part_sum, *parts_in]
-    else:
-        parts = [lax.psum(keep_probe + got_probe, ("tiles", "sub"))]
-    spot = place if direct else place * jnp.array([0, 0, 1], jnp.int32)
+    parts = [lax.psum(keep_probe + got_probe, ("tiles", "sub"))]
+    spot = place * jnp.array([0, 0, 1], jnp.int32)
     probe_grad = gather_parts(spot, [*parts, *[swap(x) for x in parts]])
     return (object_grad, probe_grad)
 

time: 85.7 us -> 84.7 us (0.988)
  waiting for transfers between devices: 36.2 us -> 32.2 us
  starting transfers between devices: 25.5 us -> 28.6 us
    ppermute x3, starting transfers between devices: 1.48 us -> 5.86 us  [rotated(): lax.ppermute(cells, axis, [(i, (i + step) % count) for i in range(count)])]
    ppermute x4, waiting for transfers between devices: 15.4 us -> 12.5 us  [with_neighbours(): lax.ppermute(cells, 'tiles', [x for a, b in pairs[turn::2] for x in ((a,...]
    ppermute x4, starting transfers between devices: 10.6 us -> 8.85 us  [with_neighbours(): lax.ppermute(cells, 'tiles', [x for a, b in pairs[turn::2] for x in ((a,...]
    ppermute x3, waiting for transfers between devices: 3.95 us -> 2.49 us  [rotated(): lax.ppermute(cells, axis, [(i, (i + step) % count) for i in range(count)])]
    pallas_call x8 -> x7, Pallas kernels: 3.15 us -> 2.3 us  [small_kernel(): pl.pallas_call(body, out_shape=out_shape, in_specs=[pl.BlockSpec(memory_s...]
  transfers between devices with their start and end apart: 22 -> 22, of which waited for: 12 -> 12; matrix products, arithmetic and copies ran while one was open for 0% -> 0% of each run, Pallas kernels for 4% -> 2%
where the time goes in v7:
time: 84.7 us; the launch traced here: 84.4 us
  waiting for transfers between devices  32.2 us (38%)
  starting transfers between devices  28.6 us (34%)
  Pallas kernels  18.8 us (22%)
  local copies, waits for them, and re-layouts  3.23 us (4%)
  between operations  1.49 us (2%)
    pallas_call x1, Pallas kernels, point_sums(): pl.pallas_call(functools.partial(point_kernel, owners=owners), out_shape=...  14.7 us
    ppermute x6, starting transfers between devices, rotate_strips(): lax.ppermute(x, 'tiles', [(i, i ^ step + 1) for i in range(tiles)])  12.7 us
    ppermute x4, waiting for transfers between devices, with_neighbours(): lax.ppermute(cells, 'tiles', [x for a, b in pairs[turn::2] for x in ((a,...  12.5 us
    ppermute x6, waiting for transfers between devices, rotate_strips(): lax.ppermute(x, 'tiles', [(i, i ^ step + 1) for i in range(tiles)])  12.5 us
    ppermute x4, starting transfers between devices, with_neighbours(): lax.ppermute(cells, 'tiles', [x for a, b in pairs[turn::2] for x in ((a,...  8.85 us
    ppermute x3, starting transfers between devices, rotated(): lax.ppermute(cells, axis, [(i, (i + step) % count) for i in range(count)])  5.86 us
    ppermute x9, waiting for transfers between devices, swap(): return lax.ppermute(cells, 'modes', [(0, 1), (1, 0)])  4.76 us
    ppermute x3, waiting for transfers between devices, rotated(): lax.ppermute(cells, axis, [(i, (i + step) % count) for i in range(count)])  2.49 us
  transfers between devices with their start and end apart: 22, of which 12 were waited for; matrix products, arithmetic and copies ran while one was open for 0% of the time, Pallas kernels for 2%

profile of v7, /device:TPU:0, one launch (start us, length us, event | category | flops | bytes accessed | tf_op | source)
XLA Modules:
  0.0 84.4 jit_solution(18436969593957859202)
XLA Ops:
  0.7 1.4 %dynamic-slice_bitcast_fusion = (f32[128,1024]{1,0:T(8,128)S(1)}, f32[128,1024]{1,0:T(8,128)S(1)}) fusion(f32[2,256,1024]{2,1,0:T(8,128)} %own.1, s32[]{:T(128)S(6)} %select_n.20, s32[]{:T(128)S(6)} %select_n.23, s32[]{:T(128)S(6)} %select_n.22), kind=kLoop, calls=%fused_computation | loop fusion | bytes 2097164 | tf_op jit(solution)/shard_map/squeeze | solution.py:504
  2.1 0.7 collective-permute-start.1
  2.8 5.9 %collective-permute-start = (f32[128,1024]{1,0:T(8,128)S(1)}, f32[128,1024]{1,0:T(8,128)S(1)}, u32[]{:S(2)}, u32[]{:S(2)}) collective-permute-start(f32[128,1024]{1,0:T(8,128)S(1)} %get-tuple-element.67), channel_id=1, source_target_pairs={{0,4},{4,0},{8,12},{12,8},{1,5},{5,1},{9,13},{13,9},{2,6},{6,2},{1... | collective-permute-start | bytes 1572872 | tf_op jit(solution)/shard_map/ppermute | solution.py:309
  8.7 11.6 %collective-permute-done.first_a = f32[128,1024]{1,0:T(8,128)S(1)} collective-permute-done((f32[128,1024]{1,0:T(8,128)S(1)}, f32[128,1024]{1,0:T(8,128)S(1)}, u32[]{:S(2)}, u32[]{:S(2)}) %collective-permute-start) | collective-permute-done | bytes 524320 | tf_op jit(solution)/shard_map/ppermute | solution.py:309
  21.5 0.9 %collective-permute-done.2.first_b = f32[128,1024]{1,0:T(8,128)} collective-permute-done((f32[128,1024]{1,0:T(8,128)S(1)}, f32[128,1024]{1,0:T(8,128)}, u32[]{:S(2)}, u32[]{:S(2)}) %collective-permute-start.2) | collective-permute-done | bytes 524320 | tf_op jit(solution)/shard_map/ppermute | solution.py:315
  22.4 1.6 %copy-done.2 = f32[2,256,1024]{2,1,0:T(8,128)S(1)} copy-done((f32[2,256,1024]{2,1,0:T(8,128)S(1)}, f32[2,256,1024]{2,1,0:T(8,128)}, u32[]{:S(2)}) %copy-start.2) | copy-done | bytes 2097176
  24.0 14.7 %point_sums.1 = (f32[2,2,512,128]{3,2,1,0:T(8,128)S(1)}, f32[2,2,512,128]{3,2,1,0:T(8,128)S(1)}, f32[2,2,512,128]{3,2,1,0:T(8,128)S(1)}, f32[2,2,512,128]{3,2,1,...) custom-call(s32[3]{0:T(128)S(1)} %pad_add_fusion.place, s32[1]{0:T(128)S(6)} %copy.10.counts, ...), custom_call_target="tpu_custom_call" | custom-call | flops 8589934592 | bytes 16777216 | tf_op jit(solution)/shard_map/point_sums/pallas_call | solution.py:282
  39.4 2.8 %collective-permute-done.5.got = f32[256,512]{1,0:T(8,128)S(1)} collective-permute-done((f32[256,512]{1,0:T(8,128)S(1)}, f32[256,512]{1,0:T(8,128)S(1)}, u32[]{:S(2)}, u32[]{:S(2)}) %collective-permute-start.5) | collective-permute-done | bytes 524320 | tf_op jit(solution)/shard_map/ppermute | solution.py:315
  42.9 1.5 %collective-permute-start.10 = (f32[2,2,256,128]{3,2,1,0:T(8,128)S(1)}, f32[2,2,256,128]{3,2,1,0:T(8,128)S(1)}, u32[]{:S(2)}, u32[]{:S(2)}) collective-permute-start(f32[2,2,256,128]{3,2,1,0:T(8,128)S(1)} %get-tuple-element.53), channel_id=1, source_target_pairs={{0,2},{2,0},{1,3},{3,1},{4,6},{6,4},{5,7},{7,5},{8,10},{10,8},{9,1... | collective-permute-start | bytes 1572872 | tf_op jit(solution)/shard_map/ppermute | solution.py:320
  45.0 1.9 %collective-permute-start.7 = (f32[64,512]{1,0:T(8,128)S(1)}, f32[64,512]{1,0:T(8,128)S(1)}, u32[]{:S(2)}, u32[]{:S(2)}) collective-permute-start(f32[64,512]{1,0:T(8,128)S(1)} %get-tuple-element.47), channel_id=1, source_target_pairs={{0,8},{4,12},{8,0},{12,4},{1,9},{5,13},{9,1},{13,5},{2,10},{6,14},... | collective-permute-start | bytes 393224 | tf_op jit(solution)/shard_map/ppermute | solution.py:540
  46.8 2.0 %collective-permute-start.8 = (f32[64,512]{1,0:T(8,128)S(1)}, f32[64,512]{1,0:T(8,128)S(1)}, u32[]{:S(2)}, u32[]{:S(2)}) collective-permute-start(f32[64,512]{1,0:T(8,128)S(1)} %get-tuple-element.48), channel_id=1, source_target_pairs={{0,12},{4,8},{8,4},{12,0},{1,13},{5,9},{9,5},{13,1},{2,14},{6,10},... | collective-permute-start | bytes 393224 | tf_op jit(solution)/shard_map/ppermute | solution.py:540
  48.8 3.2 %collective-permute-done.6.refs_1_ = f32[64,512]{1,0:T(8,128)S(1)} collective-permute-done((f32[64,512]{1,0:T(8,128)S(1)}, f32[64,512]{1,0:T(8,128)S(1)}, u32[]{:S(2)}, u32[]{:S(2)}) %collective-permute-start.6) | collective-permute-done | bytes 131104 | tf_op jit(solution)/shard_map/ppermute | solution.py:540
  52.0 5.8 %collective-permute-done.7.refs_2_ = f32[64,512]{1,0:T(8,128)S(1)} collective-permute-done((f32[64,512]{1,0:T(8,128)S(1)}, f32[64,512]{1,0:T(8,128)S(1)}, u32[]{:S(2)}, u32[]{:S(2)}) %collective-permute-start.7) | collective-permute-done | bytes 131104 | tf_op jit(solution)/shard_map/ppermute | solution.py:540
  57.9 0.7 object_mine.1
  58.6 1.9 %collective-permute-start.11 = (f32[64,512]{1,0:T(8,128)S(1)}, f32[64,512]{1,0:T(8,128)S(1)}, u32[]{:S(2)}, u32[]{:S(2)}) collective-permute-start(f32[64,512]{1,0:T(8,128)S(1)} %probe_strips_sum.1.refs_0_), channel_id=1, source_target_pairs={{0,2},{2,0},{1,3},{3,1},{4,6},{6,4},{5,7},{7,5},{8,10},{10,8},{9,1... | collective-permute-start | bytes 393224 | tf_op jit(solution)/shard_map/ppermute | solution.py:320
  61.2 2.5 %collective-permute-done.11.refs_1_ = f32[64,512]{1,0:T(8,128)S(1)} collective-permute-done((f32[64,512]{1,0:T(8,128)S(1)}, f32[64,512]{1,0:T(8,128)S(1)}, u32[]{:S(2)}, u32[]{:S(2)}) %collective-permute-start.11) | collective-permute-done | bytes 131104 | tf_op jit(solution)/shard_map/ppermute | solution.py:320
  63.7 2.4 %collective-permute-start.15 = (f32[2,2,256,128]{3,2,1,0:T(8,128)S(1)}, f32[2,2,256,128]{3,2,1,0:T(8,128)S(1)}, u32[]{:S(2)}, u32[]{:S(2)}) collective-permute-start(f32[2,2,256,128]{3,2,1,0:T(8,128)S(1)} %get-tuple-element.64), channel_id=1, source_target_pairs={{0,2},{2,0},{1,3},{3,1},{4,6},{6,4},{5,7},{7,5},{8,10},{10,8},{9,1... | collective-permute-start | bytes 1572872 | tf_op jit(solution)/shard_map/ppermute | solution.py:320
  66.1 1.6 %collective-permute-start.14 = (f32[2,2,128,128]{3,2,1,0:T(8,128)S(1)}, f32[2,2,128,128]{3,2,1,0:T(8,128)S(1)}, u32[]{:S(2)}, u32[]{:S(2)}) collective-permute-start(f32[2,2,128,128]{3,2,1,0:T(8,128)S(1)} %get-tuple-element.62), channel_id=1, source_target_pairs={{0,4},{4,0},{8,12},{12,8},{1,5},{5,1},{9,13},{13,9},{2,6},{6,2},{1... | collective-permute-start | bytes 786440 | tf_op jit(solution)/shard_map/ppermute | solution.py:309
  67.7 0.8 collective-permute-start.12
  68.6 1.9 %collective-permute-start.17 = (f32[64,512]{1,0:T(8,128)S(1)}, f32[64,512]{1,0:T(8,128)S(1)}, u32[]{:S(2)}, u32[]{:S(2)}) collective-permute-start(f32[64,512]{1,0:T(8,128)S(1)} %probe_total.1.refs_2_), channel_id=1, source_target_pairs={{0,12},{4,8},{8,4},{12,0},{1,13},{5,9},{9,5},{13,1},{2,14},{6,10},... | collective-permute-start | bytes 393224 | tf_op jit(solution)/shard_map/ppermute | solution.py:540
  70.5 5.6 %collective-permute-start.16 = (f32[64,512]{1,0:T(8,128)S(1)}, f32[64,512]{1,0:T(8,128)S(1)}, u32[]{:S(2)}, u32[]{:S(2)}) collective-permute-start(f32[64,512]{1,0:T(8,128)S(1)} %probe_total.1.refs_2_), channel_id=1, source_target_pairs={{0,4},{4,0},{8,12},{12,8},{1,5},{5,1},{9,13},{13,9},{2,6},{6,2},{1... | collective-permute-start | bytes 393224 | tf_op jit(solution)/shard_map/ppermute | solution.py:540
  76.1 0.8 collective-permute-done.14.first
  77.5 3.2 %collective-permute-done.12.refs_4_ = f32[64,512]{1,0:T(8,128)S(1)} collective-permute-done((f32[64,512]{1,0:T(8,128)S(1)}, f32[64,512]{1,0:T(8,128)S(1)}, u32[]{:S(2)}, u32[]{:S(2)}) %collective-permute-start.12) | collective-permute-done | bytes 131104 | tf_op jit(solution)/shard_map/ppermute | solution.py:540
  82.6 1.8 %end_sums.1 = (f32[2,256,256]{2,1,0:T(8,128)}, f32[2,256,512]{2,1,0:T(8,128)}) custom-call(s32[3]{0:T(128)S(1)} %pad_add_fusion.place, f32[2,2,256,128]{3,2,1,0:T(8,128)S(1)} %object_fold.1.refs_0_, f32[2,2,256,128]{3,2,1,0:T(8,128)S(1)} %collective-permute-done.15.refs_1_, f32[64,512]{1,0:T(8,128)S(1)} %probe_total.1.refs_2_, ...), custom_call_target="tpu_custom_call" | custom-call | tf_op jit(solution)/shard_map/end_sums/pallas_call | solution.py:442
  (43 shorter events, 5.6 us)
Async XLA Ops:
  0.6 20.6 %copy-start.3 = (bf16[512,256]{1,0:T(8,128)(2,1)S(1)}, bf16[512,256]{1,0:T(8,128)(2,1)}, u32[]{:S(2)}) copy-start(bf16[512,256]{1,0:T(8,128)(2,1)} %constant.32.clone.table) | copy-start | bytes 786436
  0.7 20.6 %copy-start = (bf16[1,8,256,256]{3,2,1,0:T(8,128)(2,1)S(1)}, bf16[1,8,256,256]{3,2,1,0:T(8,128)(2,1)}, u32[]{:S(2)}) copy-start(bf16[1,8,256,256]{3,2,1,0:T(8,128)(2,1)} %param.8) | copy-start | bytes 3145732
  2.1 6.6 %collective-permute-start.1 = (f32[128,1024]{1,0:T(8,128)S(1)}, f32[128,1024]{1,0:T(8,128)S(1)}, u32[]{:S(2)}, u32[]{:S(2)}) collective-permute-start(f32[128,1024]{1,0:T(8,128)S(1)} %get-tuple-element.66), channel_id=1, source_target_pairs={{4,8},{8,4},{5,9},{9,5},{6,10},{10,6},{7,11},{11,7},{20,24},{24,20... | collective-permute-start | bytes 1572872 | tf_op jit(solution)/shard_map/ppermute | solution.py:309
  2.8 17.5 %collective-permute-start = (f32[128,1024]{1,0:T(8,128)S(1)}, f32[128,1024]{1,0:T(8,128)S(1)}, u32[]{:S(2)}, u32[]{:S(2)}) collective-permute-start(f32[128,1024]{1,0:T(8,128)S(1)} %get-tuple-element.67), channel_id=1, source_target_pairs={{0,4},{4,0},{8,12},{12,8},{1,5},{5,1},{9,13},{13,9},{2,6},{6,2},{1... | collective-permute-start | bytes 1572872 | tf_op jit(solution)/shard_map/ppermute | solution.py:309
  8.7 12.8 %collective-permute-start.3 = (f32[128,1024]{1,0:T(8,128)S(1)}, f32[128,1024]{1,0:T(8,128)S(1)}, u32[]{:S(2)}, u32[]{:S(2)}) collective-permute-start(f32[128,1024]{1,0:T(8,128)S(1)} %collective-permute-done.1.second_a), channel_id=1, source_target_pairs={{0,1},{1,0},{2,3},{3,2},{4,5},{5,4},{6,7},{7,6},{8,9},{9,8},{10,11... | collective-permute-start | bytes 1572872 | tf_op jit(solution)/shard_map/ppermute | solution.py:315
  20.4 2.0 %collective-permute-start.2 = (f32[128,1024]{1,0:T(8,128)S(1)}, f32[128,1024]{1,0:T(8,128)}, u32[]{:S(2)}, u32[]{:S(2)}) collective-permute-start(f32[128,1024]{1,0:T(8,128)S(1)} %collective-permute-done.first_a), channel_id=1, source_target_pairs={{0,1},{1,0},{2,3},{3,2},{4,5},{5,4},{6,7},{7,6},{8,9},{9,8},{10,11... | collective-permute-start | bytes 1572872 | tf_op jit(solution)/shard_map/ppermute | solution.py:315
  38.7 4.1 %collective-permute-start.4 = (f32[2,2,512,128]{3,2,1,0:T(8,128)S(1)}, f32[2,2,512,128]{3,2,1,0:T(8,128)S(1)}, u32[]{:S(2)}, u32[]{:S(2)}) collective-permute-start(f32[2,2,512,128]{3,2,1,0:T(8,128)S(1)} %get-tuple-element.38), channel_id=1, source_target_pairs={{0,1},{1,0},{2,3},{3,2},{4,5},{5,4},{6,7},{7,6},{8,9},{9,8},{10,11... | collective-permute-start | bytes 3145736 | tf_op jit(solution)/shard_map/ppermute | solution.py:315
  38.9 3.3 %collective-permute-start.5 = (f32[256,512]{1,0:T(8,128)S(1)}, f32[256,512]{1,0:T(8,128)S(1)}, u32[]{:S(2)}, u32[]{:S(2)}) collective-permute-start(f32[256,512]{1,0:T(8,128)S(1)} %get-tuple-element.40), channel_id=1, source_target_pairs={{0,1},{1,0},{2,3},{3,2},{4,5},{5,4},{6,7},{7,6},{8,9},{9,8},{10,11... | collective-permute-start | bytes 1572872 | tf_op jit(solution)/shard_map/ppermute | solution.py:315
  39.3 18.6 %collective-permute-start.9 = (f32[2,2,512,128]{3,2,1,0:T(8,128)S(1)}, f32[2,2,512,128]{3,2,1,0:T(8,128)S(1)}, u32[]{:S(2)}, u32[]{:S(2)}) collective-permute-start(f32[2,2,512,128]{3,2,1,0:T(8,128)S(1)} %get-tuple-element.50), channel_id=1, source_target_pairs={{0,1},{1,0},{2,3},{3,2},{4,5},{5,4},{6,7},{7,6},{8,9},{9,8},{10,11... | collective-permute-start | bytes 3145736 | tf_op jit(solution)/shard_map/ppermute | solution.py:315
  42.9 15.0 %collective-permute-start.10 = (f32[2,2,256,128]{3,2,1,0:T(8,128)S(1)}, f32[2,2,256,128]{3,2,1,0:T(8,128)S(1)}, u32[]{:S(2)}, u32[]{:S(2)}) collective-permute-start(f32[2,2,256,128]{3,2,1,0:T(8,128)S(1)} %get-tuple-element.53), channel_id=1, source_target_pairs={{0,2},{2,0},{1,3},{3,1},{4,6},{6,4},{5,7},{7,5},{8,10},{10,8},{9,1... | collective-permute-start | bytes 1572872 | tf_op jit(solution)/shard_map/ppermute | solution.py:320
  44.4 7.6 %collective-permute-start.6 = (f32[64,512]{1,0:T(8,128)S(1)}, f32[64,512]{1,0:T(8,128)S(1)}, u32[]{:S(2)}, u32[]{:S(2)}) collective-permute-start(f32[64,512]{1,0:T(8,128)S(1)} %get-tuple-element.46), channel_id=1, source_target_pairs={{0,4},{4,0},{8,12},{12,8},{1,5},{5,1},{9,13},{13,9},{2,6},{6,2},{1... | collective-permute-start | bytes 393224 | tf_op jit(solution)/shard_map/ppermute | solution.py:540
  45.0 12.9 %collective-permute-start.7 = (f32[64,512]{1,0:T(8,128)S(1)}, f32[64,512]{1,0:T(8,128)S(1)}, u32[]{:S(2)}, u32[]{:S(2)}) collective-permute-start(f32[64,512]{1,0:T(8,128)S(1)} %get-tuple-element.47), channel_id=1, source_target_pairs={{0,8},{4,12},{8,0},{12,4},{1,9},{5,13},{9,1},{13,5},{2,10},{6,14},... | collective-permute-start | bytes 393224 | tf_op jit(solution)/shard_map/ppermute | solution.py:540
  46.8 11.0 %collective-permute-start.8 = (f32[64,512]{1,0:T(8,128)S(1)}, f32[64,512]{1,0:T(8,128)S(1)}, u32[]{:S(2)}, u32[]{:S(2)}) collective-permute-start(f32[64,512]{1,0:T(8,128)S(1)} %get-tuple-element.48), channel_id=1, source_target_pairs={{0,12},{4,8},{8,4},{12,0},{1,13},{5,9},{9,5},{13,1},{2,14},{6,10},... | collective-permute-start | bytes 393224 | tf_op jit(solution)/shard_map/ppermute | solution.py:540
  58.6 5.1 %collective-permute-start.11 = (f32[64,512]{1,0:T(8,128)S(1)}, f32[64,512]{1,0:T(8,128)S(1)}, u32[]{:S(2)}, u32[]{:S(2)}) collective-permute-start(f32[64,512]{1,0:T(8,128)S(1)} %probe_strips_sum.1.refs_0_), channel_id=1, source_target_pairs={{0,2},{2,0},{1,3},{3,1},{4,6},{6,4},{5,7},{7,5},{8,10},{10,8},{9,1... | collective-permute-start | bytes 393224 | tf_op jit(solution)/shard_map/ppermute | solution.py:320
  60.5 10.0 %collective-permute-start.13 = (f32[2,2,128,128]{3,2,1,0:T(8,128)S(1)}, f32[2,2,128,128]{3,2,1,0:T(8,128)S(1)}, u32[]{:S(2)}, u32[]{:S(2)}) collective-permute-start(f32[2,2,128,128]{3,2,1,0:T(8,128)S(1)} %get-tuple-element.61), channel_id=1, source_target_pairs={{4,8},{8,4},{5,9},{9,5},{6,10},{10,6},{7,11},{11,7},{20,24},{24,20... | collective-permute-start | bytes 786440 | tf_op jit(solution)/shard_map/ppermute | solution.py:309
  63.7 18.9 %collective-permute-start.15 = (f32[2,2,256,128]{3,2,1,0:T(8,128)S(1)}, f32[2,2,256,128]{3,2,1,0:T(8,128)S(1)}, u32[]{:S(2)}, u32[]{:S(2)}) collective-permute-start(f32[2,2,256,128]{3,2,1,0:T(8,128)S(1)} %get-tuple-element.64), channel_id=1, source_target_pairs={{0,2},{2,0},{1,3},{3,1},{4,6},{6,4},{5,7},{7,5},{8,10},{10,8},{9,1... | collective-permute-start | bytes 1572872 | tf_op jit(solution)/shard_map/ppermute | solution.py:320
  66.1 10.8 %collective-permute-start.14 = (f32[2,2,128,128]{3,2,1,0:T(8,128)S(1)}, f32[2,2,128,128]{3,2,1,0:T(8,128)S(1)}, u32[]{:S(2)}, u32[]{:S(2)}) collective-permute-start(f32[2,2,128,128]{3,2,1,0:T(8,128)S(1)} %get-tuple-element.62), channel_id=1, source_target_pairs={{0,4},{4,0},{8,12},{12,8},{1,5},{5,1},{9,13},{13,9},{2,6},{6,2},{1... | collective-permute-start | bytes 786440 | tf_op jit(solution)/shard_map/ppermute | solution.py:309
  67.7 13.0 %collective-permute-start.12 = (f32[64,512]{1,0:T(8,128)S(1)}, f32[64,512]{1,0:T(8,128)S(1)}, u32[]{:S(2)}, u32[]{:S(2)}) collective-permute-start(f32[64,512]{1,0:T(8,128)S(1)} %probe_total.1.refs_2_), channel_id=1, source_target_pairs={{0,8},{4,12},{8,0},{12,4},{1,9},{5,13},{9,1},{13,5},{2,10},{6,14},... | collective-permute-start | bytes 393224 | tf_op jit(solution)/shard_map/ppermute | solution.py:540
  68.6 12.2 %collective-permute-start.17 = (f32[64,512]{1,0:T(8,128)S(1)}, f32[64,512]{1,0:T(8,128)S(1)}, u32[]{:S(2)}, u32[]{:S(2)}) collective-permute-start(f32[64,512]{1,0:T(8,128)S(1)} %probe_total.1.refs_2_), channel_id=1, source_target_pairs={{0,12},{4,8},{8,4},{12,0},{1,13},{5,9},{9,5},{13,1},{2,14},{6,10},... | collective-permute-start | bytes 393224 | tf_op jit(solution)/shard_map/ppermute | solution.py:540
  70.5 10.5 %collective-permute-start.16 = (f32[64,512]{1,0:T(8,128)S(1)}, f32[64,512]{1,0:T(8,128)S(1)}, u32[]{:S(2)}, u32[]{:S(2)}) collective-permute-start(f32[64,512]{1,0:T(8,128)S(1)} %probe_total.1.refs_2_), channel_id=1, source_target_pairs={{0,4},{4,0},{8,12},{12,8},{1,5},{5,1},{9,13},{13,9},{2,6},{6,2},{1... | collective-permute-start | bytes 393224 | tf_op jit(solution)/shard_map/ppermute | solution.py:540
  76.9 4.6 %collective-permute-start.18 = (f32[64,512]{1,0:T(8,128)S(1)}, f32[64,512]{1,0:T(8,128)S(1)}, u32[]{:S(2)}, u32[]{:S(2)}) collective-permute-start(f32[64,512]{1,0:T(8,128)S(1)} %probe_total.1.refs_2_), channel_id=1, source_target_pairs={{0,1},{1,0},{2,3},{3,2},{4,5},{5,4},{6,7},{7,6},{8,9},{9,8},{10,11... | collective-permute-start | bytes 393224 | tf_op jit(solution)/shard_map/ppermute | solution.py:315
  80.7 1.3 %collective-permute-start.21 = (f32[64,512]{1,0:T(8,128)S(1)}, f32[64,512]{1,0:T(8,128)S(1)}, u32[]{:S(2)}, u32[]{:S(2)}) collective-permute-start(f32[64,512]{1,0:T(8,128)S(1)} %collective-permute-done.17.refs_5_), channel_id=1, source_target_pairs={{0,1},{1,0},{2,3},{3,2},{4,5},{5,4},{6,7},{7,6},{8,9},{9,8},{10,11... | collective-permute-start | bytes 393224 | tf_op jit(solution)/shard_map/ppermute | solution.py:315
  81.0 1.3 %collective-permute-start.19 = (f32[64,512]{1,0:T(8,128)S(1)}, f32[64,512]{1,0:T(8,128)S(1)}, u32[]{:S(2)}, u32[]{:S(2)}) collective-permute-start(f32[64,512]{1,0:T(8,128)S(1)} %collective-permute-done.16.refs_3_), channel_id=1, source_target_pairs={{0,1},{1,0},{2,3},{3,2},{4,5},{5,4},{6,7},{7,6},{8,9},{9,8},{10,11... | collective-permute-start | bytes 393224 | tf_op jit(solution)/shard_map/ppermute | solution.py:315
  81.2 1.3 %collective-permute-start.20 = (f32[64,512]{1,0:T(8,128)S(1)}, f32[64,512]{1,0:T(8,128)S(1)}, u32[]{:S(2)}, u32[]{:S(2)}) collective-permute-start(f32[64,512]{1,0:T(8,128)S(1)} %collective-permute-done.12.refs_4_), channel_id=1, source_target_pairs={{0,1},{1,0},{2,3},{3,2},{4,5},{5,4},{6,7},{7,6},{8,9},{9,8},{10,11... | collective-permute-start | bytes 393224 | tf_op jit(solution)/shard_map/ppermute | solution.py:315
  (3 other events, 42.5 us)
